TPU v7x, 32 devices: a whole 2x2x4 slice. The times are simulated.
32 devices in a mesh: dp: 8 (over y, x, core), mp: 4 (over z).
Axes of the slice: x: 2, y: 2, z: 4, core: 2. Of those that a mesh axis runs over, the one named last changes fastest.
Arguments:
- tokens: bfloat16 [1024, 8, 1024], P('mp', 'dp'), may hold values from -6 to 6
- memory: bfloat16 [1024, 8, 1024], P('mp', 'dp'), may hold values from -6 to 6
- self_qkv: bfloat16 [1024, 3, 1024], P(None, None, 'mp'), may hold values from -1 to 1
- self_out: bfloat16 [1024, 1024], P(None, 'mp'), may hold values from -0.75 to 0.75
- cross_q: bfloat16 [1024, 1024], P(None, 'mp'), may hold values from -1 to 1
- cross_kv: bfloat16 [1024, 2, 1024], P(None, None, 'mp'), may hold values from -1 to 1
- cross_out: bfloat16 [1024, 1024], P(None, 'mp'), may hold values from -1 to 1
- ffn_in: bfloat16 [1024, 4096], P(None, 'mp'), may hold values from -0.1875 to 0.1875
- ffn_out: bfloat16 [1024, 4096], P(None, 'mp'), may hold values from -0.375 to 0.375
- ln_gain: float32 [3, 1024], replicated, may hold values from 0.5 to 1.5
- ln_bias: float32 [3, 1024], replicated, may hold values from -1.5 to 1.5
- cotangent: bfloat16 [1024, 8, 1024], P('mp', 'dp'), may hold values from -6 to 6
Outputs:
- mixed: bfloat16 [1024, 8, 1024], P('mp', 'dp')
- token_grad: bfloat16 [1024, 8, 1024], P('mp', 'dp')
- memory_grad: bfloat16 [1024, 8, 1024], P('mp', 'dp')
- self_qkv_grad: float32 [1024, 3, 1024], P('dp', None, 'mp')
- self_out_grad: float32 [1024, 1024], P('dp', 'mp')
- cross_q_grad: float32 [1024, 1024], P('dp', 'mp')
- cross_kv_grad: float32 [1024, 2, 1024], P('dp', None, 'mp')
- cross_out_grad: float32 [1024, 1024], P('dp', 'mp')
- ffn_in_grad: float32 [1024, 4096], P('dp', 'mp')
- ffn_out_grad: float32 [1024, 4096], P('dp', 'mp')
- gain_grad: float32 [3, 1024], replicated
- bias_grad: float32 [3, 1024], replicated
All inputs are finite; a program needn't handle non-finite values.
Results may differ from a plain program's by a relative error of at most 0.025.
Values may be sent and summed in bfloat16 or wider, within the bound.
No kernel may reach another device: no remote copies, remote signals or barrier semaphores. Data moves between devices by JAX's collectives and lax.ppermute only.
A program may use at most 192 MiB of HBM per device.

v0:
```python
import math

import jax
import jax.numpy as jnp
from jax import lax
from jax.sharding import PartitionSpec as P

HD = 64


alpha_scale = 300.0**0.25
norm_eps = 1e-05


def layer_norm(value, gain, bias):
    center = value - jnp.mean(value, axis=-1, keepdims=True)
    spread = jnp.mean(center * center, axis=-1, keepdims=True)
    return center * lax.rsqrt(spread + norm_eps) * gain + bias


def gelu_tanh(value):
    return jax.nn.gelu(value, approximate=True)


def dense(left, weight):
    return jnp.einsum("tpd,df->tpf", left, weight, preferred_element_type=jnp.float32)


def weight_grad(left, grad):
    return jnp.einsum("tpd,tpf->df", left, grad, preferred_element_type=jnp.float32)


def back_dense(grad, weight):
    return jnp.einsum("tpf,df->tpd", grad, weight, preferred_element_type=jnp.float32)


def rows_times(acts, weight):
    return back_dense(acts, weight)


def split_heads(value):
    return value.reshape(value.shape[0], value.shape[1], -1, HD)


def block_scores(query_block, keys, begin, causal):
    scores = jnp.einsum(
        "qphe,kphe->phqk", query_block, keys, preferred_element_type=jnp.float32
    ) * (1.0 / math.sqrt(HD))
    if causal:
        rows_at = begin + jnp.arange(query_block.shape[0], dtype=jnp.int32)[:, None]
        cols_at = jnp.arange(keys.shape[0], dtype=jnp.int32)[None, :]
        scores = jnp.where(cols_at <= rows_at, scores, -1000000000.0)
    return scores


def attend_forward(queries, keys, values, causal):
    seq, pair_count, feature = queries.shape
    block = min(512, seq)
    query_heads = split_heads(queries)
    key_heads = split_heads(keys)
    value_heads = split_heads(values)

    def one_block(begin):
        query_block = lax.dynamic_slice_in_dim(query_heads, begin, block, 0)
        scores = block_scores(query_block, key_heads, begin, causal)
        norm_log = jax.nn.logsumexp(scores, axis=-1, keepdims=True)
        probs = jnp.exp(scores - norm_log).astype(jnp.bfloat16)
        result = jnp.einsum(
            "phqk,kphe->qphe", probs, value_heads, preferred_element_type=jnp.float32
        )
        return (result.astype(jnp.bfloat16), norm_log)

    begins = jnp.arange(seq // block, dtype=jnp.int32) * block
    result, norm_logs = lax.map(one_block, begins)
    return (result.reshape(seq, pair_count, feature), norm_logs)


def attend_backward(queries, keys, values, result_grad, norm_logs, causal):
    seq, pair_count, feature = queries.shape
    block = min(512, seq)
    factor = 1.0 / math.sqrt(HD)
    query_heads = split_heads(queries)
    key_heads = split_heads(keys)
    value_heads = split_heads(values)
    grad_heads = split_heads(result_grad)

    def one_block(carry, item):
        begin, norm_log = item
        key_acc, value_acc = carry
        query_block = lax.dynamic_slice_in_dim(query_heads, begin, block, 0)
        grad_block = lax.dynamic_slice_in_dim(grad_heads, begin, block, 0)
        scores = block_scores(query_block, key_heads, begin, causal)
        probs = jnp.exp(scores - norm_log)
        value_acc = value_acc + jnp.einsum(
            "phqk,qphe->kphe",
            probs.astype(jnp.bfloat16),
            grad_block,
            preferred_element_type=jnp.float32,
        )
        prob_grad = jnp.einsum(
            "qphe,kphe->phqk", grad_block, value_heads, preferred_element_type=jnp.float32
        )
        inner = jnp.sum(prob_grad * probs, axis=-1, keepdims=True)
        score_grad = (probs * (prob_grad - inner)).astype(jnp.bfloat16)
        query_grad = (
            jnp.einsum("phqk,kphe->qphe", score_grad, key_heads, preferred_element_type=jnp.float32)
            * factor
        )
        key_acc = (
            key_acc
            + jnp.einsum(
                "phqk,qphe->kphe", score_grad, query_block, preferred_element_type=jnp.float32
            )
            * factor
        )
        return ((key_acc, value_acc), query_grad)

    begins = jnp.arange(seq // block, dtype=jnp.int32) * block
    zeros_kv = jnp.zeros(key_heads.shape, jnp.float32)
    (key_grad, value_grad), query_grad = lax.scan(
        one_block, (zeros_kv, zeros_kv), (begins, norm_logs)
    )
    span = keys.shape[0]
    return (
        query_grad.reshape(seq, pair_count, feature).astype(jnp.bfloat16),
        key_grad.reshape(span, pair_count, feature).astype(jnp.bfloat16),
        value_grad.reshape(span, pair_count, feature).astype(jnp.bfloat16),
    )


def sum_weights(grads):
    edges = []
    running = 0
    for grad in grads[:-1]:
        running = running + grad.shape[1]
        edges.append(running)
    joined = jnp.concatenate(grads, axis=1)
    summed = lax.psum_scatter(joined, "dp", scatter_dimension=0, tiled=True)
    return jnp.split(summed, edges, axis=1)


def local(
    tokens,
    memory,
    self_qkv,
    self_out,
    cross_q,
    cross_kv,
    cross_out,
    ffn_in,
    ffn_out,
    ln_gain,
    ln_bias,
    cotangent,
):
    model_width = tokens.shape[2]
    local_width = self_out.shape[1]
    qkv_flat = self_qkv.reshape(model_width, 3 * local_width)
    kv_flat = cross_kv.reshape(model_width, 2 * local_width)
    full_tokens, full_memory = (
        lax.all_gather(tokens, "mp", axis=0, tiled=True),
        lax.all_gather(memory, "mp", axis=0, tiled=True),
    )
    projected = dense(full_tokens, qkv_flat).astype(jnp.bfloat16)
    queries = projected[..., :local_width]
    keys = projected[..., local_width : 2 * local_width]
    values = projected[..., 2 * local_width :]
    attended, self_logs = attend_forward(queries, keys, values, True)
    self_branch = lax.psum_scatter(
        rows_times(attended, self_out).astype(jnp.bfloat16), "mp", scatter_dimension=0, tiled=True
    ).astype(jnp.float32)
    first, first_pull = jax.vjp(
        layer_norm, alpha_scale * tokens.astype(jnp.float32) + self_branch, ln_gain[0], ln_bias[0]
    )
    first_low = first.astype(jnp.bfloat16)
    full_first = lax.all_gather(first_low, "mp", axis=0, tiled=True)
    cross_queries = dense(full_first, cross_q).astype(jnp.bfloat16)
    cross_pair = dense(full_memory, kv_flat).astype(jnp.bfloat16)
    cross_keys = cross_pair[..., :local_width]
    cross_values = cross_pair[..., local_width:]
    cross_attended, cross_logs = attend_forward(cross_queries, cross_keys, cross_values, False)
    cross_branch = lax.psum_scatter(
        rows_times(cross_attended, cross_out).astype(jnp.bfloat16),
        "mp",
        scatter_dimension=0,
        tiled=True,
    ).astype(jnp.float32)
    second, second_pull = jax.vjp(
        layer_norm, alpha_scale * first + cross_branch, ln_gain[1], ln_bias[1]
    )
    second_low = second.astype(jnp.bfloat16)
    full_second = lax.all_gather(second_low, "mp", axis=0, tiled=True)
    hidden = dense(full_second, ffn_in)
    activation_full, gelu_pull = jax.vjp(gelu_tanh, hidden)
    activation = activation_full.astype(jnp.bfloat16)
    ffn_branch = lax.psum_scatter(
        rows_times(activation, ffn_out).astype(jnp.bfloat16), "mp", scatter_dimension=0, tiled=True
    ).astype(jnp.float32)
    mixed_full, third_pull = jax.vjp(
        layer_norm, alpha_scale * second + ffn_branch, ln_gain[2], ln_bias[2]
    )
    mixed = mixed_full.astype(jnp.bfloat16)
    third_grad, gain_three, bias_three = third_pull(cotangent.astype(jnp.float32))
    full_ffn_grad = lax.all_gather(third_grad.astype(jnp.bfloat16), "mp", axis=0, tiled=True)
    grad_ffn_out = weight_grad(full_ffn_grad, activation)
    activation_grad = jnp.einsum(
        "tpo,of->tpf", full_ffn_grad, ffn_out, preferred_element_type=jnp.float32
    ).astype(jnp.bfloat16)
    hidden_grad = gelu_pull(activation_grad.astype(jnp.float32))[0].astype(jnp.bfloat16)
    grad_ffn_in = weight_grad(full_second, hidden_grad)
    second_part = lax.psum_scatter(
        rows_times(hidden_grad, ffn_in).astype(jnp.bfloat16), "mp", scatter_dimension=0, tiled=True
    ).astype(jnp.float32)
    second_grad = alpha_scale * third_grad + second_part
    cross_grad, gain_two, bias_two = second_pull(second_grad)
    full_cross_grad = lax.all_gather(cross_grad.astype(jnp.bfloat16), "mp", axis=0, tiled=True)
    grad_cross_out = weight_grad(full_cross_grad, cross_attended)
    cross_attended_grad = jnp.einsum(
        "tpo,of->tpf", full_cross_grad, cross_out, preferred_element_type=jnp.float32
    ).astype(jnp.bfloat16)
    cross_queries_grad, cross_keys_grad, cross_values_grad = attend_backward(
        cross_queries, cross_keys, cross_values, cross_attended_grad, cross_logs, False
    )
    cross_pair_grad = jnp.concatenate([cross_keys_grad, cross_values_grad], axis=-1)
    grad_cross_q = weight_grad(full_first, cross_queries_grad)
    grad_cross_kv = weight_grad(full_memory, cross_pair_grad)
    memory_term = back_dense(cross_pair_grad, kv_flat)
    first_part = lax.psum_scatter(
        rows_times(cross_queries_grad, cross_q).astype(jnp.bfloat16),
        "mp",
        scatter_dimension=0,
        tiled=True,
    ).astype(jnp.float32)
    first_grad = alpha_scale * cross_grad + first_part
    self_grad, gain_one, bias_one = first_pull(first_grad)
    full_self_grad = lax.all_gather(self_grad.astype(jnp.bfloat16), "mp", axis=0, tiled=True)
    grad_self_out = weight_grad(full_self_grad, attended)
    attended_grad = jnp.einsum(
        "tpo,of->tpf", full_self_grad, self_out, preferred_element_type=jnp.float32
    ).astype(jnp.bfloat16)
    queries_grad, keys_grad, values_grad = attend_backward(
        queries, keys, values, attended_grad, self_logs, True
    )
    projected_grad = jnp.concatenate([queries_grad, keys_grad, values_grad], axis=-1)
    grad_self_qkv = weight_grad(full_tokens, projected_grad)
    token_term = back_dense(projected_grad, qkv_flat)
    token_part, memory_part = (
        lax.psum_scatter(
            token_term.astype(jnp.bfloat16), "mp", scatter_dimension=0, tiled=True
        ).astype(jnp.float32),
        lax.psum_scatter(
            memory_term.astype(jnp.bfloat16), "mp", scatter_dimension=0, tiled=True
        ).astype(jnp.float32),
    )
    token_grad = (alpha_scale * self_grad + token_part).astype(jnp.bfloat16)
    memory_grad = memory_part.astype(jnp.bfloat16)
    final_parts = sum_weights(
        [
            grad_ffn_in,
            grad_ffn_out,
            grad_cross_q,
            grad_cross_kv,
            grad_cross_out,
            grad_self_qkv,
            grad_self_out,
        ]
    )
    gain_local = jnp.stack([gain_one, gain_two, gain_three])
    bias_local = jnp.stack([bias_one, bias_two, bias_three])
    gain_grad, bias_grad = lax.psum((gain_local, bias_local), ("dp", "mp"))
    ffn_in_grad = final_parts[0]
    ffn_out_grad = final_parts[1]
    cross_q_grad = final_parts[2]
    cross_kv_grad = final_parts[3].reshape(-1, 2, local_width)
    cross_out_grad = final_parts[4]
    self_qkv_grad = final_parts[5].reshape(-1, 3, local_width)
    self_out_grad = final_parts[6]
    return (
        mixed,
        token_grad,
        memory_grad,
        self_qkv_grad,
        self_out_grad,
        cross_q_grad,
        cross_kv_grad,
        cross_out_grad,
        ffn_in_grad,
        ffn_out_grad,
        gain_grad,
        bias_grad,
    )


def solution(mesh):
    in_specs = (
        P("mp", "dp", None),
        P("mp", "dp", None),
        P(None, None, "mp"),
        P(None, "mp"),
        P(None, "mp"),
        P(None, None, "mp"),
        P(None, "mp"),
        P(None, "mp"),
        P(None, "mp"),
        P(),
        P(),
        P("mp", "dp", None),
    )
    out_specs = (
        P("mp", "dp", None),
        P("mp", "dp", None),
        P("mp", "dp", None),
        P("dp", None, "mp"),
        P("dp", "mp"),
        P("dp", "mp"),
        P("dp", None, "mp"),
        P("dp", "mp"),
        P("dp", "mp"),
        P("dp", "mp"),
        P(),
        P(),
    )
    return jax.shard_map(local, mesh=mesh, in_specs=in_specs, out_specs=out_specs, check_vma=False)
```

profile of v0, /device:TPU:0, one launch (start us, length us, event | category | flops | bytes accessed | tf_op | source)
XLA Modules:
  0.0 983.8 jit_solution(1934167714065036217)
XLA Ops:
  10.6 47.7 %all-gather.8.cloned.1.call-done = bf16[1024,1,1024]{2,0,1:T(8,128)(2,1)} async-done(((bf16[256,1,1024]{2,0,1:T(8,128)(2,1)}), bf16[1024,1,1024]{2,0,1:T(8,128)(2,1)}) %all-gather.8.cloned.1.call-update) | async-done | bytes 2097168 | tf_op jit(solution)/shard_map/all_gather | solution.py:161
  58.3 3.9 fusion.142
  64.1 24.1 %while.54 = (s32[]{:T(128)}, bf16[2,512,1,4,64]{1,4,3,2,0:T(8,128)(2,1)}, f32[2,1,4,512,1]{3,2,4,1,0:T(4,128)S(1)}, s32[2]{0:T(128)S(1)}, bf16[1024,1,4,64]{0,3,...) while((s32[]{:T(128)}, ...), condition=%wide.region_3.4_spmd, body=%wide.region_0.3_spmd.sunk | while | flops 560611840 | bytes 35229948 | solution.py:74
  94.9 41.9 %reduce-scatter.9.cloned.1.call-done = bf16[256,1,1024]{2,0,1:T(8,128)(2,1)} async-done(((bf16[1024,1,1024]{2,0,1:T(8,128)(2,1)}), bf16[256,1,1024]{2,0,1:T(8,128)(2,1)}) %reduce-scatter.9.cloned.1.call-update) | async-done | bytes 524304 | tf_op jit(solution)/shard_map/reduce_scatter | solution.py:169
  143.4 40.3 %all-gather.12.cloned.1.call-done = bf16[1024,1,1024]{2,0,1:T(8,128)(2,1)} async-done(((bf16[256,1,1024]{2,0,1:T(8,128)(2,1)}), bf16[1024,1,1024]{2,0,1:T(8,128)(2,1)}) %all-gather.12.cloned.1.call-update) | async-done | bytes 2097168 | tf_op jit(solution)/shard_map/all_gather | solution.py:162
  186.7 43.8 %all-gather.10.cloned.1.call-done = bf16[1024,1,1024]{2,0,1:T(8,128)(2,1)} async-done(((bf16[256,1,1024]{2,0,1:T(8,128)(2,1)}), bf16[1024,1,1024]{2,0,1:T(8,128)(2,1)}) %all-gather.10.cloned.1.call-update) | async-done | bytes 2097168 | tf_op jit(solution)/shard_map/all_gather | solution.py:176
  234.5 19.0 %while.55 = (s32[]{:T(128)}, bf16[2,512,1,4,64]{1,4,3,2,0:T(8,128)(2,1)}, f32[2,1,4,512,1]{3,2,4,1,0:T(4,128)S(1)}, s32[2]{0:T(128)S(1)}, bf16[1024,1,4,64]{0,3,...) while((s32[]{:T(128)}, ...), condition=%wide.region_10.11_spmd, body=%wide.region_7.10_spmd.sunk | while | flops 553795584 | bytes 31031520 | solution.py:74
  259.3 42.7 %reduce-scatter.11.cloned.1.call-done = bf16[256,1,1024]{2,0,1:T(8,128)(2,1)} async-done(((bf16[1024,1,1024]{2,0,1:T(8,128)(2,1)}), bf16[256,1,1024]{2,0,1:T(8,128)(2,1)}) %reduce-scatter.11.cloned.1.call-update) | async-done | bytes 524304 | tf_op jit(solution)/shard_map/reduce_scatter | solution.py:182
  306.0 45.4 %all-gather.14.cloned.1.call-done = bf16[1024,1,1024]{2,0,1:T(8,128)(2,1)} async-done(((bf16[256,1,1024]{2,0,1:T(8,128)(2,1)}), bf16[1024,1,1024]{2,0,1:T(8,128)(2,1)}) %all-gather.14.cloned.1.call-update) | async-done | bytes 2097168 | tf_op jit(solution)/shard_map/all_gather | solution.py:192
  351.3 4.5 fusion.119
  357.9 4.0 convert_bitcast_fusion.4
  362.4 42.3 %reduce-scatter.13.cloned.1.call-done = bf16[256,1,1024]{2,0,1:T(8,128)(2,1)} async-done(((bf16[1024,1,1024]{2,0,1:T(8,128)(2,1)}), bf16[256,1,1024]{2,0,1:T(8,128)(2,1)}) %reduce-scatter.13.cloned.1.call-update) | async-done | bytes 524304 | tf_op jit(solution)/shard_map/reduce_scatter | solution.py:196
  412.2 45.4 %all-gather.16.cloned.1.call-done = bf16[1024,1,1024]{2,0,1:T(8,128)(2,1)} async-done(((bf16[256,1,1024]{2,0,1:T(8,128)(2,1)}), bf16[1024,1,1024]{2,0,1:T(8,128)(2,1)}) %all-gather.16.cloned.1.call-update) | async-done | bytes 2097168 | tf_op jit(solution)/shard_map/all_gather | solution.py:204
  457.5 7.1 fusion.99
  466.0 3.7 convert_bitcast_fusion.3
  469.7 42.7 %reduce-scatter.15.cloned.1.call-done = bf16[256,1,1024]{2,0,1:T(8,128)(2,1)} async-done(((bf16[1024,1,1024]{2,0,1:T(8,128)(2,1)}), bf16[256,1,1024]{2,0,1:T(8,128)(2,1)}) %reduce-scatter.15.cloned.1.call-update) | async-done | bytes 524304 | tf_op jit(solution)/shard_map/reduce_scatter | solution.py:211
  518.5 45.2 %all-gather.18.cloned.1.call-done = bf16[1024,1,1024]{2,0,1:T(8,128)(2,1)} async-done(((bf16[256,1,1024]{2,0,1:T(8,128)(2,1)}), bf16[1024,1,1024]{2,0,1:T(8,128)(2,1)}) %all-gather.18.cloned.1.call-update) | async-done | bytes 2097168 | tf_op jit(solution)/shard_map/all_gather | solution.py:216
  567.7 42.3 %while.56 = (s32[]{:T(128)}, f32[1024,1,4,64]{0,3,2,1:T(8,128)S(1)}, f32[1024,1,4,64]{0,3,2,1:T(8,128)S(1)}, bf16[2,512,1,4,64]{1,4,3,2,0:T(8,128)(2,1)}, s32[2]...) while((s32[]{:T(128)}, ...), condition=%wide.region_24.25_spmd.clone, body=%wide.region_22.24_spmd.clone.sunk | while | flops 1368782848 | bytes 162587024 | solution.py:120
  579.6 3.4 fusion.274
  616.2 42.7 %reduce-scatter.17.cloned.1.call-done = bf16[256,1,1024]{2,0,1:T(8,128)(2,1)} async-done(((bf16[1024,1,1024]{2,0,1:T(8,128)(2,1)}), bf16[256,1,1024]{2,0,1:T(8,128)(2,1)}) %reduce-scatter.17.cloned.1.call-update) | async-done | bytes 524304 | tf_op jit(solution)/shard_map/reduce_scatter | solution.py:228
  664.6 45.3 %all-gather.20.cloned.1.call-done = bf16[1024,1,1024]{2,0,1:T(8,128)(2,1)} async-done(((bf16[256,1,1024]{2,0,1:T(8,128)(2,1)}), bf16[1024,1,1024]{2,0,1:T(8,128)(2,1)}) %all-gather.20.cloned.1.call-update) | async-done | bytes 2097168 | tf_op jit(solution)/shard_map/all_gather | solution.py:236
  714.0 46.6 %while.57 = (s32[]{:T(128)}, f32[1024,1,4,64]{0,3,2,1:T(8,128)S(1)}, f32[1024,1,4,64]{0,3,2,1:T(8,128)}, bf16[2,512,1,4,64]{1,4,3,2,0:T(8,128)(2,1)}, s32[2]{0:T...) while((s32[]{:T(128)}, ...), condition=%wide.region_30.31_spmd.clone, body=%wide.region_28.30_spmd.clone.sunk | while | flops 1375599104 | bytes 164688304 | solution.py:120
  722.6 3.7 multiply_convert_fusion.8
  731.1 3.6 fusion.287
  745.2 3.7 multiply_convert_fusion.8
  753.7 4.8 fusion.287
  764.0 4.7 convert_bitcast_fusion.1
  769.1 6.7 convolution_dynamic-update-slice_fusion.1
  775.9 4.8 convolution_dynamic-update-slice_fusion
  796.3 39.7 %all-reduce = (f32[3,1024]{1,0:T(4,128)}, f32[3,1024]{1,0:T(4,128)}) all-reduce(f32[3,1024]{1,0:T(4,128)S(1)} %get-tuple-element.410, f32[3,1024]{1,0:T(4,128)S(1)} %get-tuple-element.411), channel_id=1, replica_groups=mesh['dp'=8,'mp'=4] {'dp','mp'}, use_global_device_ids=true, to_apply=%region_37.38 | all-reduce | flops 6144 | bytes 49152 | tf_op jit(solution)/shard_map/psum | solution.py:270
  838.3 92.0 %reduce-scatter.23.cloned.1.call-done = f32[128,4096]{0,1:T(8,128)} async-done(((f32[1024,4096]{0,1:T(8,128)}), f32[128,4096]{0,1:T(8,128)}) %reduce-scatter.23.cloned.1.call-update) | async-done | bytes 2097168 | tf_op jit(solution)/shard_map/reduce_scatter | solution.py:138
  940.6 36.3 %reduce-scatter.21.cloned.1.call-done = bf16[256,1,1024]{2,0,1:T(8,128)(2,1)} async-done(((bf16[1024,1,1024]{2,0,1:T(8,128)(2,1)}), bf16[256,1,1024]{2,0,1:T(8,128)(2,1)}) %reduce-scatter.21.cloned.1.call-update) | async-done | bytes 524304 | tf_op jit(solution)/shard_map/reduce_scatter | solution.py:251
  (360 shorter events, 200.1 us)
Async XLA Ops:
  7.2 350.7 %copy-start = (bf16[1024,1024]{1,0:T(8,128)(2,1)S(1)}, bf16[1024,1024]{1,0:T(8,128)(2,1)}, u32[]{:S(2)}) copy-start(bf16[1024,1024]{1,0:T(8,128)(2,1)} %param.28) | copy-start | bytes 6291460
  7.2 51.1 %all-gather.8.cloned.1.call-start = ((), (), s32[]{:S(2)}) async-start(), calls=%async_computation.8 | async-start | bytes 2621440 | tf_op jit(solution)/shard_map/all_gather | solution.py:161
  7.9 128.9 %reduce-scatter.9.cloned.1.call-start = ((), (), s32[]{:S(2)}) async-start(), calls=%async_computation.9 | async-start | bytes 2621440 | tf_op jit(solution)/shard_map/reduce_scatter | solution.py:169
  88.1 50.0 %copy-start.8 = (bf16[1024,1,4,64]{0,3,2,1:T(8,128)(2,1)}, bf16[1024,1,4,64]{0,3,2,1:T(8,128)(2,1)S(1)}, u32[]{:S(2)}) copy-start(bf16[1024,1,4,64]{0,3,2,1:T(8,128)(2,1)S(1)} %get-tuple-element.789) | copy-start | bytes 1572868
  88.1 50.0 %copy-start.55 = (f32[2,1,4,512,1]{3,2,4,1,0:T(4,128)}, f32[2,1,4,512,1]{3,2,4,1,0:T(4,128)S(1)}, u32[]{:S(2)}) copy-start(f32[2,1,4,512,1]{3,2,4,1,0:T(4,128)S(1)} %get-tuple-element.742) | copy-start | bytes 49156
  88.1 48.6 %copy-start.17 = (bf16[256,1,1024]{2,0,1:T(8,128)(2,1)S(1)}, bf16[256,1,1024]{2,0,1:T(8,128)(2,1)}, u32[]{:S(2)}) copy-start(bf16[256,1,1024]{2,0,1:T(8,128)(2,1)} %param.20) | copy-start | bytes 1572868
  94.0 89.7 %all-gather.12.cloned.1.call-start = ((), (), s32[]{:S(2)}) async-start(), calls=%async_computation.11 | async-start | bytes 2621440 | tf_op jit(solution)/shard_map/all_gather | solution.py:162
  94.8 135.7 %all-gather.10.cloned.1.call-start = ((), (), s32[]{:S(2)}) async-start(), calls=%async_computation.10 | async-start | bytes 2621440 | tf_op jit(solution)/shard_map/all_gather | solution.py:176
  139.5 47.1 %copy-start.63 = (f32[256]{0:T(256)}, f32[256]{0:T(256)S(1)}, u32[]{:S(2)}) copy-start(f32[256]{0:T(256)S(1)} %multiply_reduce_fusion.9) | copy-start | bytes 3076
  141.7 160.3 %reduce-scatter.11.cloned.1.call-start = ((), (), s32[]{:S(2)}) async-start(), calls=%async_computation.12 | async-start | bytes 2621440 | tf_op jit(solution)/shard_map/reduce_scatter | solution.py:182
  259.3 92.1 %all-gather.14.cloned.1.call-start = ((), (), s32[]{:S(2)}) async-start(), calls=%async_computation.13 | async-start | bytes 2621440 | tf_op jit(solution)/shard_map/all_gather | solution.py:192
  305.9 98.8 %reduce-scatter.13.cloned.1.call-start = ((), (), s32[]{:S(2)}) async-start(), calls=%async_computation.14 | async-start | bytes 2621440 | tf_op jit(solution)/shard_map/reduce_scatter | solution.py:196
  362.0 95.6 %all-gather.16.cloned.1.call-start = ((), (), s32[]{:S(2)}) async-start(), calls=%async_computation.15 | async-start | bytes 2621440 | tf_op jit(solution)/shard_map/all_gather | solution.py:204
  412.1 100.3 %reduce-scatter.15.cloned.1.call-start = ((), (), s32[]{:S(2)}) async-start(), calls=%async_computation.16 | async-start | bytes 2621440 | tf_op jit(solution)/shard_map/reduce_scatter | solution.py:211
  466.0 46.5 %copy-start.16 = (f32[256,1,1024]{2,0,1:T(8,128)S(1)}, f32[256,1,1024]{2,0,1:T(8,128)}, u32[]{:S(2)}) copy-start(f32[256,1,1024]{2,0,1:T(8,128)} %copy-done.15) | copy-start | bytes 3145732
  466.0 46.5 %copy-start.23 = (f32[256,1,1024]{2,0,1:T(8,128)S(1)}, f32[256,1,1024]{2,0,1:T(8,128)}, u32[]{:S(2)}) copy-start(f32[256,1,1024]{2,0,1:T(8,128)} %copy-done.22) | copy-start | bytes 3145732
  469.7 94.0 %all-gather.18.cloned.1.call-start = ((), (), s32[]{:S(2)}) async-start(), calls=%async_computation.17 | async-start | bytes 2621440 | tf_op jit(solution)/shard_map/all_gather | solution.py:216
  518.3 140.6 %reduce-scatter.17.cloned.1.call-start = ((), (), s32[]{:S(2)}) async-start(), calls=%async_computation.18 | async-start | bytes 2621440 | tf_op jit(solution)/shard_map/reduce_scatter | solution.py:228
  610.0 51.0 %copy-start.10 = (f32[1024,1,4,64]{0,3,2,1:T(8,128)}, f32[1024,1,4,64]{0,3,2,1:T(8,128)S(1)}, u32[]{:S(2)}) copy-start(f32[1024,1,4,64]{0,3,2,1:T(8,128)S(1)} %get-tuple-element.204) | copy-start | bytes 3145732
  610.0 51.0 %copy-start.13 = (f32[1024,1,4,64]{0,3,2,1:T(8,128)}, f32[1024,1,4,64]{0,3,2,1:T(8,128)S(1)}, u32[]{:S(2)}) copy-start(f32[1024,1,4,64]{0,3,2,1:T(8,128)S(1)} %get-tuple-element.205) | copy-start | bytes 3145732
  610.0 48.9 %copy-start.18 = (bf16[256,1,1024]{2,0,1:T(8,128)(2,1)S(1)}, bf16[256,1,1024]{2,0,1:T(8,128)(2,1)}, u32[]{:S(2)}) copy-start(bf16[256,1,1024]{2,0,1:T(8,128)(2,1)} %param.20) | copy-start | bytes 1572868
  610.0 48.9 %copy-start.21 = (bf16[256,1,1024]{2,0,1:T(8,128)(2,1)S(1)}, bf16[256,1,1024]{2,0,1:T(8,128)(2,1)}, u32[]{:S(2)}) copy-start(bf16[256,1,1024]{2,0,1:T(8,128)(2,1)} %reduce-scatter.9.cloned.1.call-done) | copy-start | bytes 1572868
  612.2 48.8 %copy-start.64 = (f32[256]{0:T(256)S(1)}, f32[256]{0:T(256)}, u32[]{:S(2)}) copy-start(f32[256]{0:T(256)} %copy-done.63) | copy-start | bytes 3076
  616.2 93.8 %all-gather.20.cloned.1.call-start = ((), (), s32[]{:S(2)}) async-start(), calls=%async_computation.19 | async-start | bytes 2621440 | tf_op jit(solution)/shard_map/all_gather | solution.py:236
  661.0 53.0 %copy-start.9 = (bf16[1024,1,4,64]{0,3,2,1:T(8,128)(2,1)S(1)}, bf16[1024,1,4,64]{0,3,2,1:T(8,128)(2,1)}, u32[]{:S(2)}) copy-start(bf16[1024,1,4,64]{0,3,2,1:T(8,128)(2,1)} %copy-done.8) | copy-start | bytes 1572868
  661.0 53.0 %copy-start.12 = (bf16[1024,1,4,64]{0,3,2,1:T(8,128)(2,1)S(1)}, bf16[1024,1,4,64]{0,3,2,1:T(8,128)(2,1)}, u32[]{:S(2)}) copy-start(bf16[1024,1,4,64]{0,3,2,1:T(8,128)(2,1)} %get-tuple-element.792) | copy-start | bytes 1572868
  661.0 53.0 %copy-start.20 = (bf16[1024,1,4,64]{0,3,2,1:T(8,128)(2,1)S(1)}, bf16[1024,1,4,64]{0,3,2,1:T(8,128)(2,1)}, u32[]{:S(2)}) copy-start(bf16[1024,1,4,64]{0,3,2,1:T(8,128)(2,1)} %get-tuple-element.796) | copy-start | bytes 1572868
  661.0 53.0 %copy-start.56 = (f32[2,1,4,512,1]{3,2,4,1,0:T(4,128)S(1)}, f32[2,1,4,512,1]{3,2,4,1,0:T(4,128)}, u32[]{:S(2)}) copy-start(f32[2,1,4,512,1]{3,2,4,1,0:T(4,128)} %copy-done.55) | copy-start | bytes 49156
  664.6 171.4 %reduce-scatter.19.cloned.1.call-start = ((), (), s32[]{:S(2)}) async-start(), calls=%async_computation.20 | async-start | bytes 2621440 | tf_op jit(solution)/shard_map/reduce_scatter | solution.py:248
  768.8 161.5 %reduce-scatter.23.cloned.1.call-start = ((), (), s32[]{:S(2)}) async-start(), calls=%async_computation.22 | async-start | bytes 18874368 | tf_op jit(solution)/shard_map/reduce_scatter | solution.py:138
  792.2 184.6 %reduce-scatter.21.cloned.1.call-start = ((), (), s32[]{:S(2)}) async-start(), calls=%async_computation.21 | async-start | bytes 2621440 | tf_op jit(solution)/shard_map/reduce_scatter | solution.py:251
  836.0 140.9 %copy-start.1 = (bf16[1024,1024]{1,0:T(8,128)(2,1)S(1)}, bf16[1024,1024]{1,0:T(8,128)(2,1)}, u32[]{:S(2)}) copy-start(bf16[1024,1024]{1,0:T(8,128)(2,1)} %param.28) | copy-start | bytes 6291460
  (74 other events, 312.4 us)
Sparse Core Ops, SparseCore 0:
  9.6 48.6 all-gather.7
  94.2 42.5 reduce-scatter.8
  138.4 45.2 all-gather.11
  185.8 44.6 all-gather.9
  259.4 42.5 reduce-scatter.10
  306.0 45.2 all-gather.13
  362.1 42.5 reduce-scatter.12
  412.2 45.2 all-gather.15
  469.8 42.5 reduce-scatter.14
  518.4 45.2 all-gather.17
  616.3 42.5 reduce-scatter.16
  664.7 45.2 all-gather.19
  768.9 42.5 reduce-scatter.18
  814.9 115.2 reduce-scatter.22
  933.0 43.8 reduce-scatter.20
where the time goes:
time: 992 us; the launch traced here: 984 us
  waiting for transfers between devices  655 us (66%)
  matrix products  147 us (15%)
  other arithmetic  55.3 us (6%)
  local copies, waits for them, and re-layouts  53.6 us (5%)
  blocking collectives  39.7 us (4%)
  loops' own time  16.6 us (2%)
  between operations  15.1 us (2%)
    reduce_scatter x1, waiting for transfers between devices, sum_weights(): summed = lax.psum_scatter(joined, 'dp', scatter_dimension=0, tiled=True)  92 us
    all_gather x1, waiting for transfers between devices, local(): lax.all_gather(tokens, 'mp', axis=0, tiled=True)  47.7 us
    all_gather x1, waiting for transfers between devices, local(): full_second = lax.all_gather(second_low, 'mp', axis=0, tiled=True)  45.4 us
    all_gather x1, waiting for transfers between devices, local(): lax.all_gather(third_grad.astype(jnp.bfloat16), 'mp', axis=0, tiled=True)  45.4 us
    all_gather x1, waiting for transfers between devices, local(): lax.all_gather(self_grad.astype(jnp.bfloat16), 'mp', axis=0, tiled=True)  45.3 us
    all_gather x1, waiting for transfers between devices, local(): lax.all_gather(cross_grad.astype(jnp.bfloat16), 'mp', axis=0, tiled=True)  45.2 us
    all_gather x1, waiting for transfers between devices, local(): full_first = lax.all_gather(first_low, 'mp', axis=0, tiled=True)  43.8 us
    reduce_scatter x1, waiting for transfers between devices, local(): lax.psum_scatter(rows_times(cross_queries_grad, cross_q).astype(jnp.bfloa...  42.7 us
  transfers between devices with their start and end apart: 15, of which 14 were waited for; matrix products, arithmetic and copies ran while one was open for 5% of the time, Pallas kernels for 0%

commit v1 on v0

v1 whole, which is shorter than its diff:
```python
import functools
import math

import jax
import jax.numpy as jnp
from jax import lax
from jax.experimental import pallas as pl
from jax.experimental.pallas import tpu as pltpu
from jax.sharding import PartitionSpec as P

HD = 64
CELLS = 8
BITS = (2, 4)
LOW = jnp.bfloat16
WIDE = jnp.float32
SELF_BLOCKS = (512, 512)
CROSS_BLOCKS = (1024, 256)
SELF_BACK_BLOCKS = (512, 512)
CROSS_BACK_BLOCKS = (1024, 256)
VMEM_LIMIT = 56 * 2**20

alpha_scale = 300.0**0.25
norm_eps = 1e-05

NN = (((1,), (0,)), ((), ()))
NT = (((1,), (1,)), ((), ()))
TN = (((0,), (0,)), ((), ()))


def dense(left, weight):
    return jnp.einsum("td,df->tf", left, weight, preferred_element_type=WIDE)


def weight_grad(left, grad):
    return jnp.einsum("td,tf->df", left, grad, preferred_element_type=WIDE).astype(LOW)


def back_dense(grad, weight):
    return jnp.einsum("tf,df->td", grad, weight, preferred_element_type=WIDE)


def mm(left, right, dims):
    return lax.dot_general(left, right, dims, preferred_element_type=WIDE)


def keep_head(value, head):
    at = lax.broadcasted_iota(jnp.int32, value.shape, 1) // HD
    return jnp.where(at == head, value, jnp.zeros_like(value))


def masked(scores, key_begin, query_begin):
    key_at = lax.broadcasted_iota(jnp.int32, scores.shape, 0) + key_begin
    query_at = lax.broadcasted_iota(jnp.int32, scores.shape, 1) + query_begin
    return jnp.where(key_at <= query_at, scores, -1000000000.0)


def key_blocks(body, carry, query_block, key_block, keys, causal):
    if not causal:
        for j in range(keys // key_block):
            carry = body(j, carry, False)
        return carry
    per = query_block // key_block
    begin = pl.program_id(1) * per
    carry = lax.fori_loop(0, begin, lambda j, c: body(j, c, False), carry)
    for e in range(per):
        carry = body(begin + e, carry, True)
    return carry


def attend_kernel(q_ref, k_ref, v_ref, o_ref, lse_ref, *, key_block, causal):
    query_block = q_ref.shape[0]
    query_begin = pl.program_id(1) * query_block
    q = q_ref[...] * jnp.asarray(1.0 / math.sqrt(HD), LOW)

    def body(j, carry, diagonal):
        tops, sums, acc = carry[:2], carry[2:4], carry[4]
        at = pl.multiple_of(j * key_block, key_block)
        k, v = k_ref[pl.ds(at, key_block), :], v_ref[pl.ds(at, key_block), :]
        new_tops, new_sums, shrink, parts = [], [], [], []
        for head in (0, 1):
            s = mm(keep_head(k, head), q, NT)
            if diagonal:
                s = masked(s, j * key_block, query_begin)
            top = jnp.maximum(tops[head], jnp.max(s, axis=0, keepdims=True))
            p = jnp.exp(s - top)
            factor = jnp.exp(tops[head] - top)
            new_tops.append(top)
            new_sums.append(sums[head] * factor + jnp.sum(p, axis=0, keepdims=True))
            shrink.append(factor)
            parts.append(mm(keep_head(v, head), p.astype(LOW), TN))
        upper = lax.broadcasted_iota(jnp.int32, acc.shape, 0) < HD
        acc = acc * jnp.where(upper, shrink[0], shrink[1]) + (parts[0] + parts[1])
        return (*new_tops, *new_sums, acc)

    low = jnp.full((1, query_block), -1e30, WIDE)
    zero = jnp.zeros((1, query_block), WIDE)
    start = (low, low, zero, zero, jnp.zeros((2 * HD, query_block), WIDE))
    top0, top1, sum0, sum1, acc = key_blocks(
        body, start, query_block, key_block, k_ref.shape[0], causal
    )
    upper = lax.broadcasted_iota(jnp.int32, acc.shape, 0) < HD
    o_ref[...] = (acc * jnp.where(upper, 1.0 / sum0, 1.0 / sum1)).T.astype(LOW)
    lse_ref[0] = jnp.concatenate(
        [top0 + jnp.log(sum0), top1 + jnp.log(sum1), jnp.zeros((6, query_block), WIDE)], axis=0
    )


def attend_back_kernel(
    q_ref, g_ref, o_ref, lse_ref, k_ref, v_ref, dq_ref, dk_ref, dv_ref, dk_acc, dv_acc, *, key_block, causal
):
    query_block = q_ref.shape[0]
    query_begin = pl.program_id(1) * query_block

    @pl.when(pl.program_id(1) == 0)
    def _():
        dk_acc[...] = jnp.zeros_like(dk_acc)
        dv_acc[...] = jnp.zeros_like(dv_acc)

    q = q_ref[...] * jnp.asarray(1.0 / math.sqrt(HD), LOW)
    g = g_ref[...]
    q_heads = [keep_head(q, head) for head in (0, 1)]
    g_heads = [keep_head(g, head) for head in (0, 1)]
    picks = lax.broadcasted_iota(jnp.int32, (8, 2 * HD), 1) // HD
    picks = (picks == lax.broadcasted_iota(jnp.int32, (8, 2 * HD), 0)).astype(WIDE)
    inner = lax.dot_general(
        picks,
        g.astype(WIDE) * o_ref[...].astype(WIDE),
        NT,
        precision=lax.Precision.HIGHEST,
        preferred_element_type=WIDE,
    )
    lse = lse_ref[0]

    def body(j, dq, diagonal):
        at = pl.multiple_of(j * key_block, key_block)
        k, v = k_ref[pl.ds(at, key_block), :], v_ref[pl.ds(at, key_block), :]
        dk, dv = dk_acc[pl.ds(at, key_block), :], dv_acc[pl.ds(at, key_block), :]
        for head in (0, 1):
            k_head = keep_head(k, head)
            s = mm(k_head, q, NT)
            if diagonal:
                s = masked(s, j * key_block, query_begin)
            p = jnp.exp(s - lse[head : head + 1])
            dp = mm(keep_head(v, head), g, NT)
            ds = (p * (dp - inner[head : head + 1])).astype(LOW)
            dv = dv + mm(p.astype(LOW), g_heads[head], NN)
            dk = dk + mm(ds, q_heads[head], NN)
            dq = dq + mm(k_head, ds, TN)
        dk_acc[pl.ds(at, key_block), :] = dk
        dv_acc[pl.ds(at, key_block), :] = dv
        return dq

    dq = key_blocks(
        body, jnp.zeros((2 * HD, query_block), WIDE), query_block, key_block, k_ref.shape[0], causal
    )
    dq_ref[...] = (dq * (1.0 / math.sqrt(HD))).T.astype(LOW)

    @pl.when(pl.program_id(1) == pl.num_programs(1) - 1)
    def _():
        dk_ref[...] = dk_acc[...].astype(LOW)
        dv_ref[...] = dv_acc[...].astype(LOW)


def columns_of(rows, first, whole):
    if whole:
        return pl.BlockSpec((rows, 2 * HD), lambda p, i: (0, first + p))
    return pl.BlockSpec((rows, 2 * HD), lambda p, i: (i, first + p))


def attend(width, queries, keys, values, causal, query_block, key_block):
    seq, span = queries[0].shape[0], keys[0].shape[0]
    pairs = width // (2 * HD)
    return pl.pallas_call(
        functools.partial(attend_kernel, key_block=key_block, causal=causal),
        grid=(pairs, seq // query_block),
        in_specs=[
            columns_of(query_block, queries[1], False),
            columns_of(span, keys[1], True),
            columns_of(span, values[1], True),
        ],
        out_specs=[
            columns_of(query_block, 0, False),
            pl.BlockSpec((1, 8, query_block), lambda p, i: (p, 0, i)),
        ],
        out_shape=[
            jax.ShapeDtypeStruct((seq, width), LOW),
            jax.ShapeDtypeStruct((pairs, 8, seq), WIDE),
        ],
        compiler_params=pltpu.CompilerParams(vmem_limit_bytes=VMEM_LIMIT),
        cost_estimate=pl.CostEstimate(
            flops=8 * seq * span * width, bytes_accessed=8 * seq * width, transcendentals=0
        ),
        name="attend",
    )(queries[0], keys[0], values[0])


def attend_back(width, queries, keys, values, grad, result, lse, causal, query_block, key_block):
    seq, span = queries[0].shape[0], keys[0].shape[0]
    pairs = width // (2 * HD)
    whole = columns_of(span, 0, True)
    return pl.pallas_call(
        functools.partial(attend_back_kernel, key_block=key_block, causal=causal),
        grid=(pairs, seq // query_block),
        in_specs=[
            columns_of(query_block, queries[1], False),
            columns_of(query_block, 0, False),
            columns_of(query_block, 0, False),
            pl.BlockSpec((1, 8, query_block), lambda p, i: (p, 0, i)),
            columns_of(span, keys[1], True),
            columns_of(span, values[1], True),
        ],
        out_specs=[columns_of(query_block, 0, False), whole, whole],
        out_shape=[
            jax.ShapeDtypeStruct((seq, width), LOW),
            jax.ShapeDtypeStruct((span, width), LOW),
            jax.ShapeDtypeStruct((span, width), LOW),
        ],
        scratch_shapes=[pltpu.VMEM((span, 2 * HD), WIDE), pltpu.VMEM((span, 2 * HD), WIDE)],
        compiler_params=pltpu.CompilerParams(vmem_limit_bytes=VMEM_LIMIT),
        cost_estimate=pl.CostEstimate(
            flops=16 * seq * span * width, bytes_accessed=16 * seq * width, transcendentals=0
        ),
        name="attend_back",
    )(queries[0], grad, result, lse, keys[0], values[0])


def normalized(value):
    center = value - jnp.mean(value, axis=-1, keepdims=True)
    scale = lax.rsqrt(jnp.mean(center * center, axis=-1, keepdims=True) + norm_eps)
    return center * scale, scale


def norm_back(grad, gain, n, scale):
    e = grad * gain
    mean_e = jnp.mean(e, axis=-1, keepdims=True)
    mean_en = jnp.mean(e * n, axis=-1, keepdims=True)
    terms = jnp.concatenate(
        [jnp.sum(grad * n, axis=0, keepdims=True), jnp.sum(grad, axis=0, keepdims=True)], axis=0
    )
    return (e - mean_e - n * mean_en) * scale, terms


def gelu_with_slope(value):
    c = math.sqrt(2.0 / math.pi)
    square = value * value
    t = jnp.tanh(c * value * (1.0 + 0.044715 * square))
    half = 0.5 * (1.0 + t)
    slope = half + 0.5 * value * (1.0 - t * t) * (c * (1.0 + 3 * 0.044715 * square))
    return value * half, slope


def cell_copies(parts, first, target, sems, pick):
    cell = lax.rem(lax.axis_index("dp"), CELLS)
    rows = target.shape[-2] // CELLS
    copies = []
    for j in range(CELLS):
        part = parts[(j & 1) * 2 + (1 if j & (6 - first) else 0)].at[1 if j & first else 0]
        at = pl.multiple_of(jnp.bitwise_xor(cell, j) * rows, rows)
        copies.append(pltpu.make_async_copy(*pick(part, target, pl.ds(at, rows)), sems.at[j]))
    return copies


def start_all(copies):
    for copy in copies:
        copy.start()


def wait_all(copies):
    for copy in copies:
        copy.wait()


def enter_cross_kernel(
    tokens_ref, gain_ref, bias_ref, *refs, width, count
):
    attended, refs = refs[:count], refs[count:]
    parts, refs = refs[:4], refs[4:]
    n_ref, scale_ref, low_ref = refs[:3]
    queries, (weights, sems) = refs[3 : 3 + count], refs[3 + count :]
    copies = cell_copies(parts, 2, weights, sems, lambda part, to, at: (part, to.at[:, at, :]))
    shards = [jnp.bitwise_xor(lax.axis_index("mp"), k) for k in range(count)]
    start_all(copies)
    value = alpha_scale * tokens_ref[...].astype(WIDE)
    wait_all(copies)
    for k in range(count):
        value = value + mm(attended[k][...], weights[shards[k], :, :width], NT)
    n, scale = normalized(value)
    n_ref[...] = n
    scale_ref[...] = jnp.broadcast_to(scale, scale_ref.shape)
    low = (n * gain_ref[0:1, :] + bias_ref[0:1, :]).astype(LOW)
    low_ref[...] = low
    for k in range(count):
        queries[k][...] = mm(low, weights[shards[k], :, width:], NN).astype(LOW)


def leave_cross_kernel(
    cross_grad_ref, gain_ref, n_ref, scale_ref, *refs, width, count
):
    queries, refs = refs[:count], refs[count:]
    parts, refs = refs[:4], refs[4:]
    self_grad_ref, low_ref, terms_ref = refs[:3]
    grads, (weights, sems) = refs[3 : 3 + count], refs[3 + count :]
    copies = cell_copies(parts, 2, weights, sems, lambda part, to, at: (part, to.at[:, at, :]))
    shards = [jnp.bitwise_xor(lax.axis_index("mp"), k) for k in range(count)]
    start_all(copies)
    grad = alpha_scale * cross_grad_ref[...]
    wait_all(copies)
    for k in range(count):
        grad = grad + mm(queries[k][...], weights[shards[k], :, width:], NT)
    self_grad, terms_ref[...] = norm_back(grad, gain_ref[0:1, :], n_ref[...], scale_ref[:, :1])
    self_grad_ref[...] = self_grad
    low = self_grad.astype(LOW)
    low_ref[...] = low
    for k in range(count):
        grads[k][...] = mm(low, weights[shards[k], :, :width], NN).astype(LOW)


def feed_forward_kernel(
    first_n_ref, cotangent_ref, gain_ref, bias_ref, *refs, width, count
):
    attended, refs = refs[:count], refs[count:]
    parts, refs = (refs[:4], refs[4:8]), refs[8:]
    mixed_ref, second_low_ref, third_low_ref, cross_grad_ref, cross_low_ref, terms_ref = refs[:6]
    act_ref, hidden_grad_ref = refs[6:8]
    grads, refs = refs[8 : 8 + count], refs[8 + count :]
    w_in, w_out, w_cross, slope_ref, sum_ref, in_sems, out_sems, cross_sems = refs
    hidden = w_in.shape[2]
    chunk = min(512, hidden)
    half = count // 2

    shards = [jnp.bitwise_xor(lax.axis_index("mp"), k) for k in range(count)]

    cross_copies = []
    for h in range(2):
        cross_copies += cell_copies(
            parts[h],
            BITS[h],
            w_cross,
            cross_sems.at[h],
            lambda part, to, at: (part.at[:, :, 2 * hidden :], to.at[pl.ds(h * half, half), at, :]),
        )
    start_all(cross_copies)
    in_copies, out_copies = [], []
    for s in range(count):
        h = s // half
        in_copies.append(
            cell_copies(
                parts[h],
                BITS[h],
                w_in,
                in_sems.at[s],
                lambda part, to, at: (part.at[s % half, :, :hidden], to.at[s, at, :]),
            )
        )
        out_copies.append(
            cell_copies(
                parts[h],
                BITS[h],
                w_out,
                out_sems.at[s],
                lambda part, to, at: (part.at[s % half, :, hidden : 2 * hidden], to.at[s, at, :]),
            )
        )
        start_all(in_copies[s])
        start_all(out_copies[s])

    second = alpha_scale * (first_n_ref[...] * gain_ref[0:1, :] + bias_ref[0:1, :])
    wait_all(cross_copies)
    for k in range(count):
        second = second + mm(attended[k][...], w_cross[shards[k]], NT)
    second_n, second_scale = normalized(second)
    second = second_n * gain_ref[1:2, :] + bias_ref[1:2, :]
    second_low = second.astype(LOW)
    second_low_ref[...] = second_low
    sum_ref[...] = alpha_scale * second
    for k in range(count):
        wait_all(in_copies[k])
        for begin in range(0, hidden, chunk):
            cut = slice(begin, begin + chunk)
            value = mm(second_low, w_in[k, :, cut], NN)
            act, slope = gelu_with_slope(value)
            slope_ref[k, :, cut] = slope
            act_ref[k, :, cut] = act.astype(LOW)
        wait_all(out_copies[k])
        sum_ref[...] += mm(act_ref[k], w_out[k], NT)
    third_n, third_scale = normalized(sum_ref[...])
    mixed_ref[...] = (third_n * gain_ref[2:3, :] + bias_ref[2:3, :]).astype(LOW)
    third_grad, third_terms = norm_back(
        cotangent_ref[...].astype(WIDE), gain_ref[2:3, :], third_n, third_scale
    )
    third_low = third_grad.astype(LOW)
    third_low_ref[...] = third_low
    sum_ref[...] = alpha_scale * third_grad
    for k in range(count):
        for begin in range(0, hidden, chunk):
            cut = slice(begin, begin + chunk)
            act_grad = mm(third_low, w_out[k, :, cut], NN).astype(LOW).astype(WIDE)
            hidden_grad_ref[k, :, cut] = (act_grad * slope_ref[k, :, cut]).astype(LOW)
        sum_ref[...] += mm(hidden_grad_ref[k], w_in[k], NT)
    cross_grad, second_terms = norm_back(sum_ref[...], gain_ref[1:2, :], second_n, second_scale)
    terms_ref[...] = jnp.concatenate([second_terms, third_terms], axis=0)
    cross_grad_ref[...] = cross_grad
    cross_low = cross_grad.astype(LOW)
    cross_low_ref[...] = cross_low
    for k in range(count):
        grads[k][...] = mm(cross_low, w_cross[shards[k]], NN).astype(LOW)


def call(kernel, operands, streamed, results, scratch, flops, name):
    here, there = pl.BlockSpec(memory_space=pltpu.VMEM), pl.BlockSpec(memory_space=pl.ANY)
    arrays = [*operands, *streamed]
    size = sum(v.size * v.dtype.itemsize for v in arrays)
    return pl.pallas_call(
        kernel,
        in_specs=[here] * len(operands) + [there] * len(streamed),
        out_specs=[here] * len(results),
        out_shape=[jax.ShapeDtypeStruct(shape, dtype) for shape, dtype in results],
        scratch_shapes=scratch,
        compiler_params=pltpu.CompilerParams(vmem_limit_bytes=VMEM_LIMIT),
        cost_estimate=pl.CostEstimate(flops=flops, bytes_accessed=size, transcendentals=0),
        name=name,
    )(*arrays)


def enter_cross(tokens, gain, bias, attended, parts):
    rows, model = tokens.shape
    count, width = len(attended), attended[0].shape[1]
    return call(
        functools.partial(enter_cross_kernel, width=width, count=count),
        [tokens, gain, bias, *attended],
        parts,
        [((rows, model), WIDE), ((rows, 128), WIDE), ((rows, model), LOW)]
        + [((rows, width), LOW)] * count,
        [
            pltpu.VMEM((count, model, 2 * width), LOW),
            pltpu.SemaphoreType.DMA((CELLS,)),
        ],
        4 * rows * model * width * count,
        "enter_cross",
    )


def leave_cross(cross_grad, gain, n, scale, queries, parts):
    rows, model = n.shape
    count, width = len(queries), queries[0].shape[1]
    return call(
        functools.partial(leave_cross_kernel, width=width, count=count),
        [cross_grad, gain, n, scale, *queries],
        parts,
        [((rows, model), WIDE), ((rows, model), LOW), ((2, model), WIDE)]
        + [((rows, width), LOW)] * count,
        [
            pltpu.VMEM((count, model, 2 * width), LOW),
            pltpu.SemaphoreType.DMA((CELLS,)),
        ],
        4 * rows * model * width * count,
        "leave_cross",
    )


def feed_forward(first_n, cotangent, gain, bias, attended, hidden, parts):
    rows, model = first_n.shape
    count, width = len(attended), attended[0].shape[1]
    sems = pltpu.SemaphoreType.DMA((count, CELLS))
    return call(
        functools.partial(feed_forward_kernel, width=width, count=count),
        [first_n, cotangent, gain, bias, *attended],
        [*parts[0], *parts[1]],
        [
            ((rows, model), LOW),
            ((rows, model), LOW),
            ((rows, model), LOW),
            ((rows, model), WIDE),
            ((rows, model), LOW),
            ((4, model), WIDE),
            ((count, rows, hidden), LOW),
            ((count, rows, hidden), LOW),
        ]
        + [((rows, width), LOW)] * count,
        [
            pltpu.VMEM((count, model, hidden), LOW),
            pltpu.VMEM((count, model, hidden), LOW),
            pltpu.VMEM((count, model, width), LOW),
            pltpu.VMEM((count, rows, hidden), WIDE),
            pltpu.VMEM((rows, model), WIDE),
            sems,
            sems,
            pltpu.SemaphoreType.DMA((2, CELLS)),
        ],
        8 * rows * model * hidden * count,
        "feed_forward",
    )


def weight_grads_kernel(*refs, other_core):
    count = (len(refs) - 2) // 2
    lefts, rights, out_ref, turned = refs[:count], refs[count:-2], refs[-2], refs[-1]
    block = turned.shape[1] // (CELLS // 2)

    @pl.when(pl.program_id(0) == 0)
    def _():
        cell = lax.rem(lax.axis_index("dp"), CELLS)
        for i, left in enumerate(lefts):
            for c in range(CELLS // 2):
                at = jnp.bitwise_xor(cell, 2 * c + other_core) * block
                columns = left[:, pl.ds(pl.multiple_of(at, block), block)]
                turned[i, c * block : (c + 1) * block, :] = columns.T

    at = 0
    for i, right in enumerate(rights):
        width = right.shape[2]
        value = mm(turned[i], right[0], NN).astype(LOW)
        out_ref[0, :, :, at : at + width] = value.reshape(CELLS // 2, block, width)
        at += width


def weight_grads(lefts, rights, relative, shards, other_core):
    rows, model = lefts[0].shape
    count, block = len(shards), model // CELLS
    width = sum(right.shape[2] for right in rights)

    def right_at(flag):
        def at(s, mp):
            shard = s + shards[0]
            return (jnp.bitwise_xor(shard, mp[0]) if flag else shard), 0, 0

        return at

    return pl.pallas_call(
        lambda mp, *refs: weight_grads_kernel(*refs, other_core=other_core),
        grid_spec=pltpu.PrefetchScalarGridSpec(
            num_scalar_prefetch=1,
            grid=(count,),
            in_specs=[pl.BlockSpec((rows, model), lambda s, mp: (0, 0))] * len(lefts)
            + [
                pl.BlockSpec((1, rows, right.shape[2]), right_at(flag))
                for right, flag in zip(rights, relative)
            ],
            out_specs=pl.BlockSpec((1, CELLS // 2, block, width), lambda s, mp: (s, 0, 0, 0)),
            scratch_shapes=[pltpu.VMEM((len(lefts), model // 2, rows), LOW)],
        ),
        out_shape=jax.ShapeDtypeStruct((count, CELLS // 2, block, width), LOW),
        compiler_params=pltpu.CompilerParams(vmem_limit_bytes=VMEM_LIMIT),
        cost_estimate=pl.CostEstimate(
            flops=rows * model * width * count,
            bytes_accessed=count * model * width,
            transcendentals=0,
        ),
        name="weight_grads",
    )(lax.axis_index("mp").astype(jnp.int32).reshape(1), *lefts, *rights)


def pass_kernel(*refs):
    del refs


def after(values, *others):
    keep = pl.BlockSpec(memory_space=pl.ANY)
    count = len(values)
    return pl.pallas_call(
        pass_kernel,
        in_specs=[keep] * (count + len(others)),
        out_specs=[keep] * count,
        out_shape=[jax.ShapeDtypeStruct(v.shape, v.dtype) for v in values],
        input_output_aliases={i: i for i in range(count)},
        cost_estimate=pl.CostEstimate(flops=0, bytes_accessed=0, transcendentals=0),
        name="order",
    )(*values, *others)


class Layout:
    def __init__(self, dp, mp):
        self.dp, self.mp = dp, mp

    def permute(self, value, move):
        pairs = []
        for d in range(self.dp):
            for m in range(self.mp):
                to_d, to_m = move(d, m)
                pairs.append((d * self.mp + m, to_d * self.mp + to_m))
        return lax.ppermute(value, ("dp", "mp"), pairs)

    def flip(self, value, bits):
        return self.permute(value, lambda d, m: (d ^ bits, m))

    def flip_mp(self, value, bits):
        return self.permute(value, lambda d, m: (d, m ^ bits))

    def cell(self):
        return lax.rem(lax.axis_index("dp"), CELLS)

    def swap_mp(self, blocks):
        return [b if k == 0 else self.flip_mp(b, k) for k, b in enumerate(blocks)]

    def rows_for(self, value):
        rows = value.shape[0] // self.mp
        me = lax.axis_index("mp")
        return [
            lax.dynamic_slice_in_dim(value, jnp.bitwise_xor(me, k) * rows, rows, 0)
            for k in range(self.mp)
        ]

    def in_order(self, blocks):
        rows = blocks[0].shape[0]
        me = lax.axis_index("mp")
        out = jnp.zeros((rows * self.mp,) + blocks[0].shape[1:], blocks[0].dtype)
        for k, b in enumerate(blocks):
            out = lax.dynamic_update_slice_in_dim(out, b, jnp.bitwise_xor(me, k) * rows, 0)
        return out

    def piece(self, slab):
        rows = slab.shape[0] // CELLS
        return lax.dynamic_slice_in_dim(slab, self.cell() * rows, rows, 0)

    def near(self, here, bit):
        return jnp.stack([here, self.flip(here, bit)])

    def core_halves(self, left):
        rows = left.shape[1] // CELLS
        cell = self.cell()
        parts = [
            lax.dynamic_slice_in_dim(left, jnp.bitwise_xor(cell, j) * rows, rows, 1)
            for j in range(CELLS)
        ]
        return jnp.concatenate(parts[0::2], axis=1), jnp.concatenate(parts[1::2], axis=1)

    def fold(self, value, got):
        return (value.astype(WIDE) + got.astype(WIDE)).astype(LOW)

    def chip_halves(self, value, bit):
        count, width = value.shape[0], value.shape[-1]
        value = value.reshape(count, 2, 2, -1, width)
        if bit == 2:
            return value[:, :, 0], value[:, :, 1]
        return value[:, 0], value[:, 1]

    def last_halves(self, value):
        return value[:, 0], value[:, 1]

    def to_rows(self, mine):
        groups = self.dp // CELLS
        if groups == 1:
            return mine
        mine = lax.psum_scatter(
            mine,
            "dp",
            scatter_dimension=1,
            tiled=True,
            axis_index_groups=[[g * CELLS + c for g in range(groups)] for c in range(CELLS)],
        )
        return self.permute(mine, lambda d, m: ((d % CELLS) * groups + d // CELLS, m))

    def sum_all(self, value):
        step = 1
        while step < self.dp:
            value = value + self.flip(value, step)
            step *= 2
        step = 1
        while step < self.mp:
            value = value + self.flip_mp(value, step)
            step *= 2
        return value


def local(
    layout,
    tokens,
    memory,
    self_qkv,
    self_out,
    cross_q,
    cross_kv,
    cross_out,
    ffn_in,
    ffn_out,
    ln_gain,
    ln_bias,
    cotangent,
):
    model_width = tokens.shape[2]
    w = self_out.shape[1]
    n = layout.mp
    tokens, memory, cotangent = (
        v.reshape(v.shape[0], model_width) for v in (tokens, memory, cotangent)
    )
    rows = tokens.shape[0]
    qkv_flat = self_qkv.reshape(model_width, 3 * w)
    kv_flat = cross_kv.reshape(model_width, 2 * w)
    n_hidden = ffn_in.shape[1]
    half = n // 2
    pieces = [layout.piece(v) for v in (self_out, cross_q, ffn_in, ffn_out, cross_out)]
    weights = lax.all_gather(jnp.concatenate(pieces, axis=1), "mp", axis=0, tiled=False)
    (tokens_there,) = after([tokens], weights)
    full_tokens = lax.all_gather(tokens_there, "mp", axis=0, tiled=True)
    attn_here = layout.near(weights[:, :, : 2 * w], 2)
    ffn_own = after(
        [weights[h * half : (h + 1) * half, :, 2 * w :] for h in range(2)], attn_here
    )
    attn_there = layout.flip(attn_here, 4)
    ffn_here = [layout.near(part, bit) for part, bit in zip(ffn_own, BITS)]
    full_tokens, *ffn_here = after([full_tokens, *ffn_here], weights)
    (memory_there,) = after([memory], full_tokens)
    full_memory = lax.all_gather(memory_there, "mp", axis=0, tiled=True)

    projected = dense(full_tokens, qkv_flat).astype(LOW)
    pairs = w // (2 * HD)
    self_operands = (projected, 0), (projected, pairs), (projected, 2 * pairs)
    home_attended, self_logs = attend(w, *self_operands, True, *SELF_BLOCKS)
    attended_blocks = layout.swap_mp(layout.rows_for(home_attended))
    attn_here, attn_there = after([attn_here, attn_there], home_attended)
    ffn_there = [layout.flip(part, 6 - bit) for part, bit in zip(ffn_here, BITS)]
    attn_parts = [attn_here, attn_there, layout.flip(attn_here, 1), layout.flip(attn_there, 1)]
    first_n, first_scale, first_low, *query_blocks = enter_cross(
        tokens, ln_gain, ln_bias, attended_blocks, attn_parts
    )
    query_blocks = layout.swap_mp(query_blocks)
    cross_queries = jnp.concatenate(query_blocks)
    ffn_here_other = [layout.flip(part, 1) for part in ffn_here]
    cross_pair = dense(full_memory, kv_flat).astype(LOW)
    cross_operands = (cross_queries, 0), (cross_pair, 0), (cross_pair, pairs)
    home_cross, cross_logs = attend(w, *cross_operands, False, *CROSS_BLOCKS)
    ffn_there = after(ffn_there, home_cross)
    ffn_there_other = [layout.flip(part, 1) for part in ffn_there]
    ffn_parts = list(zip(ffn_here, ffn_there, ffn_here_other, ffn_there_other))
    cross_blocks = layout.swap_mp(list(home_cross.reshape(n, rows, w)))
    (
        mixed,
        second_low,
        third_low,
        cross_grad,
        cross_grad_low,
        later_terms,
        activation,
        hidden_grad,
        *cross_grad_blocks,
    ) = feed_forward(
        first_n, cotangent, ln_gain, ln_bias, cross_blocks, n_hidden, ffn_parts
    )
    cross_grad_blocks = layout.swap_mp(cross_grad_blocks)
    cross_attended = jnp.stack(cross_blocks)

    def fold_chip(pair, bit):
        return layout.chip_halves(layout.fold(*pair), bit)

    def send(pair, bit):
        return pair[0], layout.flip(pair[1], bit)

    def fold_last(pair):
        return layout.last_halves(layout.fold(*pair))

    ffn_grads = functools.partial(
        weight_grads,
        [second_low, third_low, cross_grad_low],
        [hidden_grad, activation, cross_attended],
        [False, False, True],
    )
    cuts = (range(0, half), range(half, n))
    ffn_sums = [send((None, ffn_grads(cut, 1)), 1)[1] for cut in cuts]
    ffn_sums = [(ffn_grads(cut, 0), got) for cut, got in zip(cuts, ffn_sums)]
    (cross_attended_grad,) = after(
        [jnp.concatenate(cross_grad_blocks)], *(here for here, _ in ffn_sums)
    )
    cross_queries_grad, cross_keys_grad, cross_values_grad = attend_back(
        w, *cross_operands, cross_attended_grad, home_cross, cross_logs, False, *CROSS_BACK_BLOCKS
    )
    first_terms = layout.swap_mp(list(cross_queries_grad.reshape(n, rows, w)))
    cross_pair_grad = jnp.concatenate([cross_keys_grad, cross_values_grad], axis=-1)
    memory_term = back_dense(cross_pair_grad, kv_flat).astype(LOW)
    memory_grad = lax.psum_scatter(memory_term, "mp", scatter_dimension=0, tiled=True)
    ffn_sums = [fold_chip(pair, bit) for pair, bit in zip(ffn_sums, BITS)]
    first_terms[1:] = after(first_terms[1:], memory_term, *(there for _, there in ffn_sums))
    ffn_sums = [send(pair, bit) for pair, bit in zip(ffn_sums, BITS)]
    self_grad, self_grad_low, first_norm_terms, *attended_grad_blocks = leave_cross(
        cross_grad, ln_gain, first_n, first_scale, first_terms, attn_parts
    )
    attended_grad = layout.in_order(layout.swap_mp(attended_grad_blocks))
    attn_grads = functools.partial(
        weight_grads,
        [self_grad_low, first_low],
        [jnp.stack(attended_blocks), jnp.stack(first_terms)],
        [True, True],
        range(n),
    )
    attn_here, attn_there = attn_grads(0), attn_grads(1)
    (attended_grad,) = after([attended_grad], attn_here, attn_there, memory_grad)
    attn_sum = attn_here, layout.flip(attn_there, 1)
    queries_grad, keys_grad, values_grad = attend_back(
        w, *self_operands, attended_grad, home_attended, self_logs, True, *SELF_BACK_BLOCKS
    )
    projected_grad = jnp.concatenate([queries_grad, keys_grad, values_grad], axis=-1)
    token_term = back_dense(projected_grad, qkv_flat).astype(LOW)
    token_part = lax.psum_scatter(token_term, "mp", scatter_dimension=0, tiled=True)
    token_grad = (alpha_scale * self_grad + token_part.astype(WIDE)).astype(LOW)
    home_grads = [
        jnp.concatenate(
            [weight_grad(a, cross_pair_grad), weight_grad(b, projected_grad)], axis=1
        )[None]
        for a, b in zip(layout.core_halves(full_memory), layout.core_halves(full_tokens))
    ]
    ffn_sums = [fold_last(pair) for pair in ffn_sums]
    ffn_sums = [send(pair, 6 - bit) for pair, bit in zip(ffn_sums, BITS)]
    attn_sum = send(fold_chip(attn_sum, 2), 2)
    home_sum = send(fold_chip((home_grads[0], layout.flip(home_grads[1], 1)), 4), 4)
    attn_sum = send(fold_last(attn_sum), 4)
    home_sum = send(fold_last(home_sum), 2)
    ffn_sums = jnp.concatenate([layout.fold(*pair) for pair in ffn_sums])
    shards = jnp.concatenate([layout.fold(*attn_sum), ffn_sums], axis=2)
    shard = lax.psum_scatter(shards, "mp", scatter_dimension=0, tiled=True)
    shard = layout.to_rows(shard)[0].astype(WIDE)
    home_grad = layout.to_rows(layout.fold(*home_sum))[0].astype(WIDE)
    sums = layout.sum_all(jnp.concatenate([first_norm_terms, later_terms]))
    edges = (w, 2 * w, 2 * w + n_hidden, 2 * w + 2 * n_hidden)
    self_out_grad, cross_q_grad, ffn_in_grad, ffn_out_grad, cross_out_grad = jnp.split(
        shard, edges, axis=1
    )
    return (
        mixed[:, None],
        token_grad[:, None],
        memory_grad[:, None],
        home_grad[:, 2 * w :].reshape(-1, 3, w),
        self_out_grad,
        cross_q_grad,
        home_grad[:, : 2 * w].reshape(-1, 2, w),
        cross_out_grad,
        ffn_in_grad,
        ffn_out_grad,
        sums[0::2],
        sums[1::2],
    )


def solution(mesh):
    layout = Layout(mesh.shape["dp"], mesh.shape["mp"])
    in_specs = (
        P("mp", "dp", None),
        P("mp", "dp", None),
        P(None, None, "mp"),
        P(None, "mp"),
        P(None, "mp"),
        P(None, None, "mp"),
        P(None, "mp"),
        P(None, "mp"),
        P(None, "mp"),
        P(),
        P(),
        P("mp", "dp", None),
    )
    out_specs = (
        P("mp", "dp", None),
        P("mp", "dp", None),
        P("mp", "dp", None),
        P("dp", None, "mp"),
        P("dp", "mp"),
        P("dp", "mp"),
        P("dp", None, "mp"),
        P("dp", "mp"),
        P("dp", "mp"),
        P("dp", "mp"),
        P(),
        P(),
    )

    def whole(*arrays):
        return local(layout, *arrays)

    return jax.shard_map(whole, mesh=mesh, in_specs=in_specs, out_specs=out_specs, check_vma=False)
```

time: 992 us -> 547 us (0.55)
  waiting for transfers between devices: 655 us -> 253 us
  matrix products: 147 us -> 20 us
  Pallas kernels: 0 us -> 110 us
  starting transfers between devices: 1.66 us -> 49.3 us
  blocking collectives: 39.7 us -> 0 us
  other arithmetic: 55.3 us -> 33 us
  loops' own time: 16.6 us -> 0 us
    reduce_scatter x8 -> x3, waiting for transfers between devices: 340 us -> 0.02 us  [the longest x1 0.02 us: local(): lax.psum_scatter(memory_term, 'mp', scatter_dimension=0, tiled=True)]
    all_gather x7 -> x3, waiting for transfers between devices: 313 us -> 61.2 us  [the longest x1 61.2 us: local(): lax.all_gather(jnp.concatenate(pieces, axis=1), 'mp', axis=0, tiled=False)]
    ppermute x0 -> x47, waiting for transfers between devices: none -> 192 us  [permute(): return lax.ppermute(value, ('dp', 'mp'), pairs)]
    dot_general x49 -> x8, matrix products: 147 us -> 20 us  [the longest x2 8.34 us: dense(): return jnp.einsum('td,df->tf', left, weight, preferred_element_type=WIDE)]
    pallas_call x0 -> x22, Pallas kernels: none -> 110 us  [the longest x3 33.8 us: call(): pl.pallas_call(kernel, in_specs=[here] * len(operands) + [there] * len(st...]
    ppermute x0 -> x47, starting transfers between devices: none -> 48.8 us  [permute(): return lax.ppermute(value, ('dp', 'mp'), pairs)]
    psum x1 -> x0, blocking collectives: 39.7 us -> none  [local(): gain_grad, bias_grad = lax.psum((gain_local, bias_local), ('dp', 'mp'))]
    reduce_sum x16 -> x0, other arithmetic: 26.9 us -> none  [the longest x6 10.3 us: layer_norm(): center = value - jnp.mean(value, axis=-1, keepdims=True)]
  transfers between devices with their start and end apart: 15 -> 53, of which waited for: 14 -> 23; matrix products, arithmetic and copies ran while one was open for 5% -> 15% of each run, Pallas kernels for 0% -> 16%
where the time goes in v1:
time: 547 us; the launch traced here: 537 us
  waiting for transfers between devices  253 us (46%)
  Pallas kernels  110 us (20%)
  local copies, waits for them, and re-layouts  55.5 us (10%)
  starting transfers between devices  49.3 us (9%)
  other arithmetic  33 us (6%)
  matrix products  20 us (4%)
  between operations  15.5 us (3%)
    ppermute x47, waiting for transfers between devices, permute(): return lax.ppermute(value, ('dp', 'mp'), pairs)  192 us
    all_gather x1, waiting for transfers between devices, local(): lax.all_gather(jnp.concatenate(pieces, axis=1), 'mp', axis=0, tiled=False)  61.2 us
    ppermute x47, starting transfers between devices, permute(): return lax.ppermute(value, ('dp', 'mp'), pairs)  48.8 us
    unnamed x148, local copies, waits for them, and re-layouts  35.2 us
    pallas_call x3, Pallas kernels, call(): pl.pallas_call(kernel, in_specs=[here] * len(operands) + [there] * len(st...  33.8 us
    pallas_call x6, Pallas kernels, weight_grads(): pl.pallas_call(lambda mp, *refs: weight_grads_kernel(*refs, other_core=ot...  30.8 us
    pallas_call x2, Pallas kernels, attend_back(): pl.pallas_call(functools.partial(attend_back_kernel, key_block=key_block,...  27.6 us
    convert_element_type x11, other arithmetic, fold(): return (value.astype(WIDE) + got.astype(WIDE)).astype(LOW)  18.7 us
  transfers between devices with their start and end apart: 53, of which 23 were waited for; matrix products, arithmetic and copies ran while one was open for 15% of the time, Pallas kernels for 16%

profile of v1, /device:TPU:0, one launch (start us, length us, event | category | flops | bytes accessed | tf_op | source)
XLA Modules:
  0.0 537.0 jit_solution(6141151322948762512)
XLA Ops:
  15.4 61.2 %all-gather.9.cloned.1.call-done = bf16[512,2816]{1,0:T(8,128)(2,1)} async-done(((bf16[128,2816]{1,0:T(8,128)(2,1)}), bf16[512,2816]{1,0:T(8,128)(2,1)}) %all-gather.9.cloned.1.call-update) | async-done | bytes 2883600 | tf_op jit(solution)/shard_map/all_gather | solution.py:692
  81.6 10.6 %collective-permute-done = bf16[4,128,512]{2,1,0:T(8,128)(2,1)S(1)} collective-permute-done((bf16[4,128,512]{2,1,0:T(8,128)(2,1)S(1)}, bf16[4,128,512]{2,1,0:T(8,128)(2,1)S(1)}, u32[]{:S(2)}, u32[]{:S(2)}) %collective-permute-start) | collective-permute-done | bytes 524320 | tf_op jit(solution)/shard_map/ppermute | solution.py:581
  96.2 24.2 %collective-permute-done.1 = bf16[2,128,2304]{2,1,0:T(8,128)(2,1)S(1)} collective-permute-done((bf16[2,128,2304]{2,1,0:T(8,128)(2,1)}, bf16[2,128,2304]{2,1,0:T(8,128)(2,1)S(1)}, u32[]{:S(2)}, u32[]{:S(2)}) %collective-permute-start.1) | collective-permute-done | bytes 1179680 | tf_op jit(solution)/shard_map/ppermute | solution.py:581
  136.9 8.9 %attend.2 = (bf16[1024,256]{1,0:T(8,128)(2,1)}, f32[2,8,1024]{2,1,0:T(8,128)}) custom-call(bf16[1024,768]{1,0:T(8,128)(2,1)} %convolution_convert_fusion.2.q_ref.k_ref.v_ref, bf16[1024,768]{1,0:T(8,128)(2,1)} %convolution_convert_fusion.2.q_ref.k_ref.v_ref, bf16[1024,768]{1,0:T(8,128)(2,1)} %convolution_convert_fusion.2.q_ref.k_ref.v_ref), custom_call_target="tpu_custom_call" | custom-call | flops 2147483648 | bytes 2097152 | tf_op jit(solution)/shard_map/attend/pallas_call | solution.py:173
  145.8 6.6 %collective-permute-done.6.refs_1_ = bf16[2,4,128,512]{3,2,1,0:T(8,128)(2,1)} collective-permute-done((bf16[2,4,128,512]{3,2,1,0:T(8,128)(2,1)S(1)}, bf16[2,4,128,512]{3,2,1,0:T(8,128)(2,1)}, u32[]{:S(2)}, u32[]{:S(2)}) %collective-permute-start.6) | collective-permute-done | bytes 1048608 | tf_op jit(solution)/shard_map/ppermute | solution.py:581
  154.7 15.0 %collective-permute-done.3.refs_1_ = bf16[256,256]{1,0:T(8,128)(2,1)S(1)} collective-permute-done((bf16[256,256]{1,0:T(8,128)(2,1)S(1)}, bf16[256,256]{1,0:T(8,128)(2,1)S(1)}, u32[]{:S(2)}, u32[]{:S(2)}) %collective-permute-start.3) | collective-permute-done | bytes 131104 | tf_op jit(solution)/shard_map/ppermute | solution.py:581
  169.7 8.5 %collective-permute-done.4.refs_2_ = bf16[256,256]{1,0:T(8,128)(2,1)S(1)} collective-permute-done((bf16[256,256]{1,0:T(8,128)(2,1)S(1)}, bf16[256,256]{1,0:T(8,128)(2,1)S(1)}, u32[]{:S(2)}, u32[]{:S(2)}) %collective-permute-start.4) | collective-permute-done | bytes 131104 | tf_op jit(solution)/shard_map/ppermute | solution.py:581
  179.8 5.2 collective-permute-done.5.refs_3_
  186.1 6.0 %enter_cross.1 = (f32[256,1024]{1,0:T(8,128)}, f32[256,128]{1,0:T(8,128)}, bf16[256,1024]{1,0:T(8,128)(2,1)}, bf16[256,256]{1,0:T(8,128)(2,1)}, bf16[256,256]{1,...) custom-call(bf16[256,1024]{1,0:T(8,128)(2,1)} %bitcast.140, f32[3,1024]{1,0:T(4,128)} %gain_ref.5, ...), custom_call_target="tpu_custom_call" | custom-call | flops 1073741824 | bytes 5267456 | tf_op jit(solution)/shard_map/enter_cross/pallas_call | solution.py:413
  211.1 9.2 %attend.3 = (bf16[1024,256]{1,0:T(8,128)(2,1)}, f32[2,8,1024]{2,1,0:T(8,128)}) custom-call(bf16[1024,256]{1,0:T(8,128)(2,1)} %constant_dynamic-update-slice_fusion.q_ref, bf16[1024,512]{1,0:T(8,128)(2,1)} %convolution_convert_fusion.3.k_ref.v_ref, bf16[1024,512]{1,0:T(8,128)(2,1)} %convolution_convert_fusion.3.k_ref.v_ref), custom_call_target="tpu_custom_call" | custom-call | flops 2147483648 | bytes 2097152 | tf_op jit(solution)/shard_map/attend/pallas_call | solution.py:173
  229.5 6.7 %collective-permute-done.13.refs_2_ = bf16[256,256]{1,0:T(8,128)(2,1)S(1)} collective-permute-done((bf16[256,256]{1,0:T(8,128)(2,1)S(1)}, bf16[256,256]{1,0:T(8,128)(2,1)S(1)}, u32[]{:S(2)}, u32[]{:S(2)}) %collective-permute-start.13) | collective-permute-done | bytes 131104 | tf_op jit(solution)/shard_map/ppermute | solution.py:581
  238.2 4.8 collective-permute-done.14.refs_3_
  245.3 21.2 %feed_forward.1 = (bf16[256,1024]{1,0:T(8,128)(2,1)}, bf16[256,1024]{1,0:T(8,128)(2,1)}, bf16[256,1024]{1,0:T(8,128)(2,1)}, f32[256,1024]{1,0:T(8,128)}, bf16[25...) custom-call(f32[256,1024]{1,0:T(8,128)} %get-tuple-element.66.first_, ...), custom_call_target="tpu_custom_call" | custom-call | flops 8589934592 | bytes 20996096 | tf_op jit(solution)/shard_map/feed_forward/pallas_call | solution.py:413
  266.5 5.2 weight_grads.8
  271.6 5.2 weight_grads.9
  284.3 5.3 weight_grads.6.refs_1_
  289.6 5.3 weight_grads.7.refs_2_
  295.7 14.1 %attend_back.2 = (bf16[1024,256]{1,0:T(8,128)(2,1)}, bf16[1024,256]{1,0:T(8,128)(2,1)}, bf16[1024,256]{1,0:T(8,128)(2,1)}) custom-call(bf16[1024,256]{1,0:T(8,128)(2,1)} %constant_dynamic-update-slice_fusion.q_ref, bf16[1024,256]{1,0:T(8,128)(2,1)} %order.15.g_ref, bf16[1024,256]{1,0:T(8,128)(2,1)} %get-tuple-element.71.refs_2_.o_ref, ...), custom_call_target="tpu_custom_call" | custom-call | flops 4294967296 | bytes 4194304 | tf_op jit(solution)/shard_map/attend_back/pallas_call | solution.py:201
  320.9 4.9 add_convert_fusion.1
  328.6 4.9 add_convert_fusion
  337.3 6.6 %leave_cross.1 = (f32[256,1024]{1,0:T(8,128)}, bf16[256,1024]{1,0:T(8,128)(2,1)}, f32[2,1024]{1,0:T(2,128)}, bf16[256,256]{1,0:T(8,128)(2,1)}, bf16[256,256]{1,0...) custom-call(f32[256,1024]{1,0:T(8,128)} %get-tuple-element.77.cross_grad_ref, f32[3,1024]{1,0:T(4,128)} %gain_ref.5, ...), custom_call_target="tpu_custom_call" | custom-call | flops 1073741824 | bytes 6959104 | tf_op jit(solution)/shard_map/leave_cross/pallas_call | solution.py:413
  344.8 5.0 weight_grads.11.refs_2_
  352.3 4.8 weight_grads.10.refs_1_
  366.5 6.5 %collective-permute-done.30 = bf16[256,256]{1,0:T(8,128)(2,1)S(1)} collective-permute-done((bf16[256,256]{1,0:T(8,128)(2,1)S(1)}, bf16[256,256]{1,0:T(8,128)(2,1)S(1)}, u32[]{:S(2)}, u32[]{:S(2)}) %collective-permute-start.30) | collective-permute-done | bytes 131104 | tf_op jit(solution)/shard_map/ppermute | solution.py:581
  373.9 13.6 %attend_back.3 = (bf16[1024,256]{1,0:T(8,128)(2,1)}, bf16[1024,256]{1,0:T(8,128)(2,1)}, bf16[1024,256]{1,0:T(8,128)(2,1)}) custom-call(bf16[1024,768]{1,0:T(8,128)(2,1)} %convolution_convert_fusion.2.q_ref.k_ref.v_ref, bf16[1024,256]{1,0:T(8,128)(2,1)} %order.17.g_ref, bf16[1024,256]{1,0:T(8,128)(2,1)} %get-tuple-element.63.refs_2_.o_ref, ...), custom_call_target="tpu_custom_call" | custom-call | flops 4294967296 | bytes 4194304 | tf_op jit(solution)/shard_map/attend_back/pallas_call | solution.py:201
  399.8 11.3 %collective-permute-done.40 = bf16[2,2,128,2304]{3,2,1,0:T(8,128)(2,1)} collective-permute-done((bf16[2,2,128,2304]{3,2,1,0:T(8,128)(2,1)}, bf16[2,2,128,2304]{3,2,1,0:T(8,128)(2,1)}, u32[]{:S(2)}, u32[]{:S(2)}) %collective-permute-start.40) | collective-permute-done | bytes 2359328 | tf_op jit(solution)/shard_map/ppermute | solution.py:581
  422.9 18.9 %collective-permute-done.36 = bf16[4,2,128,512]{3,2,0,1:T(8,128)(2,1)S(1)} collective-permute-done((bf16[4,2,128,512]{3,2,0,1:T(8,128)(2,1)S(1)}, bf16[4,2,128,512]{3,2,0,1:T(8,128)(2,1)S(1)}, u32[]{:S(2)}, u32[]{:S(2)}) %collective-permute-start.36) | collective-permute-done | bytes 1048608 | tf_op jit(solution)/shard_map/ppermute | solution.py:581
  443.3 22.9 %collective-permute-done.41 = bf16[2,128,2304]{2,1,0:T(8,128)(2,1)S(1)} collective-permute-done((bf16[2,128,2304]{2,1,0:T(8,128)(2,1)S(1)}, bf16[2,128,2304]{2,1,0:T(8,128)(2,1)S(1)}, u32[]{:S(2)}, u32[]{:S(2)}) %collective-permute-start.41) | collective-permute-done | bytes 1179680 | tf_op jit(solution)/shard_map/ppermute | solution.py:581
  481.1 14.3 %collective-permute-done.33 = bf16[1,2,128,1280]{2,3,1,0:T(8,128)(2,1)S(1)} collective-permute-done((bf16[1,2,128,1280]{2,3,1,0:T(8,128)(2,1)S(1)}, bf16[1,2,128,1280]{2,3,1,0:T(8,128)(2,1)S(1)}, u32[]{:S(2)}, u32[]{:S(2)}) %collective-permute-start.33) | collective-permute-done | bytes 655392 | tf_op jit(solution)/shard_map/ppermute | solution.py:581
  497.7 6.6 %collective-permute-done.43 = f32[6,1024]{1,0:T(8,128)S(1)} collective-permute-done((f32[6,1024]{1,0:T(8,128)S(1)}, f32[6,1024]{1,0:T(8,128)S(1)}, u32[]{:S(2)}, u32[]{:S(2)}) %collective-permute-start.43) | collective-permute-done | bytes 24608 | tf_op jit(solution)/shard_map/ppermute | solution.py:581
  508.4 5.1 collective-permute-done.45
  515.3 6.1 %collective-permute-done.46 = f32[6,1024]{1,0:T(8,128)S(1)} collective-permute-done((f32[6,1024]{1,0:T(8,128)S(1)}, f32[6,1024]{1,0:T(8,128)S(1)}, u32[]{:S(2)}, u32[]{:S(2)}) %collective-permute-start.46) | collective-permute-done | bytes 24608 | tf_op jit(solution)/shard_map/ppermute | solution.py:581
  (318 shorter events, 166.5 us)
Async XLA Ops:
  7.2 69.4 %all-gather.9.cloned.1.call-start = ((), (), s32[]{:S(2)}) async-start(), calls=%async_computation.8 | async-start | bytes 3604480 | tf_op jit(solution)/shard_map/all_gather | solution.py:692
  14.6 110.5 %all-gather.5.cloned.1.call-start = ((), (), s32[]{:S(2)}) async-start(), calls=%async_computation.3 | async-start | bytes 2621440 | tf_op jit(solution)/shard_map/all_gather | solution.py:694
  76.6 130.7 %all-gather.7.cloned.1.call-start = ((), (), s32[]{:S(2)}) async-start(), calls=%async_computation.4 | async-start | bytes 2621440 | tf_op jit(solution)/shard_map/all_gather | solution.py:703
  93.3 27.1 %collective-permute-start.1 = (bf16[2,128,2304]{2,1,0:T(8,128)(2,1)}, bf16[2,128,2304]{2,1,0:T(8,128)(2,1)S(1)}, u32[]{:S(2)}, u32[]{:S(2)}) collective-permute-start(bf16[2,128,2304]{2,1,0:T(8,128)(2,1)} %get-tuple-element.60), channel_id=1, source_target_pairs={{0,8},{1,9},{2,10},{3,11},{4,12},{5,13},{6,14},{7,15},{8,0},{9,1},... | collective-permute-start | bytes 3538952 | tf_op jit(solution)/shard_map/ppermute | solution.py:581
  94.8 28.6 %collective-permute-start.2 = (bf16[2,128,2304]{2,1,0:T(8,128)(2,1)}, bf16[2,128,2304]{2,1,0:T(8,128)(2,1)S(1)}, u32[]{:S(2)}, u32[]{:S(2)}) collective-permute-start(bf16[2,128,2304]{2,1,0:T(8,128)(2,1)} %get-tuple-element.61), channel_id=1, source_target_pairs={{0,16},{1,17},{2,18},{3,19},{4,20},{5,21},{6,22},{7,23},{8,24},{9,... | collective-permute-start | bytes 3538952 | tf_op jit(solution)/shard_map/ppermute | solution.py:581
  125.1 248.1 %reduce-scatter.4.cloned.1.call-start = ((), (), s32[]{:S(2)}) async-start(), calls=%async_computation.5 | async-start | bytes 2621440 | tf_op jit(solution)/shard_map/reduce_scatter | solution.py:769
  126.2 26.2 %collective-permute-start.6 = (bf16[2,4,128,512]{3,2,1,0:T(8,128)(2,1)S(1)}, bf16[2,4,128,512]{3,2,1,0:T(8,128)(2,1)}, u32[]{:S(2)}, u32[]{:S(2)}) collective-permute-start(bf16[2,4,128,512]{3,2,1,0:T(8,128)(2,1)S(1)} %copy-done), channel_id=1, source_target_pairs={{0,16},{1,17},{2,18},{3,19},{4,20},{5,21},{6,22},{7,23},{8,24},{9,... | collective-permute-start | bytes 3145736 | tf_op jit(solution)/shard_map/ppermute | solution.py:581
  130.3 90.0 %collective-permute-start.15 = (bf16[2,2,128,2304]{3,2,1,0:T(8,128)(2,1)}, bf16[2,2,128,2304]{3,2,1,0:T(8,128)(2,1)}, u32[]{:S(2)}, u32[]{:S(2)}) collective-permute-start(bf16[2,2,128,2304]{3,2,1,0:T(8,128)(2,1)} %get-tuple-element.72.refs_4_), channel_id=1, source_target_pairs={{0,16},{1,17},{2,18},{3,19},{4,20},{5,21},{6,22},{7,23},{8,24},{9,... | collective-permute-start | bytes 7077896 | tf_op jit(solution)/shard_map/ppermute | solution.py:581
  130.9 89.5 %collective-permute-start.16 = (bf16[2,2,128,2304]{3,2,1,0:T(8,128)(2,1)}, bf16[2,2,128,2304]{3,2,1,0:T(8,128)(2,1)}, u32[]{:S(2)}, u32[]{:S(2)}) collective-permute-start(bf16[2,2,128,2304]{3,2,1,0:T(8,128)(2,1)} %get-tuple-element.73.refs_8_), channel_id=1, source_target_pairs={{0,8},{1,9},{2,10},{3,11},{4,12},{5,13},{6,14},{7,15},{8,0},{9,1},... | collective-permute-start | bytes 7077896 | tf_op jit(solution)/shard_map/ppermute | solution.py:581
  152.5 32.6 %collective-permute-start.7 = (bf16[2,4,128,512]{3,2,1,0:T(8,128)(2,1)}, bf16[2,4,128,512]{3,2,1,0:T(8,128)(2,1)S(1)}, u32[]{:S(2)}, u32[]{:S(2)}) collective-permute-start(bf16[2,4,128,512]{3,2,1,0:T(8,128)(2,1)} %get-tuple-element.64.refs_4_), channel_id=1, source_target_pairs={{0,4},{1,5},{2,6},{3,7},{4,0},{5,1},{6,2},{7,3},{8,12},{9,13},{10,... | collective-permute-start | bytes 3145736 | tf_op jit(solution)/shard_map/ppermute | solution.py:581
  152.5 32.6 %collective-permute-start.8 = (bf16[2,4,128,512]{3,2,1,0:T(8,128)(2,1)}, bf16[2,4,128,512]{3,2,1,0:T(8,128)(2,1)}, u32[]{:S(2)}, u32[]{:S(2)}) collective-permute-start(bf16[2,4,128,512]{3,2,1,0:T(8,128)(2,1)} %get-tuple-element.65.refs_5_), channel_id=1, source_target_pairs={{0,4},{1,5},{2,6},{3,7},{4,0},{5,1},{6,2},{7,3},{8,12},{9,13},{10,... | collective-permute-start | bytes 3145736 | tf_op jit(solution)/shard_map/ppermute | solution.py:581
  192.5 51.4 %collective-permute-start.17 = (bf16[2,2,128,2304]{3,2,1,0:T(8,128)(2,1)}, bf16[2,2,128,2304]{3,2,1,0:T(8,128)(2,1)}, u32[]{:S(2)}, u32[]{:S(2)}) collective-permute-start(bf16[2,2,128,2304]{3,2,1,0:T(8,128)(2,1)} %get-tuple-element.72.refs_4_), channel_id=1, source_target_pairs={{0,4},{1,5},{2,6},{3,7},{4,0},{5,1},{6,2},{7,3},{8,12},{9,13},{10,... | collective-permute-start | bytes 7077896 | tf_op jit(solution)/shard_map/ppermute | solution.py:581
  206.0 37.9 %collective-permute-start.19 = (bf16[2,2,128,2304]{3,2,1,0:T(8,128)(2,1)}, bf16[2,2,128,2304]{3,2,1,0:T(8,128)(2,1)}, u32[]{:S(2)}, u32[]{:S(2)}) collective-permute-start(bf16[2,2,128,2304]{3,2,1,0:T(8,128)(2,1)} %get-tuple-element.73.refs_8_), channel_id=1, source_target_pairs={{0,4},{1,5},{2,6},{3,7},{4,0},{5,1},{6,2},{7,3},{8,12},{9,13},{10,... | collective-permute-start | bytes 7077896 | tf_op jit(solution)/shard_map/ppermute | solution.py:581
  220.4 23.5 %collective-permute-start.18 = (bf16[2,2,128,2304]{3,2,1,0:T(8,128)(2,1)}, bf16[2,2,128,2304]{3,2,1,0:T(8,128)(2,1)S(1)}, u32[]{:S(2)}, u32[]{:S(2)}) collective-permute-start(bf16[2,2,128,2304]{3,2,1,0:T(8,128)(2,1)} %get-tuple-element.74.refs_5_), channel_id=1, source_target_pairs={{0,4},{1,5},{2,6},{3,7},{4,0},{5,1},{6,2},{7,3},{8,12},{9,13},{10,... | collective-permute-start | bytes 7077896 | tf_op jit(solution)/shard_map/ppermute | solution.py:581
  220.9 23.0 %collective-permute-start.20 = (bf16[2,2,128,2304]{3,2,1,0:T(8,128)(2,1)}, bf16[2,2,128,2304]{3,2,1,0:T(8,128)(2,1)}, u32[]{:S(2)}, u32[]{:S(2)}) collective-permute-start(bf16[2,2,128,2304]{3,2,1,0:T(8,128)(2,1)} %get-tuple-element.75.refs_9_), channel_id=1, source_target_pairs={{0,4},{1,5},{2,6},{3,7},{4,0},{5,1},{6,2},{7,3},{8,12},{9,13},{10,... | collective-permute-start | bytes 7077896 | tf_op jit(solution)/shard_map/ppermute | solution.py:581
  271.6 49.3 %collective-permute-start.27 = (bf16[2,4,128,2304]{3,2,1,0:T(8,128)(2,1)}, bf16[2,4,128,2304]{3,2,1,0:T(8,128)(2,1)}, u32[]{:S(2)}, u32[]{:S(2)}) collective-permute-start(bf16[2,4,128,2304]{3,2,1,0:T(8,128)(2,1)} %weight_grads.8), channel_id=1, source_target_pairs={{0,4},{1,5},{2,6},{3,7},{4,0},{5,1},{6,2},{7,3},{8,12},{9,13},{10,... | collective-permute-start | bytes 14155784 | tf_op jit(solution)/shard_map/ppermute | solution.py:581
  276.9 51.8 %collective-permute-start.28 = (bf16[2,4,128,2304]{3,2,1,0:T(8,128)(2,1)}, bf16[2,4,128,2304]{3,2,1,0:T(8,128)(2,1)}, u32[]{:S(2)}, u32[]{:S(2)}) collective-permute-start(bf16[2,4,128,2304]{3,2,1,0:T(8,128)(2,1)} %weight_grads.9), channel_id=1, source_target_pairs={{0,4},{1,5},{2,6},{3,7},{4,0},{5,1},{6,2},{7,3},{8,12},{9,13},{10,... | collective-permute-start | bytes 14155784 | tf_op jit(solution)/shard_map/ppermute | solution.py:581
  311.7 24.8 %collective-permute-start.24 = (bf16[256,256]{1,0:T(8,128)(2,1)S(1)}, bf16[256,256]{1,0:T(8,128)(2,1)S(1)}, u32[]{:S(2)}, u32[]{:S(2)}) collective-permute-start(bf16[256,256]{1,0:T(8,128)(2,1)S(1)} %get-tuple-element.155), channel_id=1, source_target_pairs={{0,1},{1,0},{2,3},{3,2},{4,5},{5,4},{6,7},{7,6},{8,9},{9,8},{10,11... | collective-permute-start | bytes 393224 | tf_op jit(solution)/shard_map/ppermute | solution.py:581
  311.8 24.8 %collective-permute-start.25 = (bf16[256,256]{1,0:T(8,128)(2,1)S(1)}, bf16[256,256]{1,0:T(8,128)(2,1)S(1)}, u32[]{:S(2)}, u32[]{:S(2)}) collective-permute-start(bf16[256,256]{1,0:T(8,128)(2,1)S(1)} %get-tuple-element.154), channel_id=1, source_target_pairs={{0,2},{1,3},{2,0},{3,1},{4,6},{5,7},{6,4},{7,5},{8,10},{9,11},{10,... | collective-permute-start | bytes 393224 | tf_op jit(solution)/shard_map/ppermute | solution.py:581
  314.3 22.3 %collective-permute-start.26 = (bf16[256,256]{1,0:T(8,128)(2,1)S(1)}, bf16[256,256]{1,0:T(8,128)(2,1)S(1)}, u32[]{:S(2)}, u32[]{:S(2)}) collective-permute-start(bf16[256,256]{1,0:T(8,128)(2,1)S(1)} %get-tuple-element.153), channel_id=1, source_target_pairs={{0,3},{1,2},{2,1},{3,0},{4,7},{5,6},{6,5},{7,4},{8,11},{9,10},{10,... | collective-permute-start | bytes 393224 | tf_op jit(solution)/shard_map/ppermute | solution.py:581
  320.9 203.8 %reduce-scatter.6.cloned.1.call-start = ((), (), s32[]{:S(2)}) async-start(), calls=%async_computation.6 | async-start | bytes 2621440 | tf_op jit(solution)/shard_map/reduce_scatter | solution.py:792
  349.9 44.6 %collective-permute-start.35 = (bf16[4,4,128,512]{3,2,1,0:T(8,128)(2,1)}, bf16[4,4,128,512]{3,2,1,0:T(8,128)(2,1)}, u32[]{:S(2)}, u32[]{:S(2)}) collective-permute-start(bf16[4,4,128,512]{3,2,1,0:T(8,128)(2,1)} %weight_grads.11.refs_2_), channel_id=1, source_target_pairs={{0,4},{1,5},{2,6},{3,7},{4,0},{5,1},{6,2},{7,3},{8,12},{9,13},{10,... | collective-permute-start | bytes 6291464 | tf_op jit(solution)/shard_map/ppermute | solution.py:581
  357.2 53.9 %collective-permute-start.40 = (bf16[2,2,128,2304]{3,2,1,0:T(8,128)(2,1)}, bf16[2,2,128,2304]{3,2,1,0:T(8,128)(2,1)}, u32[]{:S(2)}, u32[]{:S(2)}) collective-permute-start(bf16[2,2,128,2304]{3,2,1,0:T(8,128)(2,1)} %slice_bitcast_fusion.1.refs_5_), channel_id=1, source_target_pairs={{0,16},{1,17},{2,18},{3,19},{4,20},{5,21},{6,22},{7,23},{8,24},{9,... | collective-permute-start | bytes 7077896 | tf_op jit(solution)/shard_map/ppermute | solution.py:581
  365.1 54.4 %collective-permute-start.38 = (bf16[2,2,128,2304]{3,2,0,1:T(8,128)(2,1)}, bf16[2,2,128,2304]{3,2,0,1:T(8,128)(2,1)}, u32[]{:S(2)}, u32[]{:S(2)}) collective-permute-start(bf16[2,2,128,2304]{3,2,0,1:T(8,128)(2,1)} %bitcast.126), channel_id=1, source_target_pairs={{0,8},{1,9},{2,10},{3,11},{4,12},{5,13},{6,14},{7,15},{8,0},{9,1},... | collective-permute-start | bytes 7077896 | tf_op jit(solution)/shard_map/ppermute | solution.py:581
  394.1 132.5 %reduce-scatter.8.cloned.1.call-start = ((), (), s32[]{:S(2)}) async-start(), calls=%async_computation.7 | async-start | bytes 3604480 | tf_op jit(solution)/shard_map/reduce_scatter | solution.py:808
  398.3 43.6 %collective-permute-start.36 = (bf16[4,2,128,512]{3,2,0,1:T(8,128)(2,1)S(1)}, bf16[4,2,128,512]{3,2,0,1:T(8,128)(2,1)S(1)}, u32[]{:S(2)}, u32[]{:S(2)}) collective-permute-start(bf16[4,2,128,512]{3,2,0,1:T(8,128)(2,1)S(1)} %bitcast.154), channel_id=1, source_target_pairs={{0,8},{1,9},{2,10},{3,11},{4,12},{5,13},{6,14},{7,15},{8,0},{9,1},... | collective-permute-start | bytes 3145736 | tf_op jit(solution)/shard_map/ppermute | solution.py:581
  414.1 52.1 %collective-permute-start.41 = (bf16[2,128,2304]{2,1,0:T(8,128)(2,1)S(1)}, bf16[2,128,2304]{2,1,0:T(8,128)(2,1)S(1)}, u32[]{:S(2)}, u32[]{:S(2)}) collective-permute-start(bf16[2,128,2304]{2,1,0:T(8,128)(2,1)S(1)} %slice_bitcast_fusion.2), channel_id=1, source_target_pairs={{0,8},{1,9},{2,10},{3,11},{4,12},{5,13},{6,14},{7,15},{8,0},{9,1},... | collective-permute-start | bytes 3538952 | tf_op jit(solution)/shard_map/ppermute | solution.py:581
  421.8 44.7 %collective-permute-start.39 = (bf16[2,128,2304]{2,1,0:T(8,128)(2,1)S(1)}, bf16[2,128,2304]{2,1,0:T(8,128)(2,1)S(1)}, u32[]{:S(2)}, u32[]{:S(2)}) collective-permute-start(bf16[2,128,2304]{2,1,0:T(8,128)(2,1)S(1)} %slice_bitcast_fusion.4), channel_id=1, source_target_pairs={{0,16},{1,17},{2,18},{3,19},{4,20},{5,21},{6,22},{7,23},{8,24},{9,... | collective-permute-start | bytes 3538952 | tf_op jit(solution)/shard_map/ppermute | solution.py:581
  442.2 24.6 %collective-permute-start.37 = (bf16[4,128,512]{2,1,0:T(8,128)(2,1)S(1)}, bf16[4,128,512]{2,1,0:T(8,128)(2,1)S(1)}, u32[]{:S(2)}, u32[]{:S(2)}) collective-permute-start(bf16[4,128,512]{2,1,0:T(8,128)(2,1)S(1)} %slice_bitcast_fusion.6), channel_id=1, source_target_pairs={{0,16},{1,17},{2,18},{3,19},{4,20},{5,21},{6,22},{7,23},{8,24},{9,... | collective-permute-start | bytes 1572872 | tf_op jit(solution)/shard_map/ppermute | solution.py:581
  479.4 15.9 %collective-permute-start.33 = (bf16[1,2,128,1280]{2,3,1,0:T(8,128)(2,1)S(1)}, bf16[1,2,128,1280]{2,3,1,0:T(8,128)(2,1)S(1)}, u32[]{:S(2)}, u32[]{:S(2)}) collective-permute-start(bf16[1,2,128,1280]{2,3,1,0:T(8,128)(2,1)S(1)} %bitcast.156), channel_id=1, source_target_pairs={{0,16},{1,17},{2,18},{3,19},{4,20},{5,21},{6,22},{7,23},{8,24},{9,... | collective-permute-start | bytes 1966088 | tf_op jit(solution)/shard_map/ppermute | solution.py:581
  480.7 16.5 %collective-permute-start.42 = (f32[6,1024]{1,0:T(8,128)S(1)}, f32[6,1024]{1,0:T(8,128)S(1)}, u32[]{:S(2)}, u32[]{:S(2)}) collective-permute-start(f32[6,1024]{1,0:T(8,128)S(1)} %pad_maximum_fusion.7), channel_id=1, source_target_pairs={{0,4},{1,5},{2,6},{3,7},{4,0},{5,1},{6,2},{7,3},{8,12},{9,13},{10,... | collective-permute-start | bytes 73736 | tf_op jit(solution)/shard_map/ppermute | solution.py:581
  495.6 27.2 %collective-permute-start.34 = (bf16[1,128,1280]{1,2,0:T(8,128)(2,1)S(1)}, bf16[1,128,1280]{1,2,0:T(8,128)(2,1)S(1)}, u32[]{:S(2)}, u32[]{:S(2)}) collective-permute-start(bf16[1,128,1280]{1,2,0:T(8,128)(2,1)S(1)} %slice_bitcast_fusion.8), channel_id=1, source_target_pairs={{0,8},{1,9},{2,10},{3,11},{4,12},{5,13},{6,14},{7,15},{8,0},{9,1},... | collective-permute-start | bytes 983048 | tf_op jit(solution)/shard_map/ppermute | solution.py:581
  (85 other events, 459.3 us)
Sparse Core Ops, SparseCore 0:
  14.7 61.8 all-gather.8
  78.7 44.6 all-gather.4
  125.5 46.0 all-gather.6
  321.0 48.2 reduce-scatter.3
  394.3 44.9 reduce-scatter.5
  468.9 57.1 reduce-scatter.7

commit v2 on v1

--- a/solution.py
+++ b/solution.py
@@ -260,6 +260,17 @@
     return copies
 
 
+def attention_copies(own, parts, weights, sems, width):
+    count = weights.shape[0]
+    copies = [
+        pltpu.make_async_copy(own[0], weights.at[0, :, :width], sems.at[CELLS]),
+        pltpu.make_async_copy(own[1], weights.at[0, :, width:], sems.at[CELLS + 1]),
+    ]
+    return copies + cell_copies(
+        parts, 2, weights, sems, lambda part, to, at: (part, to.at[pl.ds(1, count - 1), at, :])
+    )
+
+
 def start_all(copies):
     for copy in copies:
         copy.start()
@@ -274,100 +285,95 @@
     tokens_ref, gain_ref, bias_ref, *refs, width, count
 ):
     attended, refs = refs[:count], refs[count:]
-    parts, refs = refs[:4], refs[4:]
+    own, parts, refs = refs[:2], refs[2:6], refs[6:]
     n_ref, scale_ref, low_ref = refs[:3]
     queries, (weights, sems) = refs[3 : 3 + count], refs[3 + count :]
-    copies = cell_copies(parts, 2, weights, sems, lambda part, to, at: (part, to.at[:, at, :]))
-    shards = [jnp.bitwise_xor(lax.axis_index("mp"), k) for k in range(count)]
+    copies = attention_copies(own, parts, weights, sems, width)
     start_all(copies)
     value = alpha_scale * tokens_ref[...].astype(WIDE)
     wait_all(copies)
     for k in range(count):
-        value = value + mm(attended[k][...], weights[shards[k], :, :width], NT)
+        value = value + mm(attended[k][...], weights[k, :, :width], NT)
     n, scale = normalized(value)
     n_ref[...] = n
     scale_ref[...] = jnp.broadcast_to(scale, scale_ref.shape)
     low = (n * gain_ref[0:1, :] + bias_ref[0:1, :]).astype(LOW)
     low_ref[...] = low
     for k in range(count):
-        queries[k][...] = mm(low, weights[shards[k], :, width:], NN).astype(LOW)
+        queries[k][...] = mm(low, weights[k, :, width:], NN).astype(LOW)
 
 
 def leave_cross_kernel(
     cross_grad_ref, gain_ref, n_ref, scale_ref, *refs, width, count
 ):
     queries, refs = refs[:count], refs[count:]
-    parts, refs = refs[:4], refs[4:]
+    own, parts, refs = refs[:2], refs[2:6], refs[6:]
     self_grad_ref, low_ref, terms_ref = refs[:3]
     grads, (weights, sems) = refs[3 : 3 + count], refs[3 + count :]
-    copies = cell_copies(parts, 2, weights, sems, lambda part, to, at: (part, to.at[:, at, :]))
-    shards = [jnp.bitwise_xor(lax.axis_index("mp"), k) for k in range(count)]
+    copies = attention_copies(own, parts, weights, sems, width)
     start_all(copies)
     grad = alpha_scale * cross_grad_ref[...]
     wait_all(copies)
     for k in range(count):
-        grad = grad + mm(queries[k][...], weights[shards[k], :, width:], NT)
+        grad = grad + mm(queries[k][...], weights[k, :, width:], NT)
     self_grad, terms_ref[...] = norm_back(grad, gain_ref[0:1, :], n_ref[...], scale_ref[:, :1])
     self_grad_ref[...] = self_grad
     low = self_grad.astype(LOW)
     low_ref[...] = low
     for k in range(count):
-        grads[k][...] = mm(low, weights[shards[k], :, :width], NN).astype(LOW)
+        grads[k][...] = mm(low, weights[k, :, :width], NN).astype(LOW)
 
 
 def feed_forward_kernel(
     first_n_ref, cotangent_ref, gain_ref, bias_ref, *refs, width, count
 ):
     attended, refs = refs[:count], refs[count:]
-    parts, refs = (refs[:4], refs[4:8]), refs[8:]
+    own, in_parts, out_parts, refs = refs[:3], refs[3:7], refs[7:11], refs[11:]
     mixed_ref, second_low_ref, third_low_ref, cross_grad_ref, cross_low_ref, terms_ref = refs[:6]
     act_ref, hidden_grad_ref = refs[6:8]
     grads, refs = refs[8 : 8 + count], refs[8 + count :]
     w_in, w_out, w_cross, slope_ref, sum_ref, in_sems, out_sems, cross_sems = refs
     hidden = w_in.shape[2]
     chunk = min(512, hidden)
-    half = count // 2
-
-    shards = [jnp.bitwise_xor(lax.axis_index("mp"), k) for k in range(count)]
-
-    cross_copies = []
-    for h in range(2):
-        cross_copies += cell_copies(
-            parts[h],
-            BITS[h],
-            w_cross,
-            cross_sems.at[h],
-            lambda part, to, at: (part.at[:, :, 2 * hidden :], to.at[pl.ds(h * half, half), at, :]),
-        )
+
+    cross_copies = [pltpu.make_async_copy(own[2], w_cross.at[0], cross_sems.at[CELLS])]
+    cross_copies += cell_copies(
+        out_parts,
+        4,
+        w_cross,
+        cross_sems,
+        lambda part, to, at: (part.at[:, :, hidden:], to.at[pl.ds(1, count - 1), at, :]),
+    )
     start_all(cross_copies)
-    in_copies, out_copies = [], []
-    for s in range(count):
-        h = s // half
+    in_copies = [[pltpu.make_async_copy(own[0], w_in.at[0], in_sems.at[0, 0])]]
+    out_copies = [[pltpu.make_async_copy(own[1], w_out.at[0], out_sems.at[0, 0])]]
+    for k in range(1, count):
         in_copies.append(
             cell_copies(
-                parts[h],
-                BITS[h],
+                in_parts,
+                2,
                 w_in,
-                in_sems.at[s],
-                lambda part, to, at: (part.at[s % half, :, :hidden], to.at[s, at, :]),
+                in_sems.at[k],
+                lambda part, to, at: (part.at[k - 1], to.at[k, at, :]),
             )
         )
         out_copies.append(
             cell_copies(
-                parts[h],
-                BITS[h],
+                out_parts,
+                4,
                 w_out,
-                out_sems.at[s],
-                lambda part, to, at: (part.at[s % half, :, hidden : 2 * hidden], to.at[s, at, :]),
+                out_sems.at[k],
+                lambda part, to, at: (part.at[k - 1, :, :hidden], to.at[k, at, :]),
             )
         )
-        start_all(in_copies[s])
-        start_all(out_copies[s])
+    for copies in zip(in_copies, out_copies):
+        start_all(copies[0])
+        start_all(copies[1])
 
     second = alpha_scale * (first_n_ref[...] * gain_ref[0:1, :] + bias_ref[0:1, :])
     wait_all(cross_copies)
     for k in range(count):
-        second = second + mm(attended[k][...], w_cross[shards[k]], NT)
+        second = second + mm(attended[k][...], w_cross[k], NT)
     second_n, second_scale = normalized(second)
     second = second_n * gain_ref[1:2, :] + bias_ref[1:2, :]
     second_low = second.astype(LOW)
@@ -403,7 +409,7 @@
     cross_low = cross_grad.astype(LOW)
     cross_low_ref[...] = cross_low
     for k in range(count):
-        grads[k][...] = mm(cross_low, w_cross[shards[k]], NN).astype(LOW)
+        grads[k][...] = mm(cross_low, w_cross[k], NN).astype(LOW)
 
 
 def call(kernel, operands, streamed, results, scratch, flops, name):
@@ -422,50 +428,75 @@
     )(*arrays)
 
 
-def enter_cross(tokens, gain, bias, attended, parts):
+def project_kernel(*refs, count):
+    blocks, (weight_ref, tokens_ref, out_ref) = refs[:count], refs[count:]
+    rows = tokens_ref.shape[0] // count
+    for k in range(count):
+        at = jnp.bitwise_xor(lax.axis_index("mp"), k) * rows
+        at = pl.ds(pl.multiple_of(at, rows), rows)
+        block = blocks[k][:rows, :]
+        tokens_ref[at, :] = block
+        out_ref[at, :] = mm(block, weight_ref[...], NN).astype(LOW)
+
+
+def project(blocks, rows, weight):
+    count, model = len(blocks), blocks[0].shape[1]
+    return call(
+        functools.partial(project_kernel, count=count),
+        [*blocks, weight],
+        [],
+        [((count * rows, model), LOW), ((count * rows, weight.shape[1]), LOW)],
+        [],
+        2 * count * rows * model * weight.shape[1],
+        "project",
+    )
+
+
+def enter_cross(tokens, gain, bias, attended, own, parts):
     rows, model = tokens.shape
     count, width = len(attended), attended[0].shape[1]
     return call(
         functools.partial(enter_cross_kernel, width=width, count=count),
         [tokens, gain, bias, *attended],
-        parts,
+        [*own, *parts],
         [((rows, model), WIDE), ((rows, 128), WIDE), ((rows, model), LOW)]
         + [((rows, width), LOW)] * count,
         [
             pltpu.VMEM((count, model, 2 * width), LOW),
-            pltpu.SemaphoreType.DMA((CELLS,)),
+            pltpu.SemaphoreType.DMA((CELLS + 2,)),
         ],
         4 * rows * model * width * count,
         "enter_cross",
     )
 
 
-def leave_cross(cross_grad, gain, n, scale, queries, parts):
+def leave_cross(cross_grad, gain, n, scale, queries, own, parts):
     rows, model = n.shape
     count, width = len(queries), queries[0].shape[1]
     return call(
         functools.partial(leave_cross_kernel, width=width, count=count),
         [cross_grad, gain, n, scale, *queries],
-        parts,
+        [*own, *parts],
         [((rows, model), WIDE), ((rows, model), LOW), ((2, model), WIDE)]
         + [((rows, width), LOW)] * count,
         [
             pltpu.VMEM((count, model, 2 * width), LOW),
-            pltpu.SemaphoreType.DMA((CELLS,)),
+            pltpu.SemaphoreType.DMA((CELLS + 2,)),
         ],
         4 * rows * model * width * count,
         "leave_cross",
     )
 
 
-def feed_forward(first_n, cotangent, gain, bias, attended, hidden, parts):
+def feed_forward(first_n, cotangent, gain, bias, attended, own, in_parts, out_parts):
     rows, model = first_n.shape
     count, width = len(attended), attended[0].shape[1]
+    hidden = own[0].shape[1]
     sems = pltpu.SemaphoreType.DMA((count, CELLS))
     return call(
         functools.partial(feed_forward_kernel, width=width, count=count),
         [first_n, cotangent, gain, bias, *attended],
-        [*parts[0], *parts[1]],
+        [*own, *in_parts, *out_parts],
         [
             ((rows, model), LOW),
             ((rows, model), LOW),
@@ -485,16 +516,21 @@
             pltpu.VMEM((rows, model), WIDE),
             sems,
             sems,
-            pltpu.SemaphoreType.DMA((2, CELLS)),
+            pltpu.SemaphoreType.DMA((CELLS + 1,)),
         ],
         8 * rows * model * hidden * count,
         "feed_forward",
     )
 
 
-def weight_grads_kernel(*refs, other_core):
-    count = (len(refs) - 2) // 2
-    lefts, rights, out_ref, turned = refs[:count], refs[count:-2], refs[-2], refs[-1]
+def chip_cells(bit):
+    keep = [c for c in range(CELLS // 2) if not (2 * c) & bit]
+    return keep, [c for c in range(CELLS // 2) if (2 * c) & bit]
+
+
+def weight_grads_kernel(*refs, count, other_core, bit):
+    lefts, rights, refs = refs[:count], refs[count : 2 * count], refs[2 * count :]
+    turned = refs[-1]
     block = turned.shape[1] // (CELLS // 2)
 
     @pl.when(pl.program_id(0) == 0)
@@ -508,38 +544,48 @@
 
     at = 0
     for i, right in enumerate(rights):
-        width = right.shape[2]
-        value = mm(turned[i], right[0], NN).astype(LOW)
-        out_ref[0, :, :, at : at + width] = value.reshape(CELLS // 2, block, width)
-        at += width
-
-
-def weight_grads(lefts, rights, relative, shards, other_core):
+        cut = slice(at, at + right.shape[2])
+        at += right.shape[2]
+        value = mm(turned[i], right[0], NN).reshape(CELLS // 2, block, right.shape[2])
+        if bit is None:
+            refs[0][:, 0, :, cut] = value.astype(LOW)
+            continue
+        got, *outs = refs[:3]
+        for out, cells in zip(outs, chip_cells(bit)):
+            for e, c in enumerate(cells):
+                out[e, 0, :, cut] = (value[c] + got[c, 0, :, cut].astype(WIDE)).astype(LOW)
+
+
+def weight_grads(lefts, rights, shards, other_core, got=None, bit=None):
     rows, model = lefts[0].shape
-    count, block = len(shards), model // CELLS
+    count, block, cells = len(shards), model // CELLS, CELLS // 2
     width = sum(right.shape[2] for right in rights)
 
-    def right_at(flag):
-        def at(s, mp):
-            shard = s + shards[0]
-            return (jnp.bitwise_xor(shard, mp[0]) if flag else shard), 0, 0
-
-        return at
-
+    def right_at(s, mp):
+        return jnp.bitwise_xor(s + shards[0], mp[0]), 0, 0
+
+    def whole(cells):
+        return pl.BlockSpec((cells, 1, block, width), lambda s, mp: (0, s, 0, 0))
+
+    def result(cells):
+        return jax.ShapeDtypeStruct((cells, count, block, width), LOW)
+
+    halves = got is not None
+    kernel = functools.partial(
+        weight_grads_kernel, count=len(lefts), other_core=other_core, bit=bit
+    )
     return pl.pallas_call(
-        lambda mp, *refs: weight_grads_kernel(*refs, other_core=other_core),
+        lambda mp, *refs: kernel(*refs),
         grid_spec=pltpu.PrefetchScalarGridSpec(
             num_scalar_prefetch=1,
             grid=(count,),
             in_specs=[pl.BlockSpec((rows, model), lambda s, mp: (0, 0))] * len(lefts)
-            + [
-                pl.BlockSpec((1, rows, right.shape[2]), right_at(flag))
-                for right, flag in zip(rights, relative)
-            ],
-            out_specs=pl.BlockSpec((1, CELLS // 2, block, width), lambda s, mp: (s, 0, 0, 0)),
+            + [pl.BlockSpec((1, rows, right.shape[2]), right_at) for right in rights]
+            + [whole(cells)] * halves,
+            out_specs=[whole(cells // 2)] * 2 if halves else whole(cells),
             scratch_shapes=[pltpu.VMEM((len(lefts), model // 2, rows), LOW)],
         ),
-        out_shape=jax.ShapeDtypeStruct((count, CELLS // 2, block, width), LOW),
+        out_shape=[result(cells // 2)] * 2 if halves else result(cells),
         compiler_params=pltpu.CompilerParams(vmem_limit_bytes=VMEM_LIMIT),
         cost_estimate=pl.CostEstimate(
             flops=rows * model * width * count,
@@ -547,7 +593,12 @@
             transcendentals=0,
         ),
         name="weight_grads",
-    )(lax.axis_index("mp").astype(jnp.int32).reshape(1), *lefts, *rights)
+    )(
+        lax.axis_index("mp").astype(jnp.int32).reshape(1),
+        *lefts,
+        *rights,
+        *([got] if halves else []),
+    )
 
 
 def pass_kernel(*refs):
@@ -627,16 +678,6 @@
     def fold(self, value, got):
         return (value.astype(WIDE) + got.astype(WIDE)).astype(LOW)
 
-    def chip_halves(self, value, bit):
-        count, width = value.shape[0], value.shape[-1]
-        value = value.reshape(count, 2, 2, -1, width)
-        if bit == 2:
-            return value[:, :, 0], value[:, :, 1]
-        return value[:, 0], value[:, 1]
-
-    def last_halves(self, value):
-        return value[:, 0], value[:, 1]
-
     def to_rows(self, mine):
         groups = self.dp // CELLS
         if groups == 1:
@@ -650,14 +691,10 @@
         )
         return self.permute(mine, lambda d, m: ((d % CELLS) * groups + d // CELLS, m))
 
-    def sum_all(self, value):
+    def sum_dp(self, value):
         step = 1
         while step < self.dp:
             value = value + self.flip(value, step)
-            step *= 2
-        step = 1
-        while step < self.mp:
-            value = value + self.flip_mp(value, step)
             step *= 2
         return value
 
@@ -688,40 +725,40 @@
     kv_flat = cross_kv.reshape(model_width, 2 * w)
     n_hidden = ffn_in.shape[1]
     half = n // 2
+    order = [jnp.bitwise_xor(lax.axis_index("mp"), k) for k in range(n)]
+
+    full_tokens = lax.all_gather(tokens, "mp", axis=0, tiled=True)
     pieces = [layout.piece(v) for v in (self_out, cross_q, ffn_in, ffn_out, cross_out)]
-    weights = lax.all_gather(jnp.concatenate(pieces, axis=1), "mp", axis=0, tiled=False)
-    (tokens_there,) = after([tokens], weights)
-    full_tokens = lax.all_gather(tokens_there, "mp", axis=0, tiled=True)
-    attn_here = layout.near(weights[:, :, : 2 * w], 2)
-    ffn_own = after(
-        [weights[h * half : (h + 1) * half, :, 2 * w :] for h in range(2)], attn_here
-    )
+    attn_here = jnp.stack(layout.swap_mp([jnp.concatenate(pieces[:2], axis=1)] * n)[1:])
+    attn_here = layout.near(attn_here, 2)
     attn_there = layout.flip(attn_here, 4)
-    ffn_here = [layout.near(part, bit) for part, bit in zip(ffn_own, BITS)]
-    full_tokens, *ffn_here = after([full_tokens, *ffn_here], weights)
-    (memory_there,) = after([memory], full_tokens)
-    full_memory = lax.all_gather(memory_there, "mp", axis=0, tiled=True)
-
+    attn_parts = [attn_here, attn_there, layout.flip(attn_here, 1), layout.flip(attn_there, 1)]
+    full_tokens, *attn_parts = after([full_tokens, *attn_parts])
+    (ffn_piece,) = after([jnp.concatenate(pieces[2:], axis=1)], full_tokens)
+    ffn_all = lax.all_gather(ffn_piece, "mp", axis=0, tiled=False)
     projected = dense(full_tokens, qkv_flat).astype(LOW)
     pairs = w // (2 * HD)
     self_operands = (projected, 0), (projected, pairs), (projected, 2 * pairs)
     home_attended, self_logs = attend(w, *self_operands, True, *SELF_BLOCKS)
     attended_blocks = layout.swap_mp(layout.rows_for(home_attended))
-    attn_here, attn_there = after([attn_here, attn_there], home_attended)
-    ffn_there = [layout.flip(part, 6 - bit) for part, bit in zip(ffn_here, BITS)]
-    attn_parts = [attn_here, attn_there, layout.flip(attn_here, 1), layout.flip(attn_there, 1)]
     first_n, first_scale, first_low, *query_blocks = enter_cross(
-        tokens, ln_gain, ln_bias, attended_blocks, attn_parts
+        tokens, ln_gain, ln_bias, attended_blocks, (self_out, cross_q), attn_parts
     )
     query_blocks = layout.swap_mp(query_blocks)
-    cross_queries = jnp.concatenate(query_blocks)
-    ffn_here_other = [layout.flip(part, 1) for part in ffn_here]
+    memory_there, ffn_all = after([memory, ffn_all], *query_blocks[1:])
+    full_memory = lax.all_gather(memory_there, "mp", axis=0, tiled=True)
+    ffn_here = jnp.concatenate([lax.dynamic_slice_in_dim(ffn_all, k, 1, 0) for k in order[1:]])
+    in_here = layout.near(ffn_here[:, :, :n_hidden], 2)
+    out_here = layout.near(ffn_here[:, :, n_hidden:], 4)
+    in_there, out_there = layout.flip(in_here, 4), layout.flip(out_here, 2)
+    here_others = [layout.flip(in_here, 1), layout.flip(out_here, 1)]
+    (cross_queries,) = after([jnp.concatenate(query_blocks)], *here_others)
     cross_pair = dense(full_memory, kv_flat).astype(LOW)
     cross_operands = (cross_queries, 0), (cross_pair, 0), (cross_pair, pairs)
     home_cross, cross_logs = attend(w, *cross_operands, False, *CROSS_BLOCKS)
-    ffn_there = after(ffn_there, home_cross)
-    ffn_there_other = [layout.flip(part, 1) for part in ffn_there]
-    ffn_parts = list(zip(ffn_here, ffn_there, ffn_here_other, ffn_there_other))
+    in_there, out_there = after([in_there, out_there], home_cross)
+    in_parts = [in_here, in_there, here_others[0], layout.flip(in_there, 1)]
+    out_parts = [out_here, out_there, here_others[1], layout.flip(out_there, 1)]
     cross_blocks = layout.swap_mp(list(home_cross.reshape(n, rows, w)))
     (
         mixed,
@@ -734,32 +771,36 @@
         hidden_grad,
         *cross_grad_blocks,
     ) = feed_forward(
-        first_n, cotangent, ln_gain, ln_bias, cross_blocks, n_hidden, ffn_parts
+        first_n,
+        cotangent,
+        ln_gain,
+        ln_bias,
+        cross_blocks,
+        (ffn_in, ffn_out, cross_out),
+        in_parts,
+        out_parts,
     )
     cross_grad_blocks = layout.swap_mp(cross_grad_blocks)
     cross_attended = jnp.stack(cross_blocks)
 
-    def fold_chip(pair, bit):
-        return layout.chip_halves(layout.fold(*pair), bit)
-
     def send(pair, bit):
         return pair[0], layout.flip(pair[1], bit)
 
-    def fold_last(pair):
-        return layout.last_halves(layout.fold(*pair))
-
+    def fold_halves(pair):
+        value = layout.fold(*pair)
+        middle = value.shape[0] // 2
+        return value[:middle], value[middle:]
+
+    lefts = [second_low, third_low, cross_grad_low]
     ffn_grads = functools.partial(
         weight_grads,
-        [second_low, third_low, cross_grad_low],
+        lefts,
         [hidden_grad, activation, cross_attended],
-        [False, False, True],
     )
     cuts = (range(0, half), range(half, n))
-    ffn_sums = [send((None, ffn_grads(cut, 1)), 1)[1] for cut in cuts]
-    ffn_sums = [(ffn_grads(cut, 0), got) for cut, got in zip(cuts, ffn_sums)]
-    (cross_attended_grad,) = after(
-        [jnp.concatenate(cross_grad_blocks)], *(here for here, _ in ffn_sums)
-    )
+    ffn_there = [ffn_grads(cut, 1) for cut in cuts]
+    ffn_got = [layout.flip(part, 1) for part in ffn_there]
+    (cross_attended_grad,) = after([jnp.concatenate(cross_grad_blocks)], *ffn_there)
     cross_queries_grad, cross_keys_grad, cross_values_grad = attend_back(
         w, *cross_operands, cross_attended_grad, home_cross, cross_logs, False, *CROSS_BACK_BLOCKS
     )
@@ -767,59 +808,70 @@
     cross_pair_grad = jnp.concatenate([cross_keys_grad, cross_values_grad], axis=-1)
     memory_term = back_dense(cross_pair_grad, kv_flat).astype(LOW)
     memory_grad = lax.psum_scatter(memory_term, "mp", scatter_dimension=0, tiled=True)
-    ffn_sums = [fold_chip(pair, bit) for pair, bit in zip(ffn_sums, BITS)]
-    first_terms[1:] = after(first_terms[1:], memory_term, *(there for _, there in ffn_sums))
+    ffn_sums = [ffn_grads(cut, 0, got, bit) for cut, got, bit in zip(cuts, ffn_got, BITS)]
+    first_terms[1:] = after(first_terms[1:], memory_term, ffn_sums[0][1], ffn_sums[1][1])
     ffn_sums = [send(pair, bit) for pair, bit in zip(ffn_sums, BITS)]
     self_grad, self_grad_low, first_norm_terms, *attended_grad_blocks = leave_cross(
-        cross_grad, ln_gain, first_n, first_scale, first_terms, attn_parts
-    )
-    attended_grad = layout.in_order(layout.swap_mp(attended_grad_blocks))
+        cross_grad, ln_gain, first_n, first_scale, first_terms, (self_out, cross_q), attn_parts
+    )
+    norm_terms = jnp.concatenate([first_norm_terms, later_terms])
+    upper = norm_terms.astype(LOW)
+    lower = (norm_terms - upper.astype(WIDE)).astype(LOW)
+    norm_rows = jnp.concatenate([upper.reshape(-1, w), lower.reshape(-1, w)])
+    blocks = layout.swap_mp(
+        [jnp.concatenate([block, norm_rows]) for block in attended_grad_blocks]
+    )
+    attended_grad = layout.in_order([block[:rows] for block in blocks])
+    norm_terms = sum(block[rows:].astype(WIDE) for block in blocks)
+    norm_terms = norm_terms.reshape(2, -1, model_width).sum(axis=0)
+    (attended_grad,) = after([attended_grad], memory_grad)
+    queries_grad, keys_grad, values_grad = attend_back(
+        w, *self_operands, attended_grad, home_attended, self_logs, True, *SELF_BACK_BLOCKS
+    )
+    projected_grad = jnp.concatenate([queries_grad, keys_grad, values_grad], axis=-1)
+    token_term = back_dense(projected_grad, qkv_flat).astype(LOW)
+    (token_term,) = after([token_term], *(got for _, got in ffn_sums))
+    token_part = lax.psum_scatter(token_term, "mp", scatter_dimension=0, tiled=True)
+    token_grad = (alpha_scale * self_grad + token_part.astype(WIDE)).astype(LOW)
+    (self_grad_low,) = after([self_grad_low], token_term)
     attn_grads = functools.partial(
         weight_grads,
         [self_grad_low, first_low],
         [jnp.stack(attended_blocks), jnp.stack(first_terms)],
-        [True, True],
         range(n),
     )
-    attn_here, attn_there = attn_grads(0), attn_grads(1)
-    (attended_grad,) = after([attended_grad], attn_here, attn_there, memory_grad)
-    attn_sum = attn_here, layout.flip(attn_there, 1)
-    queries_grad, keys_grad, values_grad = attend_back(
-        w, *self_operands, attended_grad, home_attended, self_logs, True, *SELF_BACK_BLOCKS
-    )
-    projected_grad = jnp.concatenate([queries_grad, keys_grad, values_grad], axis=-1)
-    token_term = back_dense(projected_grad, qkv_flat).astype(LOW)
-    token_part = lax.psum_scatter(token_term, "mp", scatter_dimension=0, tiled=True)
-    token_grad = (alpha_scale * self_grad + token_part.astype(WIDE)).astype(LOW)
+    ffn_sums = [fold_halves(pair) for pair in ffn_sums]
+    ffn_sums = [send(pair, 6 - bit) for pair, bit in zip(ffn_sums, BITS)]
+    attn_got = layout.flip(attn_grads(1), 1)
     home_grads = [
         jnp.concatenate(
             [weight_grad(a, cross_pair_grad), weight_grad(b, projected_grad)], axis=1
-        )[None]
+        ).reshape(CELLS // 2, 1, model_width // CELLS, -1)
         for a, b in zip(layout.core_halves(full_memory), layout.core_halves(full_tokens))
     ]
-    ffn_sums = [fold_last(pair) for pair in ffn_sums]
-    ffn_sums = [send(pair, 6 - bit) for pair, bit in zip(ffn_sums, BITS)]
-    attn_sum = send(fold_chip(attn_sum, 2), 2)
-    home_sum = send(fold_chip((home_grads[0], layout.flip(home_grads[1], 1)), 4), 4)
-    attn_sum = send(fold_last(attn_sum), 4)
-    home_sum = send(fold_last(home_sum), 2)
-    ffn_sums = jnp.concatenate([layout.fold(*pair) for pair in ffn_sums])
-    shards = jnp.concatenate([layout.fold(*attn_sum), ffn_sums], axis=2)
-    shard = lax.psum_scatter(shards, "mp", scatter_dimension=0, tiled=True)
-    shard = layout.to_rows(shard)[0].astype(WIDE)
-    home_grad = layout.to_rows(layout.fold(*home_sum))[0].astype(WIDE)
-    sums = layout.sum_all(jnp.concatenate([first_norm_terms, later_terms]))
-    edges = (w, 2 * w, 2 * w + n_hidden, 2 * w + 2 * n_hidden)
-    self_out_grad, cross_q_grad, ffn_in_grad, ffn_out_grad, cross_out_grad = jnp.split(
-        shard, edges, axis=1
-    )
+    home_sum = home_grads[0], layout.flip(home_grads[1], 1)
+    attn_sum = send(attn_grads(0, attn_got, 2), 2)
+    home_sum = send(fold_halves(home_sum), 4)
+    attn_sum = send(fold_halves(attn_sum), 4)
+    home_sum = send(fold_halves(home_sum), 2)
+    ffn_sums = jnp.concatenate([layout.fold(*pair)[0] for pair in ffn_sums])
+    ffn_shard = lax.psum_scatter(ffn_sums, "mp", scatter_dimension=0, tiled=True)
+    ffn_shard = layout.to_rows(ffn_shard)[0].astype(WIDE)
+    attn_sum = layout.to_rows(layout.fold(*attn_sum)[0])
+    attn_sum = [lax.dynamic_index_in_dim(attn_sum, k, 0, keepdims=False) for k in order]
+    attn_shard = sum(term.astype(WIDE) for term in layout.swap_mp(attn_sum))
+    home_grad = layout.to_rows(layout.fold(*home_sum)[0])[0].astype(WIDE)
+    (norm_terms,) = after([norm_terms], ffn_sums)
+    sums = layout.sum_dp(norm_terms)
+    edges = (n_hidden, 2 * n_hidden)
+    ffn_in_grad, ffn_out_grad, cross_out_grad = jnp.split(ffn_shard, edges, axis=1)
     return (
         mixed[:, None],
         token_grad[:, None],
         memory_grad[:, None],
         home_grad[:, 2 * w :].reshape(-1, 3, w),
-        self_out_grad,
-        cross_q_grad,
+        attn_shard[:, :w],
+        attn_shard[:, w:],
         home_grad[:, : 2 * w].reshape(-1, 2, w),
         cross_out_grad,
         ffn_in_grad,

time: 547 us -> 508 us (0.929)
  waiting for transfers between devices: 253 us -> 195 us
  starting transfers between devices: 49.3 us -> 78.8 us
  local copies, waits for them, and re-layouts: 55.5 us -> 45.6 us
    all_gather x2, waiting for transfers between devices: 61.2 us -> 1.7 us  [the longest x1 1.41 us: local(): full_tokens = lax.all_gather(tokens, 'mp', axis=0, tiled=True)]
    ppermute x47 -> x51, starting transfers between devices: 48.8 us -> 77.8 us  [permute(): return lax.ppermute(value, ('dp', 'mp'), pairs)]
    unnamed x148 -> x154, local copies, waits for them, and re-layouts: 35.2 us -> 22 us
    all_gather x1, waiting for transfers between devices: 0.01 us -> 12 us  [local(): full_memory = lax.all_gather(memory_there, 'mp', axis=0, tiled=True)]
    convert_element_type x11 -> x6, other arithmetic: 18.7 us -> 7.12 us  [fold(): return (value.astype(WIDE) + got.astype(WIDE)).astype(LOW)]
    ppermute x47 -> x51, waiting for transfers between devices: 192 us -> 181 us  [permute(): return lax.ppermute(value, ('dp', 'mp'), pairs)]
    concatenate x2 -> x9, other arithmetic: 1.8 us -> 8.62 us  [the longest x2 2.32 us: local(): jnp.concatenate([weight_grad(a, cross_pair_grad), weight_grad(b, projecte...]
  transfers between devices with their start and end apart: 53 -> 57, of which waited for: 23 -> 29; matrix products, arithmetic and copies ran while one was open for 15% -> 16% of each run, Pallas kernels for 16% -> 17%
where the time goes in v2:
time: 508 us; the launch traced here: 501 us
  waiting for transfers between devices  195 us (38%)
  Pallas kernels  111 us (22%)
  starting transfers between devices  78.8 us (16%)
  local copies, waits for them, and re-layouts  45.6 us (9%)
  other arithmetic  34.2 us (7%)
  matrix products  20.4 us (4%)
  between operations  15.6 us (3%)
    ppermute x51, waiting for transfers between devices, permute(): return lax.ppermute(value, ('dp', 'mp'), pairs)  181 us
    ppermute x51, starting transfers between devices, permute(): return lax.ppermute(value, ('dp', 'mp'), pairs)  77.8 us
    pallas_call x3, Pallas kernels, call(): pl.pallas_call(kernel, in_specs=[here] * len(operands) + [there] * len(st...  33.1 us
    pallas_call x6, Pallas kernels, weight_grads(): pl.pallas_call(lambda mp, *refs: kernel(*refs), grid_spec=pltpu.PrefetchS...  32.2 us
    pallas_call x2, Pallas kernels, attend_back(): pl.pallas_call(functools.partial(attend_back_kernel, key_block=key_block,...  27.4 us
    unnamed x154, local copies, waits for them, and re-layouts  22 us
    pallas_call x2, Pallas kernels, attend(): pl.pallas_call(functools.partial(attend_kernel, key_block=key_block, caus...  18.5 us
    all_gather x1, waiting for transfers between devices, local(): full_memory = lax.all_gather(memory_there, 'mp', axis=0, tiled=True)  12 us
  transfers between devices with their start and end apart: 57, of which 29 were waited for; matrix products, arithmetic and copies ran while one was open for 16% of the time, Pallas kernels for 17%

profile of v2, /device:TPU:0, one launch (start us, length us, event | category | flops | bytes accessed | tf_op | source)
XLA Modules:
  0.0 500.6 jit_solution(1888219393780640548)
XLA Ops:
  10.1 5.1 %collective-permute-start.2 = (bf16[128,512]{1,0:T(8,128)(2,1)S(1)}, bf16[128,512]{1,0:T(8,128)(2,1)S(1)}, u32[]{:S(2)}, u32[]{:S(2)}) collective-permute-start(bf16[128,512]{1,0:T(8,128)(2,1)S(1)} %pad_maximum_fusion.22), channel_id=1, source_target_pairs={{0,3},{1,2},{2,1},{3,0},{4,7},{5,6},{6,5},{7,4},{8,11},{9,10},{10,... | collective-permute-start | bytes 393224 | tf_op jit(solution)/shard_map/ppermute | solution.py:632
  19.6 15.6 %collective-permute-done.1 = bf16[128,512]{1,0:T(8,128)(2,1)S(1)} collective-permute-done((bf16[128,512]{1,0:T(8,128)(2,1)S(1)}, bf16[128,512]{1,0:T(8,128)(2,1)S(1)}, u32[]{:S(2)}, u32[]{:S(2)}) %collective-permute-start.1) | collective-permute-done | bytes 131104 | tf_op jit(solution)/shard_map/ppermute | solution.py:632
  36.9 6.3 %collective-permute-done.3 = bf16[3,128,512]{2,1,0:T(8,128)(2,1)S(1)} collective-permute-done((bf16[3,128,512]{2,1,0:T(8,128)(2,1)S(1)}, bf16[3,128,512]{2,1,0:T(8,128)(2,1)S(1)}, u32[]{:S(2)}, u32[]{:S(2)}) %collective-permute-start.3) | collective-permute-done | bytes 393248 | tf_op jit(solution)/shard_map/ppermute | solution.py:632
  44.8 11.5 %collective-permute-done.4.refs_2_ = bf16[2,3,128,512]{3,2,1,0:T(8,128)(2,1)S(1)} collective-permute-done((bf16[2,3,128,512]{3,2,1,0:T(8,128)(2,1)S(1)}, bf16[2,3,128,512]{3,2,1,0:T(8,128)(2,1)S(1)}, u32[]{:S(2)}, u32[]{:S(2)}) %collective-permute-start.4) | collective-permute-done | bytes 786464 | tf_op jit(solution)/shard_map/ppermute | solution.py:632
  67.9 9.0 %attend.2 = (bf16[1024,256]{1,0:T(8,128)(2,1)}, f32[2,8,1024]{2,1,0:T(8,128)}) custom-call(bf16[1024,768]{1,0:T(8,128)(2,1)} %convolution_convert_fusion.2.q_ref.k_ref.v_ref, bf16[1024,768]{1,0:T(8,128)(2,1)} %convolution_convert_fusion.2.q_ref.k_ref.v_ref, bf16[1024,768]{1,0:T(8,128)(2,1)} %convolution_convert_fusion.2.q_ref.k_ref.v_ref), custom_call_target="tpu_custom_call" | custom-call | flops 2147483648 | bytes 2097152 | tf_op jit(solution)/shard_map/attend/pallas_call | solution.py:173
  83.0 10.3 %collective-permute-done.7.refs_1_ = bf16[256,256]{1,0:T(8,128)(2,1)S(1)} collective-permute-done((bf16[256,256]{1,0:T(8,128)(2,1)S(1)}, bf16[256,256]{1,0:T(8,128)(2,1)S(1)}, u32[]{:S(2)}, u32[]{:S(2)}) %collective-permute-start.7) | collective-permute-done | bytes 131104 | tf_op jit(solution)/shard_map/ppermute | solution.py:632
  100.0 5.9 %enter_cross.1 = (f32[256,1024]{1,0:T(8,128)}, f32[256,128]{1,0:T(8,128)}, bf16[256,1024]{1,0:T(8,128)(2,1)}, bf16[256,256]{1,0:T(8,128)(2,1)}, bf16[256,256]{1,...) custom-call(bf16[256,1024]{1,0:T(8,128)(2,1)} %bitcast.82, f32[3,1024]{1,0:T(4,128)} %gain_ref.5, ...), custom_call_target="tpu_custom_call" | custom-call | flops 1073741824 | bytes 5267456 | tf_op jit(solution)/shard_map/enter_cross/pallas_call | solution.py:419
  108.3 9.4 %collective-permute-start.11 = (bf16[256,256]{1,0:T(8,128)(2,1)}, bf16[256,256]{1,0:T(8,128)(2,1)S(1)}, u32[]{:S(2)}, u32[]{:S(2)}) collective-permute-start(bf16[256,256]{1,0:T(8,128)(2,1)} %get-tuple-element.75), channel_id=1, source_target_pairs={{0,2},{1,3},{2,0},{3,1},{4,6},{5,7},{6,4},{7,5},{8,10},{9,11},{10,... | collective-permute-start | bytes 393224 | tf_op jit(solution)/shard_map/ppermute | solution.py:632
  118.2 16.5 %collective-permute-done.11.refs_3_ = bf16[256,256]{1,0:T(8,128)(2,1)S(1)} collective-permute-done((bf16[256,256]{1,0:T(8,128)(2,1)}, bf16[256,256]{1,0:T(8,128)(2,1)S(1)}, u32[]{:S(2)}, u32[]{:S(2)}) %collective-permute-start.11) | collective-permute-done | bytes 131104 | tf_op jit(solution)/shard_map/ppermute | solution.py:632
  143.4 19.5 %collective-permute-done.15 = bf16[3,128,1280]{2,1,0:T(8,128)(2,1)} collective-permute-done((bf16[3,128,1280]{2,1,0:T(8,128)(2,1)}, bf16[3,128,1280]{2,1,0:T(8,128)(2,1)}, u32[]{:S(2)}, u32[]{:S(2)}) %collective-permute-start.15) | collective-permute-done | bytes 983072 | tf_op jit(solution)/shard_map/ppermute | solution.py:632
  172.2 12.0 %all-gather.6.cloned.1.call-done = bf16[1024,1024]{1,0:T(8,128)(2,1)} async-done(((bf16[256,1024]{1,0:T(8,128)(2,1)}), bf16[1024,1024]{1,0:T(8,128)(2,1)}) %all-gather.6.cloned.1.call-update) | async-done | bytes 2097168 | tf_op jit(solution)/shard_map/all_gather | solution.py:749
  188.0 9.5 %attend.3 = (bf16[1024,256]{1,0:T(8,128)(2,1)}, f32[2,8,1024]{2,1,0:T(8,128)}) custom-call(bf16[1024,256]{1,0:T(8,128)(2,1)} %order.14.q_ref, bf16[1024,512]{1,0:T(8,128)(2,1)} %convolution_convert_fusion.3.k_ref.v_ref, bf16[1024,512]{1,0:T(8,128)(2,1)} %convolution_convert_fusion.3.k_ref.v_ref), custom_call_target="tpu_custom_call" | custom-call | flops 2147483648 | bytes 2097152 | tf_op jit(solution)/shard_map/attend/pallas_call | solution.py:173
  197.6 7.5 %collective-permute-done.20.refs_0_ = bf16[2,3,128,1024]{3,2,1,0:T(8,128)(2,1)} collective-permute-done((bf16[2,3,128,1024]{3,2,1,0:T(8,128)(2,1)}, bf16[2,3,128,1024]{3,2,1,0:T(8,128)(2,1)}, u32[]{:S(2)}, u32[]{:S(2)}) %collective-permute-start.20) | collective-permute-done | bytes 1572896 | tf_op jit(solution)/shard_map/ppermute | solution.py:632
  205.1 7.5 %collective-permute-done.21.refs_1_ = bf16[2,3,128,1280]{3,2,1,0:T(8,128)(2,1)} collective-permute-done((bf16[2,3,128,1280]{3,2,1,0:T(8,128)(2,1)}, bf16[2,3,128,1280]{3,2,1,0:T(8,128)(2,1)}, u32[]{:S(2)}, u32[]{:S(2)}) %collective-permute-start.21) | collective-permute-done | bytes 1966112 | tf_op jit(solution)/shard_map/ppermute | solution.py:632
  220.8 6.0 %collective-permute-done.18.refs_2_ = bf16[256,256]{1,0:T(8,128)(2,1)S(1)} collective-permute-done((bf16[256,256]{1,0:T(8,128)(2,1)S(1)}, bf16[256,256]{1,0:T(8,128)(2,1)S(1)}, u32[]{:S(2)}, u32[]{:S(2)}) %collective-permute-start.18) | collective-permute-done | bytes 131104 | tf_op jit(solution)/shard_map/ppermute | solution.py:632
  229.5 20.4 %feed_forward.1 = (bf16[256,1024]{1,0:T(8,128)(2,1)}, bf16[256,1024]{1,0:T(8,128)(2,1)}, bf16[256,1024]{1,0:T(8,128)(2,1)}, f32[256,1024]{1,0:T(8,128)}, bf16[25...) custom-call(f32[256,1024]{1,0:T(8,128)} %get-tuple-element.72.first_, ...), custom_call_target="tpu_custom_call" | custom-call | flops 8589934592 | bytes 20996096 | tf_op jit(solution)/shard_map/feed_forward/pallas_call | solution.py:419
  250.0 5.2 %weight_grads.6.refs_1_ = bf16[4,2,128,2304]{3,2,1,0:T(8,128)(2,1)} custom-call(s32[1]{0:T(128)} %bitcast.16.mp, bf16[256,1024]{1,0:T(8,128)(2,1)} %get-tuple-element.89.refs_0_, bf16[256,1024]{1,0:T(8,128)(2,1)} %get-tuple-element.90.refs_1_, bf16[256,1024]{1,0:T(8,128)(2,1)} %get-tuple-element.91.refs_2_, bf16[4,256,1024]{2,1,0:T(8,128)(2,1)} %get-tuple-element.92.refs_3_, ...), custom_call_target="tpu_custom_call" | custom-call | flops 1207959552 | bytes 4718592 | tf_op jit(solution)/shard_map/weight_grads/pallas_call | solution.py:577
  255.3 5.3 %weight_grads.7.refs_2_ = bf16[4,2,128,2304]{3,2,1,0:T(8,128)(2,1)} custom-call(s32[1]{0:T(128)} %bitcast.16.mp, bf16[256,1024]{1,0:T(8,128)(2,1)} %get-tuple-element.89.refs_0_, bf16[256,1024]{1,0:T(8,128)(2,1)} %get-tuple-element.90.refs_1_, bf16[256,1024]{1,0:T(8,128)(2,1)} %get-tuple-element.91.refs_2_, bf16[4,256,1024]{2,1,0:T(8,128)(2,1)} %get-tuple-element.92.refs_3_, ...), custom_call_target="tpu_custom_call" | custom-call | flops 1207959552 | bytes 4718592 | tf_op jit(solution)/shard_map/weight_grads/pallas_call | solution.py:577
  269.2 7.5 %collective-permute-done.25 = bf16[256,256]{1,0:T(8,128)(2,1)S(1)} collective-permute-done((bf16[256,256]{1,0:T(8,128)(2,1)S(1)}, bf16[256,256]{1,0:T(8,128)(2,1)S(1)}, u32[]{:S(2)}, u32[]{:S(2)}) %collective-permute-start.25) | collective-permute-done | bytes 131104 | tf_op jit(solution)/shard_map/ppermute | solution.py:632
  277.6 13.8 %attend_back.2 = (bf16[1024,256]{1,0:T(8,128)(2,1)}, bf16[1024,256]{1,0:T(8,128)(2,1)}, bf16[1024,256]{1,0:T(8,128)(2,1)}) custom-call(bf16[1024,256]{1,0:T(8,128)(2,1)} %order.14.q_ref, bf16[1024,256]{1,0:T(8,128)(2,1)} %order.16.g_ref, bf16[1024,256]{1,0:T(8,128)(2,1)} %get-tuple-element.79.refs_2_.o_ref, f32[2,8,1024]{2,1,0:T(8,128)} %get-tuple-element.94.lse_ref, ...), custom_call_target="tpu_custom_call" | custom-call | flops 4294967296 | bytes 4194304 | tf_op jit(solution)/shard_map/attend_back/pallas_call | solution.py:201
  307.9 5.9 %weight_grads.8 = (bf16[2,2,128,2304]{3,2,1,0:T(8,128)(2,1)}, bf16[2,2,128,2304]{3,2,1,0:T(8,128)(2,1)}) custom-call(s32[1]{0:T(128)} %bitcast.16.mp, bf16[256,1024]{1,0:T(8,128)(2,1)} %get-tuple-element.89.refs_0_, bf16[256,1024]{1,0:T(8,128)(2,1)} %get-tuple-element.90.refs_1_, bf16[256,1024]{1,0:T(8,128)(2,1)} %get-tuple-element.91.refs_2_, ...), custom_call_target="tpu_custom_call" | custom-call | flops 1207959552 | bytes 4718592 | tf_op jit(solution)/shard_map/weight_grads/pallas_call | solution.py:577
  315.0 5.9 %weight_grads.9 = (bf16[2,2,128,2304]{3,2,1,0:T(8,128)(2,1)}, bf16[2,2,128,2304]{3,2,1,0:T(8,128)(2,1)}) custom-call(s32[1]{0:T(128)} %bitcast.16.mp, bf16[256,1024]{1,0:T(8,128)(2,1)} %get-tuple-element.89.refs_0_, bf16[256,1024]{1,0:T(8,128)(2,1)} %get-tuple-element.90.refs_1_, bf16[256,1024]{1,0:T(8,128)(2,1)} %get-tuple-element.91.refs_2_, ...), custom_call_target="tpu_custom_call" | custom-call | flops 1207959552 | bytes 4718592 | tf_op jit(solution)/shard_map/weight_grads/pallas_call | solution.py:577
  324.9 6.7 %leave_cross.1 = (f32[256,1024]{1,0:T(8,128)}, bf16[256,1024]{1,0:T(8,128)(2,1)}, f32[2,1024]{1,0:T(2,128)}, bf16[256,256]{1,0:T(8,128)(2,1)}, bf16[256,256]{1,0...) custom-call(f32[256,1024]{1,0:T(8,128)} %get-tuple-element.83.cross_grad_ref, f32[3,1024]{1,0:T(4,128)} %gain_ref.5, ...), custom_call_target="tpu_custom_call" | custom-call | flops 1073741824 | bytes 6959104 | tf_op jit(solution)/shard_map/leave_cross/pallas_call | solution.py:419
  333.4 9.5 %collective-permute-start.32 = (bf16[304,256]{1,0:T(8,128)(2,1)S(1)}, bf16[304,256]{1,0:T(8,128)(2,1)S(1)}, u32[]{:S(2)}, u32[]{:S(2)}) collective-permute-start(bf16[304,256]{1,0:T(8,128)(2,1)S(1)} %get-tuple-element.178), channel_id=1, source_target_pairs={{0,1},{1,0},{2,3},{3,2},{4,5},{5,4},{6,7},{7,6},{8,9},{9,8},{10,11... | collective-permute-start | bytes 466952 | tf_op jit(solution)/shard_map/ppermute | solution.py:632
  352.1 8.5 %collective-permute-done.33 = bf16[304,256]{1,0:T(8,128)(2,1)S(1)} collective-permute-done((bf16[304,256]{1,0:T(8,128)(2,1)S(1)}, bf16[304,256]{1,0:T(8,128)(2,1)S(1)}, u32[]{:S(2)}, u32[]{:S(2)}) %collective-permute-start.33) | collective-permute-done | bytes 155680 | tf_op jit(solution)/shard_map/ppermute | solution.py:632
  362.8 13.6 %attend_back.3 = (bf16[1024,256]{1,0:T(8,128)(2,1)}, bf16[1024,256]{1,0:T(8,128)(2,1)}, bf16[1024,256]{1,0:T(8,128)(2,1)}) custom-call(bf16[1024,768]{1,0:T(8,128)(2,1)} %convolution_convert_fusion.2.q_ref.k_ref.v_ref, bf16[1024,256]{1,0:T(8,128)(2,1)} %order.18.g_ref, bf16[1024,256]{1,0:T(8,128)(2,1)} %get-tuple-element.67.o_ref, ...), custom_call_target="tpu_custom_call" | custom-call | flops 4294967296 | bytes 4194304 | tf_op jit(solution)/shard_map/attend_back/pallas_call | solution.py:201
  402.6 13.2 %collective-permute-done.47 = bf16[1,2,128,2304]{3,2,1,0:T(8,128)(2,1)} collective-permute-done((bf16[1,2,128,2304]{3,2,1,0:T(8,128)(2,1)}, bf16[1,2,128,2304]{3,2,1,0:T(8,128)(2,1)}, u32[]{:S(2)}, u32[]{:S(2)}) %collective-permute-start.47) | collective-permute-done | bytes 1179680 | tf_op jit(solution)/shard_map/ppermute | solution.py:632
  427.6 5.1 %weight_grads.11 = (bf16[2,4,128,512]{3,2,1,0:T(8,128)(2,1)}, bf16[2,4,128,512]{3,2,1,0:T(8,128)(2,1)}) custom-call(s32[1]{0:T(128)} %bitcast.16.mp, bf16[256,1024]{1,0:T(8,128)(2,1)} %order.20.refs_0_, bf16[256,1024]{1,0:T(8,128)(2,1)} %get-tuple-element.115.refs_1_, bf16[4,256,256]{2,1,0:T(8,128)(2,1)} %pad_maximum_fusion.13.refs_2_, ...), custom_call_target="tpu_custom_call" | custom-call | flops 536870912 | bytes 2097152 | tf_op jit(solution)/shard_map/weight_grads/pallas_call | solution.py:577
  445.8 10.7 %collective-permute-done.41 = bf16[2,4,128,512]{3,2,1,0:T(8,128)(2,1)} collective-permute-done((bf16[2,4,128,512]{3,2,1,0:T(8,128)(2,1)}, bf16[2,4,128,512]{3,2,1,0:T(8,128)(2,1)}, u32[]{:S(2)}, u32[]{:S(2)}) %collective-permute-start.41) | collective-permute-done | bytes 1048608 | tf_op jit(solution)/shard_map/ppermute | solution.py:632
  462.2 7.6 %collective-permute-done.42 = bf16[1,4,128,512]{3,2,1,0:T(8,128)(2,1)S(1)} collective-permute-done((bf16[1,4,128,512]{3,2,1,0:T(8,128)(2,1)S(1)}, bf16[1,4,128,512]{3,2,1,0:T(8,128)(2,1)S(1)}, u32[]{:S(2)}, u32[]{:S(2)}) %collective-permute-start.42) | collective-permute-done | bytes 524320 | tf_op jit(solution)/shard_map/ppermute | solution.py:632
  470.4 5.3 %collective-permute-start.44 = (bf16[128,512]{1,0:T(8,128)(2,1)S(1)}, bf16[128,512]{1,0:T(8,128)(2,1)S(1)}, u32[]{:S(2)}, u32[]{:S(2)}) collective-permute-start(bf16[128,512]{1,0:T(8,128)(2,1)S(1)} %get-tuple-element.157), channel_id=1, source_target_pairs={{0,2},{1,3},{2,0},{3,1},{4,6},{5,7},{6,4},{7,5},{8,10},{9,11},{10,... | collective-permute-start | bytes 393224 | tf_op jit(solution)/shard_map/ppermute | solution.py:632
  481.2 6.5 %collective-permute-done.44 = bf16[128,512]{1,0:T(8,128)(2,1)S(1)} collective-permute-done((bf16[128,512]{1,0:T(8,128)(2,1)S(1)}, bf16[128,512]{1,0:T(8,128)(2,1)S(1)}, u32[]{:S(2)}, u32[]{:S(2)}) %collective-permute-start.44) | collective-permute-done | bytes 131104 | tf_op jit(solution)/shard_map/ppermute | solution.py:632
  (347 shorter events, 182.7 us)
Async XLA Ops:
  7.2 53.4 %all-gather.8.cloned.1.call-start = ((), (), s32[]{:S(2)}) async-start(), calls=%async_computation.7 | async-start | bytes 2621440 | tf_op jit(solution)/shard_map/all_gather | solution.py:730
  9.1 125.9 %all-gather.10.cloned.1.call-start = ((), (), s32[]{:S(2)}) async-start(), calls=%async_computation.8 | async-start | bytes 2949120 | tf_op jit(solution)/shard_map/all_gather | solution.py:738
  15.2 20.0 %collective-permute-start.1 = (bf16[128,512]{1,0:T(8,128)(2,1)S(1)}, bf16[128,512]{1,0:T(8,128)(2,1)S(1)}, u32[]{:S(2)}, u32[]{:S(2)}) collective-permute-start(bf16[128,512]{1,0:T(8,128)(2,1)S(1)} %pad_maximum_fusion.22), channel_id=1, source_target_pairs={{0,2},{1,3},{2,0},{3,1},{4,6},{5,7},{6,4},{7,5},{8,10},{9,11},{10,... | collective-permute-start | bytes 393224 | tf_op jit(solution)/shard_map/ppermute | solution.py:632
  15.2 20.0 %collective-permute-start = (bf16[128,512]{1,0:T(8,128)(2,1)S(1)}, bf16[128,512]{1,0:T(8,128)(2,1)S(1)}, u32[]{:S(2)}, u32[]{:S(2)}) collective-permute-start(bf16[128,512]{1,0:T(8,128)(2,1)S(1)} %pad_maximum_fusion.22), channel_id=1, source_target_pairs={{0,1},{1,0},{2,3},{3,2},{4,5},{5,4},{6,7},{7,6},{8,9},{9,8},{10,11... | collective-permute-start | bytes 393224 | tf_op jit(solution)/shard_map/ppermute | solution.py:632
  60.7 123.5 %all-gather.6.cloned.1.call-start = ((), (), s32[]{:S(2)}) async-start(), calls=%async_computation.3 | async-start | bytes 2621440 | tf_op jit(solution)/shard_map/all_gather | solution.py:749
  78.7 17.6 %collective-permute-start.8 = (bf16[256,256]{1,0:T(8,128)(2,1)S(1)}, bf16[256,256]{1,0:T(8,128)(2,1)S(1)}, u32[]{:S(2)}, u32[]{:S(2)}) collective-permute-start(bf16[256,256]{1,0:T(8,128)(2,1)S(1)} %get-tuple-element.169), channel_id=1, source_target_pairs={{0,2},{1,3},{2,0},{3,1},{4,6},{5,7},{6,4},{7,5},{8,10},{9,11},{10,... | collective-permute-start | bytes 393224 | tf_op jit(solution)/shard_map/ppermute | solution.py:632
  81.8 17.6 %collective-permute-start.9 = (bf16[256,256]{1,0:T(8,128)(2,1)S(1)}, bf16[256,256]{1,0:T(8,128)(2,1)S(1)}, u32[]{:S(2)}, u32[]{:S(2)}) collective-permute-start(bf16[256,256]{1,0:T(8,128)(2,1)S(1)} %get-tuple-element.168), channel_id=1, source_target_pairs={{0,3},{1,2},{2,1},{3,0},{4,7},{5,6},{6,5},{7,4},{8,11},{9,10},{10,... | collective-permute-start | bytes 393224 | tf_op jit(solution)/shard_map/ppermute | solution.py:632
  108.3 26.4 %collective-permute-start.11 = (bf16[256,256]{1,0:T(8,128)(2,1)}, bf16[256,256]{1,0:T(8,128)(2,1)S(1)}, u32[]{:S(2)}, u32[]{:S(2)}) collective-permute-start(bf16[256,256]{1,0:T(8,128)(2,1)} %get-tuple-element.75), channel_id=1, source_target_pairs={{0,2},{1,3},{2,0},{3,1},{4,6},{5,7},{6,4},{7,5},{8,10},{9,11},{10,... | collective-permute-start | bytes 393224 | tf_op jit(solution)/shard_map/ppermute | solution.py:632
  138.9 24.1 %collective-permute-start.15 = (bf16[3,128,1280]{2,1,0:T(8,128)(2,1)}, bf16[3,128,1280]{2,1,0:T(8,128)(2,1)}, u32[]{:S(2)}, u32[]{:S(2)}) collective-permute-start(bf16[3,128,1280]{2,1,0:T(8,128)(2,1)} %pad_maximum_fusion.5), channel_id=1, source_target_pairs={{0,16},{1,17},{2,18},{3,19},{4,20},{5,21},{6,22},{7,23},{8,24},{9,... | collective-permute-start | bytes 2949128 | tf_op jit(solution)/shard_map/ppermute | solution.py:632
  140.4 221.6 %reduce-scatter.4.cloned.1.call-start = ((), (), s32[]{:S(2)}) async-start(), calls=%async_computation.4 | async-start | bytes 2621440 | tf_op jit(solution)/shard_map/reduce_scatter | solution.py:810
  141.8 23.9 %collective-permute-start.13 = (bf16[3,128,1024]{2,1,0:T(8,128)(2,1)S(1)}, bf16[3,128,1024]{2,1,0:T(8,128)(2,1)S(1)}, u32[]{:S(2)}, u32[]{:S(2)}) collective-permute-start(bf16[3,128,1024]{2,1,0:T(8,128)(2,1)S(1)} %pad_maximum_fusion.7), channel_id=1, source_target_pairs={{0,8},{1,9},{2,10},{3,11},{4,12},{5,13},{6,14},{7,15},{8,0},{9,1},... | collective-permute-start | bytes 2359304 | tf_op jit(solution)/shard_map/ppermute | solution.py:632
  167.6 45.0 %collective-permute-start.21 = (bf16[2,3,128,1280]{3,2,1,0:T(8,128)(2,1)}, bf16[2,3,128,1280]{3,2,1,0:T(8,128)(2,1)}, u32[]{:S(2)}, u32[]{:S(2)}) collective-permute-start(bf16[2,3,128,1280]{3,2,1,0:T(8,128)(2,1)} %pad_maximum_fusion.1.refs_11_), channel_id=1, source_target_pairs={{0,8},{1,9},{2,10},{3,11},{4,12},{5,13},{6,14},{7,15},{8,0},{9,1},... | collective-permute-start | bytes 5898248 | tf_op jit(solution)/shard_map/ppermute | solution.py:632
  168.8 36.3 %collective-permute-start.20 = (bf16[2,3,128,1024]{3,2,1,0:T(8,128)(2,1)}, bf16[2,3,128,1024]{3,2,1,0:T(8,128)(2,1)}, u32[]{:S(2)}, u32[]{:S(2)}) collective-permute-start(bf16[2,3,128,1024]{3,2,1,0:T(8,128)(2,1)} %pad_maximum_fusion.2.refs_7_), channel_id=1, source_target_pairs={{0,16},{1,17},{2,18},{3,19},{4,20},{5,21},{6,22},{7,23},{8,24},{9,... | collective-permute-start | bytes 4718600 | tf_op jit(solution)/shard_map/ppermute | solution.py:632
  255.2 52.7 %collective-permute-start.30 = (bf16[4,2,128,2304]{3,2,1,0:T(8,128)(2,1)}, bf16[4,2,128,2304]{3,2,1,0:T(8,128)(2,1)}, u32[]{:S(2)}, u32[]{:S(2)}) collective-permute-start(bf16[4,2,128,2304]{3,2,1,0:T(8,128)(2,1)} %weight_grads.6.refs_1_), channel_id=1, source_target_pairs={{0,4},{1,5},{2,6},{3,7},{4,0},{5,1},{6,2},{7,3},{8,12},{9,13},{10,... | collective-permute-start | bytes 14155784 | tf_op jit(solution)/shard_map/ppermute | solution.py:632
  260.6 54.4 %collective-permute-start.31 = (bf16[4,2,128,2304]{3,2,1,0:T(8,128)(2,1)}, bf16[4,2,128,2304]{3,2,1,0:T(8,128)(2,1)}, u32[]{:S(2)}, u32[]{:S(2)}) collective-permute-start(bf16[4,2,128,2304]{3,2,1,0:T(8,128)(2,1)} %weight_grads.7.refs_2_), channel_id=1, source_target_pairs={{0,4},{1,5},{2,6},{3,7},{4,0},{5,1},{6,2},{7,3},{8,12},{9,13},{10,... | collective-permute-start | bytes 14155784 | tf_op jit(solution)/shard_map/ppermute | solution.py:632
  297.3 191.1 %reduce-scatter.6.cloned.1.call-start = ((), (), s32[]{:S(2)}) async-start(), calls=%async_computation.5 | async-start | bytes 2621440 | tf_op jit(solution)/shard_map/reduce_scatter | solution.py:834
  302.6 20.1 %collective-permute-start.27 = (bf16[256,256]{1,0:T(8,128)(2,1)}, bf16[256,256]{1,0:T(8,128)(2,1)S(1)}, u32[]{:S(2)}, u32[]{:S(2)}) collective-permute-start(bf16[256,256]{1,0:T(8,128)(2,1)} %get-tuple-element.161), channel_id=1, source_target_pairs={{0,1},{1,0},{2,3},{3,2},{4,5},{5,4},{6,7},{7,6},{8,9},{9,8},{10,11... | collective-permute-start | bytes 393224 | tf_op jit(solution)/shard_map/ppermute | solution.py:632
  302.6 21.0 %collective-permute-start.28 = (bf16[256,256]{1,0:T(8,128)(2,1)}, bf16[256,256]{1,0:T(8,128)(2,1)S(1)}, u32[]{:S(2)}, u32[]{:S(2)}) collective-permute-start(bf16[256,256]{1,0:T(8,128)(2,1)} %get-tuple-element.160), channel_id=1, source_target_pairs={{0,2},{1,3},{2,0},{3,1},{4,6},{5,7},{6,4},{7,5},{8,10},{9,11},{10,... | collective-permute-start | bytes 393224 | tf_op jit(solution)/shard_map/ppermute | solution.py:632
  304.6 19.0 %collective-permute-start.29 = (bf16[256,256]{1,0:T(8,128)(2,1)}, bf16[256,256]{1,0:T(8,128)(2,1)S(1)}, u32[]{:S(2)}, u32[]{:S(2)}) collective-permute-start(bf16[256,256]{1,0:T(8,128)(2,1)} %get-tuple-element.159), channel_id=1, source_target_pairs={{0,3},{1,2},{2,1},{3,0},{4,7},{5,6},{6,5},{7,4},{8,11},{9,10},{10,... | collective-permute-start | bytes 393224 | tf_op jit(solution)/shard_map/ppermute | solution.py:632
  313.8 68.2 %collective-permute-start.35 = (bf16[2,2,128,2304]{3,2,1,0:T(8,128)(2,1)}, bf16[2,2,128,2304]{3,2,1,0:T(8,128)(2,1)S(1)}, u32[]{:S(2)}, u32[]{:S(2)}) collective-permute-start(bf16[2,2,128,2304]{3,2,1,0:T(8,128)(2,1)} %get-tuple-element.98.refs_4_), channel_id=1, source_target_pairs={{0,8},{1,9},{2,10},{3,11},{4,12},{5,13},{6,14},{7,15},{8,0},{9,1},... | collective-permute-start | bytes 7077896 | tf_op jit(solution)/shard_map/ppermute | solution.py:632
  320.9 61.1 %collective-permute-start.36 = (bf16[2,2,128,2304]{3,2,1,0:T(8,128)(2,1)}, bf16[2,2,128,2304]{3,2,1,0:T(8,128)(2,1)}, u32[]{:S(2)}, u32[]{:S(2)}) collective-permute-start(bf16[2,2,128,2304]{3,2,1,0:T(8,128)(2,1)} %get-tuple-element.99.refs_5_), channel_id=1, source_target_pairs={{0,16},{1,17},{2,18},{3,19},{4,20},{5,21},{6,22},{7,23},{8,24},{9,... | collective-permute-start | bytes 7077896 | tf_op jit(solution)/shard_map/ppermute | solution.py:632
  333.4 18.7 %collective-permute-start.32 = (bf16[304,256]{1,0:T(8,128)(2,1)S(1)}, bf16[304,256]{1,0:T(8,128)(2,1)S(1)}, u32[]{:S(2)}, u32[]{:S(2)}) collective-permute-start(bf16[304,256]{1,0:T(8,128)(2,1)S(1)} %get-tuple-element.178), channel_id=1, source_target_pairs={{0,1},{1,0},{2,3},{3,2},{4,5},{5,4},{6,7},{7,6},{8,9},{9,8},{10,11... | collective-permute-start | bytes 466952 | tf_op jit(solution)/shard_map/ppermute | solution.py:632
  342.9 17.7 %collective-permute-start.33 = (bf16[304,256]{1,0:T(8,128)(2,1)S(1)}, bf16[304,256]{1,0:T(8,128)(2,1)S(1)}, u32[]{:S(2)}, u32[]{:S(2)}) collective-permute-start(bf16[304,256]{1,0:T(8,128)(2,1)S(1)} %get-tuple-element.177), channel_id=1, source_target_pairs={{0,2},{1,3},{2,0},{3,1},{4,6},{5,7},{6,4},{7,5},{8,10},{9,11},{10,... | collective-permute-start | bytes 466952 | tf_op jit(solution)/shard_map/ppermute | solution.py:632
  342.9 17.7 %collective-permute-start.34 = (bf16[304,256]{1,0:T(8,128)(2,1)S(1)}, bf16[304,256]{1,0:T(8,128)(2,1)S(1)}, u32[]{:S(2)}, u32[]{:S(2)}) collective-permute-start(bf16[304,256]{1,0:T(8,128)(2,1)S(1)} %get-tuple-element.176), channel_id=1, source_target_pairs={{0,3},{1,2},{2,1},{3,0},{4,7},{5,6},{6,5},{7,4},{8,11},{9,10},{10,... | collective-permute-start | bytes 466952 | tf_op jit(solution)/shard_map/ppermute | solution.py:632
  383.5 107.0 %reduce-scatter.8.cloned.1.call-start = ((), (), s32[]{:S(2)}) async-start(), calls=%async_computation.6 | async-start | bytes 2949120 | tf_op jit(solution)/shard_map/reduce_scatter | solution.py:858
  388.0 27.8 %collective-permute-start.47 = (bf16[1,2,128,2304]{3,2,1,0:T(8,128)(2,1)}, bf16[1,2,128,2304]{3,2,1,0:T(8,128)(2,1)}, u32[]{:S(2)}, u32[]{:S(2)}) collective-permute-start(bf16[1,2,128,2304]{3,2,1,0:T(8,128)(2,1)} %slice.120), channel_id=1, source_target_pairs={{0,8},{1,9},{2,10},{3,11},{4,12},{5,13},{6,14},{7,15},{8,0},{9,1},... | collective-permute-start | bytes 3538952 | tf_op jit(solution)/shard_map/ppermute | solution.py:632
  391.4 27.1 %collective-permute-start.46 = (bf16[1,2,128,2304]{3,2,1,0:T(8,128)(2,1)}, bf16[1,2,128,2304]{3,2,1,0:T(8,128)(2,1)}, u32[]{:S(2)}, u32[]{:S(2)}) collective-permute-start(bf16[1,2,128,2304]{3,2,1,0:T(8,128)(2,1)} %slice.118), channel_id=1, source_target_pairs={{0,16},{1,17},{2,18},{3,19},{4,20},{5,21},{6,22},{7,23},{8,24},{9,... | collective-permute-start | bytes 3538952 | tf_op jit(solution)/shard_map/ppermute | solution.py:632
  397.3 39.6 %collective-permute-start.37 = (bf16[4,1,128,1280]{2,3,1,0:T(8,128)(2,1)}, bf16[4,1,128,1280]{2,3,1,0:T(8,128)(2,1)}, u32[]{:S(2)}, u32[]{:S(2)}) collective-permute-start(bf16[4,1,128,1280]{2,3,1,0:T(8,128)(2,1)} %copy.48), channel_id=1, source_target_pairs={{0,4},{1,5},{2,6},{3,7},{4,0},{5,1},{6,2},{7,3},{8,12},{9,13},{10,... | collective-permute-start | bytes 3932168 | tf_op jit(solution)/shard_map/ppermute | solution.py:632
  402.1 25.5 %collective-permute-start.40 = (bf16[4,4,128,512]{3,2,1,0:T(8,128)(2,1)}, bf16[4,4,128,512]{3,2,1,0:T(8,128)(2,1)}, u32[]{:S(2)}, u32[]{:S(2)}) collective-permute-start(bf16[4,4,128,512]{3,2,1,0:T(8,128)(2,1)} %weight_grads.10), channel_id=1, source_target_pairs={{0,4},{1,5},{2,6},{3,7},{4,0},{5,1},{6,2},{7,3},{8,12},{9,13},{10,... | collective-permute-start | bytes 6291464 | tf_op jit(solution)/shard_map/ppermute | solution.py:632
  432.8 23.6 %collective-permute-start.41 = (bf16[2,4,128,512]{3,2,1,0:T(8,128)(2,1)}, bf16[2,4,128,512]{3,2,1,0:T(8,128)(2,1)}, u32[]{:S(2)}, u32[]{:S(2)}) collective-permute-start(bf16[2,4,128,512]{3,2,1,0:T(8,128)(2,1)} %get-tuple-element.117), channel_id=1, source_target_pairs={{0,8},{1,9},{2,10},{3,11},{4,12},{5,13},{6,14},{7,15},{8,0},{9,1},... | collective-permute-start | bytes 3145736 | tf_op jit(solution)/shard_map/ppermute | solution.py:632
  439.6 20.6 %collective-permute-start.38 = (bf16[2,1,128,1280]{2,3,1,0:T(8,128)(2,1)S(1)}, bf16[2,1,128,1280]{2,3,1,0:T(8,128)(2,1)S(1)}, u32[]{:S(2)}, u32[]{:S(2)}) collective-permute-start(bf16[2,1,128,1280]{2,3,1,0:T(8,128)(2,1)S(1)} %slice.108), channel_id=1, source_target_pairs={{0,16},{1,17},{2,18},{3,19},{4,20},{5,21},{6,22},{7,23},{8,24},{9,... | collective-permute-start | bytes 1966088 | tf_op jit(solution)/shard_map/ppermute | solution.py:632
  470.4 17.3 %collective-permute-start.44 = (bf16[128,512]{1,0:T(8,128)(2,1)S(1)}, bf16[128,512]{1,0:T(8,128)(2,1)S(1)}, u32[]{:S(2)}, u32[]{:S(2)}) collective-permute-start(bf16[128,512]{1,0:T(8,128)(2,1)S(1)} %get-tuple-element.157), channel_id=1, source_target_pairs={{0,2},{1,3},{2,0},{3,1},{4,6},{5,7},{6,4},{7,5},{8,10},{9,11},{10,... | collective-permute-start | bytes 393224 | tf_op jit(solution)/shard_map/ppermute | solution.py:632
  (98 other events, 629.7 us)
Sparse Core Ops, SparseCore 0:
  9.6 50.9 all-gather.7
  62.2 72.7 all-gather.9
  140.5 43.6 all-gather.5
  297.4 54.5 reduce-scatter.3
  383.6 44.4 reduce-scatter.5
  430.2 51.3 reduce-scatter.7

commit v3 on v2

--- a/solution.py
+++ b/solution.py
@@ -67,10 +67,42 @@
     return carry
 
 
-def attend_kernel(q_ref, k_ref, v_ref, o_ref, lse_ref, *, key_block, causal):
-    query_block = q_ref.shape[0]
+def take_blocks(refs, rows, query_block, ordered):
+    if not ordered:
+        return jnp.concatenate([ref[...] for ref in refs], axis=0)
+    per = query_block // rows
+    parts = []
+    for e in range(per):
+        place = jnp.bitwise_xor(pl.program_id(1) * per + e, lax.axis_index("mp"))
+        part = refs[0][:rows, :].astype(WIDE)
+        for k in range(1, len(refs)):
+            part = jnp.where(place == k, refs[k][:rows, :].astype(WIDE), part)
+        parts.append(part.astype(LOW))
+    return jnp.concatenate(parts, axis=0)
+
+
+def put_blocks(refs, value, ordered):
+    rows = refs[0].shape[0]
+    if not ordered:
+        for k, ref in enumerate(refs):
+            ref[...] = value[k * rows : (k + 1) * rows]
+        return
+    per = value.shape[0] // rows
+    for e in range(per):
+        place = jnp.bitwise_xor(pl.program_id(1) * per + e, lax.axis_index("mp"))
+        for k, ref in enumerate(refs):
+
+            @pl.when(place == k)
+            def _(ref=ref, e=e):
+                ref[...] = value[e * rows : (e + 1) * rows]
+
+
+def attend_kernel(*refs, count, key_block, causal):
+    q_refs, (k_ref, v_ref, *o_refs, lse_ref) = refs[: -count - 3], refs[-count - 3 :]
+    q = q_refs[0][...] if causal else take_blocks(q_refs, 0, 0, False)
+    q = q * jnp.asarray(1.0 / math.sqrt(HD), LOW)
+    query_block = q.shape[0]
     query_begin = pl.program_id(1) * query_block
-    q = q_ref[...] * jnp.asarray(1.0 / math.sqrt(HD), LOW)
 
     def body(j, carry, diagonal):
         tops, sums, acc = carry[:2], carry[2:4], carry[4]
@@ -99,16 +131,18 @@
         body, start, query_block, key_block, k_ref.shape[0], causal
     )
     upper = lax.broadcasted_iota(jnp.int32, acc.shape, 0) < HD
-    o_ref[...] = (acc * jnp.where(upper, 1.0 / sum0, 1.0 / sum1)).T.astype(LOW)
+    put_blocks(o_refs, (acc * jnp.where(upper, 1.0 / sum0, 1.0 / sum1)).T.astype(LOW), causal)
     lse_ref[0] = jnp.concatenate(
         [top0 + jnp.log(sum0), top1 + jnp.log(sum1), jnp.zeros((6, query_block), WIDE)], axis=0
     )
 
 
-def attend_back_kernel(
-    q_ref, g_ref, o_ref, lse_ref, k_ref, v_ref, dq_ref, dk_ref, dv_ref, dk_acc, dv_acc, *, key_block, causal
-):
-    query_block = q_ref.shape[0]
+def attend_back_kernel(*refs, count, key_block, causal):
+    queries = 1 if causal else count
+    q_refs, refs = refs[:queries], refs[queries:]
+    g_refs, o_refs, refs = refs[:count], refs[count : 2 * count], refs[2 * count :]
+    lse_ref, k_ref, v_ref, *dq_refs, dk_ref, dv_ref, dk_acc, dv_acc = refs
+    rows, query_block = o_refs[0].shape[0], lse_ref.shape[2]
     query_begin = pl.program_id(1) * query_block
 
     @pl.when(pl.program_id(1) == 0)
@@ -116,15 +150,17 @@
         dk_acc[...] = jnp.zeros_like(dk_acc)
         dv_acc[...] = jnp.zeros_like(dv_acc)
 
-    q = q_ref[...] * jnp.asarray(1.0 / math.sqrt(HD), LOW)
-    g = g_ref[...]
+    q = q_refs[0][...] if causal else take_blocks(q_refs, 0, 0, False)
+    q = q * jnp.asarray(1.0 / math.sqrt(HD), LOW)
+    g = take_blocks(g_refs, rows, query_block, causal)
+    o = take_blocks(o_refs, rows, query_block, causal)
     q_heads = [keep_head(q, head) for head in (0, 1)]
     g_heads = [keep_head(g, head) for head in (0, 1)]
     picks = lax.broadcasted_iota(jnp.int32, (8, 2 * HD), 1) // HD
     picks = (picks == lax.broadcasted_iota(jnp.int32, (8, 2 * HD), 0)).astype(WIDE)
     inner = lax.dot_general(
         picks,
-        g.astype(WIDE) * o_ref[...].astype(WIDE),
+        g.astype(WIDE) * o.astype(WIDE),
         NT,
         precision=lax.Precision.HIGHEST,
         preferred_element_type=WIDE,
@@ -153,7 +189,11 @@
     dq = key_blocks(
         body, jnp.zeros((2 * HD, query_block), WIDE), query_block, key_block, k_ref.shape[0], causal
     )
-    dq_ref[...] = (dq * (1.0 / math.sqrt(HD))).T.astype(LOW)
+    dq = (dq * (1.0 / math.sqrt(HD))).T.astype(LOW)
+    if causal:
+        dq_refs[0][...] = dq
+    else:
+        put_blocks(dq_refs, dq, False)
 
     @pl.when(pl.program_id(1) == pl.num_programs(1) - 1)
     def _():
@@ -167,53 +207,57 @@
     return pl.BlockSpec((rows, 2 * HD), lambda p, i: (i, first + p))
 
 
-def attend(width, queries, keys, values, causal, query_block, key_block):
-    seq, span = queries[0].shape[0], keys[0].shape[0]
-    pairs = width // (2 * HD)
-    return pl.pallas_call(
-        functools.partial(attend_kernel, key_block=key_block, causal=causal),
+def attend(width, queries, keys, values, count, causal, query_block, key_block):
+    span = keys[0].shape[0]
+    if causal:
+        seq, operands = queries[0].shape[0], [queries[0]]
+        specs = [columns_of(query_block, queries[1], False)]
+    else:
+        seq, operands = queries[0].shape[0] * count, list(queries)
+        specs = [columns_of(seq // count, 0, True)] * count
+    rows, pairs = seq // count, width // (2 * HD)
+    *blocks, lse = pl.pallas_call(
+        functools.partial(attend_kernel, count=count, key_block=key_block, causal=causal),
         grid=(pairs, seq // query_block),
-        in_specs=[
-            columns_of(query_block, queries[1], False),
-            columns_of(span, keys[1], True),
-            columns_of(span, values[1], True),
-        ],
-        out_specs=[
-            columns_of(query_block, 0, False),
-            pl.BlockSpec((1, 8, query_block), lambda p, i: (p, 0, i)),
-        ],
-        out_shape=[
-            jax.ShapeDtypeStruct((seq, width), LOW),
-            jax.ShapeDtypeStruct((pairs, 8, seq), WIDE),
-        ],
+        in_specs=specs + [columns_of(span, keys[1], True), columns_of(span, values[1], True)],
+        out_specs=[columns_of(rows, 0, True)] * count
+        + [pl.BlockSpec((1, 8, query_block), lambda p, i: (p, 0, i))],
+        out_shape=[jax.ShapeDtypeStruct((rows, width), LOW)] * count
+        + [jax.ShapeDtypeStruct((pairs, 8, seq), WIDE)],
         compiler_params=pltpu.CompilerParams(vmem_limit_bytes=VMEM_LIMIT),
         cost_estimate=pl.CostEstimate(
             flops=8 * seq * span * width, bytes_accessed=8 * seq * width, transcendentals=0
         ),
         name="attend",
-    )(queries[0], keys[0], values[0])
-
-
-def attend_back(width, queries, keys, values, grad, result, lse, causal, query_block, key_block):
-    seq, span = queries[0].shape[0], keys[0].shape[0]
-    pairs = width // (2 * HD)
+    )(*operands, keys[0], values[0])
+    return blocks, lse
+
+
+def attend_back(width, queries, keys, values, grads, results, lse, causal, query_block, key_block):
+    span, seq, count = keys[0].shape[0], lse.shape[2], len(grads)
+    rows, pairs = seq // count, width // (2 * HD)
     whole = columns_of(span, 0, True)
-    return pl.pallas_call(
-        functools.partial(attend_back_kernel, key_block=key_block, causal=causal),
+    blocks = [columns_of(rows, 0, True)] * count
+    if causal:
+        operands, specs = [queries[0]], [columns_of(query_block, queries[1], False)]
+        out_specs, out_shape = [columns_of(query_block, 0, False)], [(seq, width)]
+    else:
+        operands, specs = list(queries), blocks
+        out_specs, out_shape = blocks, [(rows, width)] * count
+    *dq, dk, dv = pl.pallas_call(
+        functools.partial(attend_back_kernel, count=count, key_block=key_block, causal=causal),
         grid=(pairs, seq // query_block),
-        in_specs=[
-            columns_of(query_block, queries[1], False),
-            columns_of(query_block, 0, False),
-            columns_of(query_block, 0, False),
+        in_specs=specs
+        + [columns_of(grad.shape[0], 0, True) for grad in grads]
+        + blocks
+        + [
             pl.BlockSpec((1, 8, query_block), lambda p, i: (p, 0, i)),
             columns_of(span, keys[1], True),
             columns_of(span, values[1], True),
         ],
-        out_specs=[columns_of(query_block, 0, False), whole, whole],
+        out_specs=out_specs + [whole, whole],
         out_shape=[
-            jax.ShapeDtypeStruct((seq, width), LOW),
-            jax.ShapeDtypeStruct((span, width), LOW),
-            jax.ShapeDtypeStruct((span, width), LOW),
+            jax.ShapeDtypeStruct(shape, LOW) for shape in out_shape + [(span, width)] * 2
         ],
         scratch_shapes=[pltpu.VMEM((span, 2 * HD), WIDE), pltpu.VMEM((span, 2 * HD), WIDE)],
         compiler_params=pltpu.CompilerParams(vmem_limit_bytes=VMEM_LIMIT),
@@ -221,7 +265,8 @@
             flops=16 * seq * span * width, bytes_accessed=16 * seq * width, transcendentals=0
         ),
         name="attend_back",
-    )(queries[0], grad, result, lse, keys[0], values[0])
+    )(*operands, *grads, *results, lse, keys[0], values[0])
+    return (dq[0] if causal else dq), dk, dv
 
 
 def normalized(value):
@@ -260,14 +305,21 @@
     return copies
 
 
-def attention_copies(own, parts, weights, sems, width):
-    count = weights.shape[0]
+def attention_copies(own, parts, weights, sems, begin):
+    count, width = weights.shape[0], own[0].shape[1]
     copies = [
-        pltpu.make_async_copy(own[0], weights.at[0, :, :width], sems.at[CELLS]),
-        pltpu.make_async_copy(own[1], weights.at[0, :, width:], sems.at[CELLS + 1]),
+        pltpu.make_async_copy(
+            ref, weights.at[0, :, i * width : (i + 1) * width], sems.at[CELLS + i]
+        )
+        for i, ref in enumerate(own)
     ]
+    columns = slice(begin, begin + width * len(own))
     return copies + cell_copies(
-        parts, 2, weights, sems, lambda part, to, at: (part, to.at[pl.ds(1, count - 1), at, :])
+        parts,
+        2,
+        weights,
+        sems,
+        lambda part, to, at: (part.at[:, :, columns], to.at[pl.ds(1, count - 1), at, :]),
     )
 
 
@@ -288,7 +340,7 @@
     own, parts, refs = refs[:2], refs[2:6], refs[6:]
     n_ref, scale_ref, low_ref = refs[:3]
     queries, (weights, sems) = refs[3 : 3 + count], refs[3 + count :]
-    copies = attention_copies(own, parts, weights, sems, width)
+    copies = attention_copies(own, parts, weights, sems, 0)
     start_all(copies)
     value = alpha_scale * tokens_ref[...].astype(WIDE)
     wait_all(copies)
@@ -303,32 +355,47 @@
         queries[k][...] = mm(low, weights[k, :, width:], NN).astype(LOW)
 
 
+def term_rows(terms, width):
+    rows = [
+        terms[t : t + 1, at : at + width]
+        for t in range(terms.shape[0])
+        for at in range(0, terms.shape[1], width)
+    ]
+    rows = jnp.concatenate(rows, axis=0)
+    upper = rows.astype(LOW)
+    return jnp.concatenate([upper, (rows - upper.astype(WIDE)).astype(LOW)], axis=0)
+
+
 def leave_cross_kernel(
-    cross_grad_ref, gain_ref, n_ref, scale_ref, *refs, width, count
+    cross_grad_ref, gain_ref, n_ref, scale_ref, later_ref, *refs, width, count
 ):
     queries, refs = refs[:count], refs[count:]
     own, parts, refs = refs[:2], refs[2:6], refs[6:]
-    self_grad_ref, low_ref, terms_ref = refs[:3]
-    grads, (weights, sems) = refs[3 : 3 + count], refs[3 + count :]
-    copies = attention_copies(own, parts, weights, sems, width)
+    self_grad_ref, low_ref = refs[:2]
+    grads, (weights, sems) = refs[2 : 2 + count], refs[2 + count :]
+    copies = attention_copies(own, parts, weights, sems, 0)
     start_all(copies)
     grad = alpha_scale * cross_grad_ref[...]
     wait_all(copies)
     for k in range(count):
         grad = grad + mm(queries[k][...], weights[k, :, width:], NT)
-    self_grad, terms_ref[...] = norm_back(grad, gain_ref[0:1, :], n_ref[...], scale_ref[:, :1])
+    self_grad, terms = norm_back(grad, gain_ref[0:1, :], n_ref[...], scale_ref[:, :1])
+    terms = term_rows(jnp.concatenate([terms, later_ref[...]], axis=0), width)
+    rows = low_ref.shape[0]
     self_grad_ref[...] = self_grad
     low = self_grad.astype(LOW)
     low_ref[...] = low
     for k in range(count):
-        grads[k][...] = mm(low, weights[k, :, :width], NN).astype(LOW)
+        grads[k][:rows, :] = mm(low, weights[k, :, :width], NN).astype(LOW)
+        grads[k][rows:, :] = terms
 
 
 def feed_forward_kernel(
     first_n_ref, cotangent_ref, gain_ref, bias_ref, *refs, width, count
 ):
     attended, refs = refs[:count], refs[count:]
-    own, in_parts, out_parts, refs = refs[:3], refs[3:7], refs[7:11], refs[11:]
+    own, attn_parts, in_parts, out_parts = refs[:3], refs[3:7], refs[7:11], refs[11:15]
+    refs = refs[15:]
     mixed_ref, second_low_ref, third_low_ref, cross_grad_ref, cross_low_ref, terms_ref = refs[:6]
     act_ref, hidden_grad_ref = refs[6:8]
     grads, refs = refs[8 : 8 + count], refs[8 + count :]
@@ -336,14 +403,7 @@
     hidden = w_in.shape[2]
     chunk = min(512, hidden)
 
-    cross_copies = [pltpu.make_async_copy(own[2], w_cross.at[0], cross_sems.at[CELLS])]
-    cross_copies += cell_copies(
-        out_parts,
-        4,
-        w_cross,
-        cross_sems,
-        lambda part, to, at: (part.at[:, :, hidden:], to.at[pl.ds(1, count - 1), at, :]),
-    )
+    cross_copies = attention_copies(own[2:], attn_parts, w_cross, cross_sems, 2 * width)
     start_all(cross_copies)
     in_copies = [[pltpu.make_async_copy(own[0], w_in.at[0], in_sems.at[0, 0])]]
     out_copies = [[pltpu.make_async_copy(own[1], w_out.at[0], out_sems.at[0, 0])]]
@@ -363,7 +423,7 @@
                 4,
                 w_out,
                 out_sems.at[k],
-                lambda part, to, at: (part.at[k - 1, :, :hidden], to.at[k, at, :]),
+                lambda part, to, at: (part.at[k - 1], to.at[k, at, :]),
             )
         )
     for copies in zip(in_copies, out_copies):
@@ -452,6 +512,31 @@
     )
 
 
+def back_terms_kernel(*refs, count):
+    parts, (weight_ref, term_ref, joined_ref) = refs[:count], refs[count:]
+    for i, part in enumerate(parts):
+        joined_ref[:, i * part.shape[1] : (i + 1) * part.shape[1]] = part[...]
+    chunk = term_ref.shape[0] // 4
+
+    @pl.loop(0, 4)
+    def _(i):
+        at = pl.ds(pl.multiple_of(i * chunk, chunk), chunk)
+        term_ref[at, :] = mm(joined_ref[at, :], weight_ref[...], NT).astype(LOW)
+
+
+def back_terms(parts, weight):
+    rows, model = parts[0].shape[0], weight.shape[0]
+    return call(
+        functools.partial(back_terms_kernel, count=len(parts)),
+        [*parts, weight],
+        [],
+        [((rows, model), LOW), ((rows, weight.shape[1]), LOW)],
+        [],
+        2 * rows * model * weight.shape[1],
+        "back_terms",
+    )
+
+
 def enter_cross(tokens, gain, bias, attended, own, parts):
     rows, model = tokens.shape
     count, width = len(attended), attended[0].shape[1]
@@ -470,15 +555,15 @@
     )
 
 
-def leave_cross(cross_grad, gain, n, scale, queries, own, parts):
+def leave_cross(cross_grad, gain, n, scale, later_terms, queries, own, parts):
     rows, model = n.shape
     count, width = len(queries), queries[0].shape[1]
     return call(
         functools.partial(leave_cross_kernel, width=width, count=count),
-        [cross_grad, gain, n, scale, *queries],
+        [cross_grad, gain, n, scale, later_terms, *queries],
         [*own, *parts],
-        [((rows, model), WIDE), ((rows, model), LOW), ((2, model), WIDE)]
-        + [((rows, width), LOW)] * count,
+        [((rows, model), WIDE), ((rows, model), LOW)]
+        + [((rows + 2 * (2 + later_terms.shape[0]) * model // width, width), LOW)] * count,
         [
             pltpu.VMEM((count, model, 2 * width), LOW),
             pltpu.SemaphoreType.DMA((CELLS + 2,)),
@@ -488,7 +573,7 @@
     )
 
 
-def feed_forward(first_n, cotangent, gain, bias, attended, own, in_parts, out_parts):
+def feed_forward(first_n, cotangent, gain, bias, attended, own, attn_parts, in_parts, out_parts):
     rows, model = first_n.shape
     count, width = len(attended), attended[0].shape[1]
     hidden = own[0].shape[1]
@@ -496,7 +581,7 @@
     return call(
         functools.partial(feed_forward_kernel, width=width, count=count),
         [first_n, cotangent, gain, bias, *attended],
-        [*own, *in_parts, *out_parts],
+        [*own, *attn_parts, *in_parts, *out_parts],
         [
             ((rows, model), LOW),
             ((rows, model), LOW),
@@ -528,8 +613,12 @@
     return keep, [c for c in range(CELLS // 2) if (2 * c) & bit]
 
 
-def weight_grads_kernel(*refs, count, other_core, bit):
-    lefts, rights, refs = refs[:count], refs[count : 2 * count], refs[2 * count :]
+def weight_grads_kernel(*refs, count, sizes, begin, other_core, bit):
+    lefts, rights, refs = refs[:count], [], refs[count:]
+    for size in sizes:
+        rights.append(refs[:size])
+        refs = refs[size:]
+    place = jnp.bitwise_xor(pl.program_id(0) + begin, lax.axis_index("mp"))
     turned = refs[-1]
     block = turned.shape[1] // (CELLS // 2)
 
@@ -544,9 +633,17 @@
 
     at = 0
     for i, right in enumerate(rights):
-        cut = slice(at, at + right.shape[2])
-        at += right.shape[2]
-        value = mm(turned[i], right[0], NN).reshape(CELLS // 2, block, right.shape[2])
+        wide = right[0].shape[-1]
+        cut = slice(at, at + wide)
+        at += wide
+        if len(right) == 1:
+            operand = right[0][0]
+        else:
+            operand = right[0][...].astype(WIDE)
+            for k in range(1, len(right)):
+                operand = jnp.where(place == k, right[k][...].astype(WIDE), operand)
+            operand = operand.astype(LOW)
+        value = mm(turned[i], operand, NN).reshape(CELLS // 2, block, wide)
         if bit is None:
             refs[0][:, 0, :, cut] = value.astype(LOW)
             continue
@@ -559,7 +656,8 @@
 def weight_grads(lefts, rights, shards, other_core, got=None, bit=None):
     rows, model = lefts[0].shape
     count, block, cells = len(shards), model // CELLS, CELLS // 2
-    width = sum(right.shape[2] for right in rights)
+    rights = [right if isinstance(right, (list, tuple)) else [right] for right in rights]
+    width = sum(right[0].shape[-1] for right in rights)
 
     def right_at(s, mp):
         return jnp.bitwise_xor(s + shards[0], mp[0]), 0, 0
@@ -572,15 +670,26 @@
 
     halves = got is not None
     kernel = functools.partial(
-        weight_grads_kernel, count=len(lefts), other_core=other_core, bit=bit
-    )
+        weight_grads_kernel,
+        count=len(lefts),
+        sizes=[len(right) for right in rights],
+        begin=shards[0],
+        other_core=other_core,
+        bit=bit,
+    )
+    right_specs = []
+    for right in rights:
+        if len(right) == 1:
+            right_specs.append(pl.BlockSpec((1, rows, right[0].shape[2]), right_at))
+        else:
+            right_specs += [pl.BlockSpec(v.shape, lambda s, mp: (0, 0)) for v in right]
     return pl.pallas_call(
         lambda mp, *refs: kernel(*refs),
         grid_spec=pltpu.PrefetchScalarGridSpec(
             num_scalar_prefetch=1,
             grid=(count,),
             in_specs=[pl.BlockSpec((rows, model), lambda s, mp: (0, 0))] * len(lefts)
-            + [pl.BlockSpec((1, rows, right.shape[2]), right_at) for right in rights]
+            + right_specs
             + [whole(cells)] * halves,
             out_specs=[whole(cells // 2)] * 2 if halves else whole(cells),
             scratch_shapes=[pltpu.VMEM((len(lefts), model // 2, rows), LOW)],
@@ -596,7 +705,7 @@
     )(
         lax.axis_index("mp").astype(jnp.int32).reshape(1),
         *lefts,
-        *rights,
+        *(v for right in rights for v in right),
         *([got] if halves else []),
     )
 
@@ -643,22 +752,6 @@
     def swap_mp(self, blocks):
         return [b if k == 0 else self.flip_mp(b, k) for k, b in enumerate(blocks)]
 
-    def rows_for(self, value):
-        rows = value.shape[0] // self.mp
-        me = lax.axis_index("mp")
-        return [
-            lax.dynamic_slice_in_dim(value, jnp.bitwise_xor(me, k) * rows, rows, 0)
-            for k in range(self.mp)
-        ]
-
-    def in_order(self, blocks):
-        rows = blocks[0].shape[0]
-        me = lax.axis_index("mp")
-        out = jnp.zeros((rows * self.mp,) + blocks[0].shape[1:], blocks[0].dtype)
-        for k, b in enumerate(blocks):
-            out = lax.dynamic_update_slice_in_dim(out, b, jnp.bitwise_xor(me, k) * rows, 0)
-        return out
-
     def piece(self, slab):
         rows = slab.shape[0] // CELLS
         return lax.dynamic_slice_in_dim(slab, self.cell() * rows, rows, 0)
@@ -690,13 +783,6 @@
             axis_index_groups=[[g * CELLS + c for g in range(groups)] for c in range(CELLS)],
         )
         return self.permute(mine, lambda d, m: ((d % CELLS) * groups + d // CELLS, m))
-
-    def sum_dp(self, value):
-        step = 1
-        while step < self.dp:
-            value = value + self.flip(value, step)
-            step *= 2
-        return value
 
 
 def local(
@@ -728,38 +814,38 @@
     order = [jnp.bitwise_xor(lax.axis_index("mp"), k) for k in range(n)]
 
     full_tokens = lax.all_gather(tokens, "mp", axis=0, tiled=True)
-    pieces = [layout.piece(v) for v in (self_out, cross_q, ffn_in, ffn_out, cross_out)]
-    attn_here = jnp.stack(layout.swap_mp([jnp.concatenate(pieces[:2], axis=1)] * n)[1:])
+    pieces = [layout.piece(v) for v in (self_out, cross_q, cross_out, ffn_in, ffn_out)]
+    attn_here = jnp.stack(layout.swap_mp([jnp.concatenate(pieces[:3], axis=1)] * n)[1:])
     attn_here = layout.near(attn_here, 2)
     attn_there = layout.flip(attn_here, 4)
-    attn_parts = [attn_here, attn_there, layout.flip(attn_here, 1), layout.flip(attn_there, 1)]
-    full_tokens, *attn_parts = after([full_tokens, *attn_parts])
-    (ffn_piece,) = after([jnp.concatenate(pieces[2:], axis=1)], full_tokens)
+    (full_tokens,) = after([full_tokens], attn_here, qkv_flat, kv_flat)
+    (ffn_piece,) = after([jnp.concatenate(pieces[3:], axis=1)], full_tokens)
     ffn_all = lax.all_gather(ffn_piece, "mp", axis=0, tiled=False)
     projected = dense(full_tokens, qkv_flat).astype(LOW)
     pairs = w // (2 * HD)
     self_operands = (projected, 0), (projected, pairs), (projected, 2 * pairs)
-    home_attended, self_logs = attend(w, *self_operands, True, *SELF_BLOCKS)
-    attended_blocks = layout.swap_mp(layout.rows_for(home_attended))
+    home_attended, self_logs = attend(w, *self_operands, n, True, *SELF_BLOCKS)
+    *home_attended, attn_there = after([*home_attended, attn_there])
+    attn_parts = [attn_here, attn_there, layout.flip(attn_here, 1), layout.flip(attn_there, 1)]
+    attended_blocks = layout.swap_mp(home_attended)
     first_n, first_scale, first_low, *query_blocks = enter_cross(
         tokens, ln_gain, ln_bias, attended_blocks, (self_out, cross_q), attn_parts
     )
-    query_blocks = layout.swap_mp(query_blocks)
-    memory_there, ffn_all = after([memory, ffn_all], *query_blocks[1:])
+    memory_there, ffn_all = after([memory, ffn_all], *query_blocks)
     full_memory = lax.all_gather(memory_there, "mp", axis=0, tiled=True)
     ffn_here = jnp.concatenate([lax.dynamic_slice_in_dim(ffn_all, k, 1, 0) for k in order[1:]])
     in_here = layout.near(ffn_here[:, :, :n_hidden], 2)
     out_here = layout.near(ffn_here[:, :, n_hidden:], 4)
     in_there, out_there = layout.flip(in_here, 4), layout.flip(out_here, 2)
     here_others = [layout.flip(in_here, 1), layout.flip(out_here, 1)]
-    (cross_queries,) = after([jnp.concatenate(query_blocks)], *here_others)
+    query_blocks = layout.swap_mp(after(query_blocks, *here_others))
     cross_pair = dense(full_memory, kv_flat).astype(LOW)
-    cross_operands = (cross_queries, 0), (cross_pair, 0), (cross_pair, pairs)
-    home_cross, cross_logs = attend(w, *cross_operands, False, *CROSS_BLOCKS)
-    in_there, out_there = after([in_there, out_there], home_cross)
+    cross_operands = query_blocks, (cross_pair, 0), (cross_pair, pairs)
+    home_cross, cross_logs = attend(w, *cross_operands, n, False, *CROSS_BLOCKS)
+    in_there, out_there = after([in_there, out_there], home_cross[0])
     in_parts = [in_here, in_there, here_others[0], layout.flip(in_there, 1)]
     out_parts = [out_here, out_there, here_others[1], layout.flip(out_there, 1)]
-    cross_blocks = layout.swap_mp(list(home_cross.reshape(n, rows, w)))
+    cross_blocks = layout.swap_mp(home_cross)
     (
         mixed,
         second_low,
@@ -777,11 +863,11 @@
         ln_bias,
         cross_blocks,
         (ffn_in, ffn_out, cross_out),
+        attn_parts,
         in_parts,
         out_parts,
     )
     cross_grad_blocks = layout.swap_mp(cross_grad_blocks)
-    cross_attended = jnp.stack(cross_blocks)
 
     def send(pair, bit):
         return pair[0], layout.flip(pair[1], bit)
@@ -795,84 +881,108 @@
     ffn_grads = functools.partial(
         weight_grads,
         lefts,
-        [hidden_grad, activation, cross_attended],
+        [hidden_grad, activation, cross_blocks],
     )
     cuts = (range(0, half), range(half, n))
     ffn_there = [ffn_grads(cut, 1) for cut in cuts]
     ffn_got = [layout.flip(part, 1) for part in ffn_there]
-    (cross_attended_grad,) = after([jnp.concatenate(cross_grad_blocks)], *ffn_there)
+    cross_grad_blocks[1:] = after(cross_grad_blocks[1:], *ffn_there)
     cross_queries_grad, cross_keys_grad, cross_values_grad = attend_back(
-        w, *cross_operands, cross_attended_grad, home_cross, cross_logs, False, *CROSS_BACK_BLOCKS
-    )
-    first_terms = layout.swap_mp(list(cross_queries_grad.reshape(n, rows, w)))
-    cross_pair_grad = jnp.concatenate([cross_keys_grad, cross_values_grad], axis=-1)
-    memory_term = back_dense(cross_pair_grad, kv_flat).astype(LOW)
+        w, *cross_operands, cross_grad_blocks, home_cross, cross_logs, False, *CROSS_BACK_BLOCKS
+    )
+    first_terms = layout.swap_mp(cross_queries_grad)
+    memory_term, cross_pair_grad = back_terms([cross_keys_grad, cross_values_grad], kv_flat)
     memory_grad = lax.psum_scatter(memory_term, "mp", scatter_dimension=0, tiled=True)
+    ffn_got = after(ffn_got, *first_terms[2:])
     ffn_sums = [ffn_grads(cut, 0, got, bit) for cut, got, bit in zip(cuts, ffn_got, BITS)]
     first_terms[1:] = after(first_terms[1:], memory_term, ffn_sums[0][1], ffn_sums[1][1])
     ffn_sums = [send(pair, bit) for pair, bit in zip(ffn_sums, BITS)]
-    self_grad, self_grad_low, first_norm_terms, *attended_grad_blocks = leave_cross(
-        cross_grad, ln_gain, first_n, first_scale, first_terms, (self_out, cross_q), attn_parts
-    )
-    norm_terms = jnp.concatenate([first_norm_terms, later_terms])
-    upper = norm_terms.astype(LOW)
-    lower = (norm_terms - upper.astype(WIDE)).astype(LOW)
-    norm_rows = jnp.concatenate([upper.reshape(-1, w), lower.reshape(-1, w)])
-    blocks = layout.swap_mp(
-        [jnp.concatenate([block, norm_rows]) for block in attended_grad_blocks]
-    )
-    attended_grad = layout.in_order([block[:rows] for block in blocks])
+    self_grad, self_grad_low, *attended_grad_blocks = leave_cross(
+        cross_grad,
+        ln_gain,
+        first_n,
+        first_scale,
+        later_terms,
+        first_terms,
+        (self_out, cross_q),
+        attn_parts,
+    )
+    blocks = layout.swap_mp(attended_grad_blocks)
     norm_terms = sum(block[rows:].astype(WIDE) for block in blocks)
     norm_terms = norm_terms.reshape(2, -1, model_width).sum(axis=0)
-    (attended_grad,) = after([attended_grad], memory_grad)
+
+    def send_with_terms(there, terms, bit):
+        upper = terms.astype(LOW)
+        both = jnp.concatenate([upper, (terms - upper.astype(WIDE)).astype(LOW)])
+        width = there.shape[-1]
+        both = jnp.pad(both, ((0, 16 - both.shape[0]), (0, width - both.shape[1])))
+        got = layout.flip(jnp.concatenate([there.reshape(-1, width), both]), bit)
+        count = terms.shape[0]
+        more = got[-16:, : terms.shape[1]].astype(WIDE)
+        terms = terms + more[:count] + more[count : 2 * count]
+        return got[:-16].reshape(there.shape), terms
+
+    blocks[1:] = after(blocks[1:], memory_grad)
     queries_grad, keys_grad, values_grad = attend_back(
-        w, *self_operands, attended_grad, home_attended, self_logs, True, *SELF_BACK_BLOCKS
-    )
-    projected_grad = jnp.concatenate([queries_grad, keys_grad, values_grad], axis=-1)
-    token_term = back_dense(projected_grad, qkv_flat).astype(LOW)
-    (token_term,) = after([token_term], *(got for _, got in ffn_sums))
+        w, *self_operands, blocks, home_attended, self_logs, True, *SELF_BACK_BLOCKS
+    )
+    token_term, projected_grad = back_terms([queries_grad, keys_grad, values_grad], qkv_flat)
+    chip_got = [got for _, got in ffn_sums]
     token_part = lax.psum_scatter(token_term, "mp", scatter_dimension=0, tiled=True)
     token_grad = (alpha_scale * self_grad + token_part.astype(WIDE)).astype(LOW)
-    (self_grad_low,) = after([self_grad_low], token_term)
+    (self_grad_low,) = after([self_grad_low], token_term, *chip_got)
     attn_grads = functools.partial(
         weight_grads,
         [self_grad_low, first_low],
-        [jnp.stack(attended_blocks), jnp.stack(first_terms)],
+        [attended_blocks, first_terms],
         range(n),
     )
     ffn_sums = [fold_halves(pair) for pair in ffn_sums]
     ffn_sums = [send(pair, 6 - bit) for pair, bit in zip(ffn_sums, BITS)]
     attn_got = layout.flip(attn_grads(1), 1)
+    attn_sum = attn_grads(0, attn_got, 2)
+    cross_pair_grad, projected_grad, full_memory = after(
+        [cross_pair_grad, projected_grad, full_memory], attn_sum[1]
+    )
     home_grads = [
         jnp.concatenate(
             [weight_grad(a, cross_pair_grad), weight_grad(b, projected_grad)], axis=1
         ).reshape(CELLS // 2, 1, model_width // CELLS, -1)
         for a, b in zip(layout.core_halves(full_memory), layout.core_halves(full_tokens))
     ]
-    home_sum = home_grads[0], layout.flip(home_grads[1], 1)
-    attn_sum = send(attn_grads(0, attn_got, 2), 2)
-    home_sum = send(fold_halves(home_sum), 4)
-    attn_sum = send(fold_halves(attn_sum), 4)
-    home_sum = send(fold_halves(home_sum), 2)
+    home_got, norm_terms = send_with_terms(home_grads[1], norm_terms, 1)
+    ffn_got = after([got for _, got in ffn_sums], attn_sum[1], *home_grads)
+    ffn_sums = [(here, got) for (here, _), got in zip(ffn_sums, ffn_got)]
+    attn_sum = send(attn_sum, 2)
+    home_here, home_there = fold_halves((home_grads[0], home_got))
+    home_got, norm_terms = send_with_terms(home_there, norm_terms, 4)
+    home_here, home_there = fold_halves((home_here, home_got))
+    home_got, sums = send_with_terms(home_there, norm_terms, 2)
+    attn_here, attn_there = fold_halves(attn_sum)
+    (attn_there,) = after([attn_there], home_got)
+    attn_sum = send((attn_here, attn_there), 4)
+    home_sum = home_here, home_got
     ffn_sums = jnp.concatenate([layout.fold(*pair)[0] for pair in ffn_sums])
     ffn_shard = lax.psum_scatter(ffn_sums, "mp", scatter_dimension=0, tiled=True)
-    ffn_shard = layout.to_rows(ffn_shard)[0].astype(WIDE)
+    home_grad = layout.to_rows(layout.fold(*home_sum)[0])[0].astype(WIDE)
+    kv_grad = home_grad[:, : 2 * w].reshape(-1, 2, w)
+    qkv_grad = home_grad[:, 2 * w :].reshape(-1, 3, w)
     attn_sum = layout.to_rows(layout.fold(*attn_sum)[0])
     attn_sum = [lax.dynamic_index_in_dim(attn_sum, k, 0, keepdims=False) for k in order]
-    attn_shard = sum(term.astype(WIDE) for term in layout.swap_mp(attn_sum))
-    home_grad = layout.to_rows(layout.fold(*home_sum)[0])[0].astype(WIDE)
-    (norm_terms,) = after([norm_terms], ffn_sums)
-    sums = layout.sum_dp(norm_terms)
+    attn_sum = layout.swap_mp(attn_sum)
+    attn_shard = sum(term.astype(WIDE) for term in attn_sum)
+    (ffn_shard,) = after([ffn_shard], attn_shard, token_grad, kv_grad, qkv_grad, sums)
+    ffn_shard = layout.to_rows(ffn_shard)[0].astype(WIDE)
     edges = (n_hidden, 2 * n_hidden)
     ffn_in_grad, ffn_out_grad, cross_out_grad = jnp.split(ffn_shard, edges, axis=1)
     return (
         mixed[:, None],
         token_grad[:, None],
         memory_grad[:, None],
-        home_grad[:, 2 * w :].reshape(-1, 3, w),
+        qkv_grad,
         attn_shard[:, :w],
         attn_shard[:, w:],
-        home_grad[:, : 2 * w].reshape(-1, 2, w),
+        kv_grad,
         cross_out_grad,
         ffn_in_grad,
         ffn_out_grad,

time: 508 us -> 498 us (0.980)
  Pallas kernels: 111 us -> 123 us
  starting transfers between devices: 78.8 us -> 71.5 us
  matrix products: 20.4 us -> 13.5 us
    ppermute x51 -> x48, waiting for transfers between devices: 181 us -> 152 us  [permute(): return lax.ppermute(value, ('dp', 'mp'), pairs)]
    all_gather x1, waiting for transfers between devices: 1.41 us -> 17.1 us  [local(): full_tokens = lax.all_gather(tokens, 'mp', axis=0, tiled=True)]
    pallas_call x3 -> x5, Pallas kernels: 33.1 us -> 43.7 us  [call(): pl.pallas_call(kernel, in_specs=[here] * len(operands) + [there] * len(st...]
    all_gather x1, waiting for transfers between devices: 12 us -> 22.3 us  [local(): full_memory = lax.all_gather(memory_there, 'mp', axis=0, tiled=True)]
    ppermute x51 -> x48, starting transfers between devices: 77.8 us -> 70.8 us  [permute(): return lax.ppermute(value, ('dp', 'mp'), pairs)]
    dot_general x2 -> x0, matrix products: 5.85 us -> none  [back_dense(): return jnp.einsum('tf,df->td', grad, weight, preferred_element_type=WIDE)]
    unnamed x154 -> x130, local copies, waits for them, and re-layouts: 22 us -> 19.8 us
  transfers between devices with their start and end apart: 57 -> 54, of which waited for: 29 -> 27; matrix products, arithmetic and copies ran while one was open for 16% -> 14% of each run, Pallas kernels for 17% -> 20%
where the time goes in v3:
time: 498 us; the launch traced here: 491 us
  waiting for transfers between devices  194 us (39%)
  Pallas kernels  123 us (25%)
  starting transfers between devices  71.5 us (14%)
  local copies, waits for them, and re-layouts  43.9 us (9%)
  other arithmetic  29.8 us (6%)
  between operations  15.1 us (3%)
  matrix products  13.5 us (3%)
    ppermute x48, waiting for transfers between devices, permute(): return lax.ppermute(value, ('dp', 'mp'), pairs)  152 us
    ppermute x48, starting transfers between devices, permute(): return lax.ppermute(value, ('dp', 'mp'), pairs)  70.8 us
    pallas_call x5, Pallas kernels, call(): pl.pallas_call(kernel, in_specs=[here] * len(operands) + [there] * len(st...  43.7 us
    pallas_call x6, Pallas kernels, weight_grads(): pl.pallas_call(lambda mp, *refs: kernel(*refs), grid_spec=pltpu.PrefetchS...  33.1 us
    pallas_call x2, Pallas kernels, attend_back(): pl.pallas_call(functools.partial(attend_back_kernel, count=count, key_blo...  27.7 us
    all_gather x1, waiting for transfers between devices, local(): full_memory = lax.all_gather(memory_there, 'mp', axis=0, tiled=True)  22.3 us
    unnamed x130, local copies, waits for them, and re-layouts  19.8 us
    pallas_call x2, Pallas kernels, attend(): pl.pallas_call(functools.partial(attend_kernel, count=count, key_block=ke...  18.5 us
  transfers between devices with their start and end apart: 54, of which 27 were waited for; matrix products, arithmetic and copies ran while one was open for 14% of the time, Pallas kernels for 20%

profile of v3, /device:TPU:0, one launch (start us, length us, event | category | flops | bytes accessed | tf_op | source)
XLA Modules:
  0.0 490.8 jit_solution(2364434099284527965)
XLA Ops:
  16.6 5.7 %collective-permute-done = bf16[128,768]{1,0:T(8,128)(2,1)S(1)} collective-permute-done((bf16[128,768]{1,0:T(8,128)(2,1)S(1)}, bf16[128,768]{1,0:T(8,128)(2,1)S(1)}, u32[]{:S(2)}, u32[]{:S(2)}) %collective-permute-start) | collective-permute-done | bytes 196640 | tf_op jit(solution)/shard_map/ppermute | solution.py:741
  22.4 14.5 %collective-permute-done.1 = bf16[128,768]{1,0:T(8,128)(2,1)S(1)} collective-permute-done((bf16[128,768]{1,0:T(8,128)(2,1)S(1)}, bf16[128,768]{1,0:T(8,128)(2,1)S(1)}, u32[]{:S(2)}, u32[]{:S(2)}) %collective-permute-start.1) | collective-permute-done | bytes 196640 | tf_op jit(solution)/shard_map/ppermute | solution.py:741
  51.0 17.1 %all-gather.8.cloned.1.call-done = bf16[1024,1,1024]{2,0,1:T(8,128)(2,1)} async-done(((bf16[256,1,1024]{2,0,1:T(8,128)(2,1)}), bf16[1024,1,1024]{2,0,1:T(8,128)(2,1)}) %all-gather.8.cloned.1.call-update) | async-done | bytes 2097168 | tf_op jit(solution)/shard_map/all_gather | solution.py:816
  70.9 4.4 convolution_convert_fusion.refs_0_.refs_1_.refs_2_.refs_10_.refs_11_
  75.2 9.2 %attend.2 = (bf16[256,256]{1,0:T(8,128)(2,1)}, bf16[256,256]{1,0:T(8,128)(2,1)}, bf16[256,256]{1,0:T(8,128)(2,1)}, bf16[256,256]{1,0:T(8,128)(2,1)}, f32[2,8,1024]{2,1,0:T(8,128)}) custom-call(bf16[1024,768]{1,0:T(8,128)(2,1)} %convolution_convert_fusion.refs_0_.refs_1_.refs_2_.refs_10_.refs_11_, ...), custom_call_target="tpu_custom_call" | custom-call | flops 2147483648 | bytes 2097152 | tf_op jit(solution)/shard_map/attend/pallas_call | solution.py:219
  84.4 12.8 %collective-permute-done.4.refs_4_ = bf16[2,3,128,768]{3,2,1,0:T(8,128)(2,1)S(1)} collective-permute-done((bf16[2,3,128,768]{3,2,1,0:T(8,128)(2,1)S(1)}, bf16[2,3,128,768]{3,2,1,0:T(8,128)(2,1)S(1)}, u32[]{:S(2)}, u32[]{:S(2)}) %collective-permute-start.4) | collective-permute-done | bytes 1179680 | tf_op jit(solution)/shard_map/ppermute | solution.py:741
  102.7 10.8 %collective-permute-done.5.refs_1_.refs_3_ = bf16[256,256]{1,0:T(8,128)(2,1)S(1)} collective-permute-done((bf16[256,256]{1,0:T(8,128)(2,1)}, bf16[256,256]{1,0:T(8,128)(2,1)S(1)}, u32[]{:S(2)}, u32[]{:S(2)}) %collective-permute-start.5) | collective-permute-done | bytes 131104 | tf_op jit(solution)/shard_map/ppermute | solution.py:741
  119.4 5.9 %enter_cross.1 = (f32[256,1024]{1,0:T(8,128)}, f32[256,128]{1,0:T(8,128)}, bf16[256,1024]{1,0:T(8,128)(2,1)}, bf16[256,256]{1,0:T(8,128)(2,1)}, bf16[256,256]{1,...) custom-call(bf16[256,1024]{1,0:T(8,128)(2,1)} %bitcast.92, f32[3,1024]{1,0:T(4,128)} %gain_ref.5, ...), custom_call_target="tpu_custom_call" | custom-call | flops 1073741824 | bytes 6840320 | tf_op jit(solution)/shard_map/enter_cross/pallas_call | solution.py:479
  133.0 16.4 %collective-permute-done.12 = bf16[3,128,1024]{2,1,0:T(8,128)(2,1)S(1)} collective-permute-done((bf16[3,128,1024]{2,1,0:T(8,128)(2,1)S(1)}, bf16[3,128,1024]{2,1,0:T(8,128)(2,1)S(1)}, u32[]{:S(2)}, u32[]{:S(2)}) %collective-permute-start.12) | collective-permute-done | bytes 786464 | tf_op jit(solution)/shard_map/ppermute | solution.py:741
  156.7 5.7 %collective-permute-start.14 = (bf16[256,256]{1,0:T(8,128)(2,1)}, bf16[256,256]{1,0:T(8,128)(2,1)S(1)}, u32[]{:S(2)}, u32[]{:S(2)}) collective-permute-start(bf16[256,256]{1,0:T(8,128)(2,1)} %get-tuple-element.111), channel_id=1, source_target_pairs={{0,1},{1,0},{2,3},{3,2},{4,5},{5,4},{6,7},{7,6},{8,9},{9,8},{10,11... | collective-permute-start | bytes 393224 | tf_op jit(solution)/shard_map/ppermute | solution.py:741
  164.8 22.3 %all-gather.6.cloned.1.call-done.refs_2_ = bf16[1024,1024]{1,0:T(8,128)(2,1)} async-done(((bf16[256,1024]{1,0:T(8,128)(2,1)}), bf16[1024,1024]{1,0:T(8,128)(2,1)}) %all-gather.6.cloned.1.call-update) | async-done | bytes 2097168 | tf_op jit(solution)/shard_map/all_gather | solution.py:835
  187.1 3.8 convolution_convert_fusion.1.refs_4_.refs_5_.refs_13_.refs_14_
  191.6 9.3 %attend.3 = (bf16[256,256]{1,0:T(8,128)(2,1)}, bf16[256,256]{1,0:T(8,128)(2,1)}, bf16[256,256]{1,0:T(8,128)(2,1)}, bf16[256,256]{1,0:T(8,128)(2,1)}, f32[2,8,1024]{2,1,0:T(8,128)}) custom-call(bf16[256,256]{1,0:T(8,128)(2,1)} %get-tuple-element.110.refs_0_, bf16[256,256]{1,0:T(8,128)(2,1)} %copy-done.52, bf16[256,256]{1,0:T(8,128)(2,1)} %copy-done.53, ...), custom_call_target="tpu_custom_call" | custom-call | flops 2147483648 | bytes 2097152 | tf_op jit(solution)/shard_map/attend/pallas_call | solution.py:219
  209.0 5.8 %collective-permute-done.18.refs_2_.refs_7_ = bf16[256,256]{1,0:T(8,128)(2,1)S(1)} collective-permute-done((bf16[256,256]{1,0:T(8,128)(2,1)S(1)}, bf16[256,256]{1,0:T(8,128)(2,1)S(1)}, u32[]{:S(2)}, u32[]{:S(2)}) %collective-permute-start.18) | collective-permute-done | bytes 131104 | tf_op jit(solution)/shard_map/ppermute | solution.py:741
  216.7 20.5 %feed_forward.1 = (bf16[256,1024]{1,0:T(8,128)(2,1)}, bf16[256,1024]{1,0:T(8,128)(2,1)}, bf16[256,1024]{1,0:T(8,128)(2,1)}, f32[256,1024]{1,0:T(8,128)}, bf16[25...) custom-call(f32[256,1024]{1,0:T(8,128)} %get-tuple-element.104.first, ...), custom_call_target="tpu_custom_call" | custom-call | flops 8589934592 | bytes 24141824 | tf_op jit(solution)/shard_map/feed_forward/pallas_call | solution.py:479
  237.1 5.1 %weight_grads.7.refs_4_ = bf16[4,2,128,2304]{3,2,1,0:T(8,128)(2,1)} custom-call(s32[1]{0:T(128)} %bitcast.16.mp, bf16[256,1024]{1,0:T(8,128)(2,1)} %get-tuple-element.129.refs_0_, bf16[256,1024]{1,0:T(8,128)(2,1)} %get-tuple-element.130.refs_1_, bf16[256,1024]{1,0:T(8,128)(2,1)} %get-tuple-element.131.refs_2_, ...), custom_call_target="tpu_custom_call" | custom-call | flops 1207959552 | bytes 4718592 | tf_op jit(solution)/shard_map/weight_grads/pallas_call | solution.py:686
  242.4 5.2 %weight_grads.6.refs_3_ = bf16[4,2,128,2304]{3,2,1,0:T(8,128)(2,1)} custom-call(s32[1]{0:T(128)} %bitcast.16.mp, bf16[256,1024]{1,0:T(8,128)(2,1)} %get-tuple-element.129.refs_0_, bf16[256,1024]{1,0:T(8,128)(2,1)} %get-tuple-element.130.refs_1_, bf16[256,1024]{1,0:T(8,128)(2,1)} %get-tuple-element.131.refs_2_, ...), custom_call_target="tpu_custom_call" | custom-call | flops 1207959552 | bytes 4718592 | tf_op jit(solution)/shard_map/weight_grads/pallas_call | solution.py:686
  255.6 7.5 %collective-permute-done.25.refs_1_ = bf16[256,256]{1,0:T(8,128)(2,1)S(1)} collective-permute-done((bf16[256,256]{1,0:T(8,128)(2,1)S(1)}, bf16[256,256]{1,0:T(8,128)(2,1)S(1)}, u32[]{:S(2)}, u32[]{:S(2)}) %collective-permute-start.25) | collective-permute-done | bytes 131104 | tf_op jit(solution)/shard_map/ppermute | solution.py:741
  264.4 13.7 %attend_back.2 = (bf16[256,256]{1,0:T(8,128)(2,1)}, bf16[256,256]{1,0:T(8,128)(2,1)}, bf16[256,256]{1,0:T(8,128)(2,1)}, bf16[256,256]{1,0:T(8,128)(2,1)}, bf16[1...) custom-call(bf16[256,256]{1,0:T(8,128)(2,1)} %get-tuple-element.110.refs_0_, bf16[256,256]{1,0:T(8,128)(2,1)} %copy-done.52, ...), custom_call_target="tpu_custom_call" | custom-call | flops 4294967296 | bytes 4194304 | tf_op jit(solution)/shard_map/attend_back/pallas_call | solution.py:247
  278.2 4.9 back_terms.2
  287.2 16.2 %collective-permute-done.28.refs_2_.refs_1_ = bf16[256,256]{1,0:T(8,128)(2,1)S(1)} collective-permute-done((bf16[256,256]{1,0:T(8,128)(2,1)S(1)}, bf16[256,256]{1,0:T(8,128)(2,1)S(1)}, u32[]{:S(2)}, u32[]{:S(2)}) %collective-permute-start.28) | collective-permute-done | bytes 131104 | tf_op jit(solution)/shard_map/ppermute | solution.py:741
  304.1 6.4 %weight_grads.9 = (bf16[2,2,128,2304]{3,2,1,0:T(8,128)(2,1)}, bf16[2,2,128,2304]{3,2,1,0:T(8,128)(2,1)}) custom-call(s32[1]{0:T(128)} %bitcast.16.mp, bf16[256,1024]{1,0:T(8,128)(2,1)} %get-tuple-element.129.refs_0_, bf16[256,1024]{1,0:T(8,128)(2,1)} %get-tuple-element.130.refs_1_, bf16[256,1024]{1,0:T(8,128)(2,1)} %get-tuple-element.131.refs_2_, ...), custom_call_target="tpu_custom_call" | custom-call | flops 1207959552 | bytes 4718592 | tf_op jit(solution)/shard_map/weight_grads/pallas_call | solution.py:686
  311.9 6.0 %weight_grads.8 = (bf16[2,2,128,2304]{3,2,1,0:T(8,128)(2,1)}, bf16[2,2,128,2304]{3,2,1,0:T(8,128)(2,1)}) custom-call(s32[1]{0:T(128)} %bitcast.16.mp, bf16[256,1024]{1,0:T(8,128)(2,1)} %get-tuple-element.129.refs_0_, bf16[256,1024]{1,0:T(8,128)(2,1)} %get-tuple-element.130.refs_1_, bf16[256,1024]{1,0:T(8,128)(2,1)} %get-tuple-element.131.refs_2_, ...), custom_call_target="tpu_custom_call" | custom-call | flops 1207959552 | bytes 4718592 | tf_op jit(solution)/shard_map/weight_grads/pallas_call | solution.py:686
  319.4 8.9 %collective-permute-start.27 = (bf16[256,256]{1,0:T(8,128)(2,1)S(1)}, bf16[256,256]{1,0:T(8,128)(2,1)S(1)}, u32[]{:S(2)}, u32[]{:S(2)}) collective-permute-start(bf16[256,256]{1,0:T(8,128)(2,1)S(1)} %copy-done.51), channel_id=1, source_target_pairs={{0,1},{1,0},{2,3},{3,2},{4,5},{5,4},{6,7},{7,6},{8,9},{9,8},{10,11... | collective-permute-start | bytes 393224 | tf_op jit(solution)/shard_map/ppermute | solution.py:741
  331.9 6.7 %leave_cross.1 = (f32[256,1024]{1,0:T(8,128)}, bf16[256,1024]{1,0:T(8,128)(2,1)}, bf16[304,256]{1,0:T(8,128)(2,1)}, bf16[304,256]{1,0:T(8,128)(2,1)}, bf16[304,2...) custom-call(f32[256,1024]{1,0:T(8,128)} %get-tuple-element.122.cross_grad_ref, f32[3,1024]{1,0:T(4,128)} %gain_ref.5, ...), custom_call_target="tpu_custom_call" | custom-call | flops 1073741824 | bytes 8548352 | tf_op jit(solution)/shard_map/leave_cross/pallas_call | solution.py:479
  345.3 5.0 %collective-permute-done.33.refs_1_ = bf16[304,256]{1,0:T(8,128)(2,1)S(1)} collective-permute-done((bf16[304,256]{1,0:T(8,128)(2,1)}, bf16[304,256]{1,0:T(8,128)(2,1)S(1)}, u32[]{:S(2)}, u32[]{:S(2)}) %collective-permute-start.33) | collective-permute-done | bytes 155680 | tf_op jit(solution)/shard_map/ppermute | solution.py:741
  351.2 14.0 %attend_back.3 = (bf16[1024,256]{1,0:T(8,128)(2,1)}, bf16[1024,256]{1,0:T(8,128)(2,1)}, bf16[1024,256]{1,0:T(8,128)(2,1)}) custom-call(bf16[1024,768]{1,0:T(8,128)(2,1)} %convolution_convert_fusion.refs_0_.refs_1_.refs_2_.refs_10_.refs_11_, bf16[304,256]{1,0:T(8,128)(2,1)} %get-tuple-element.153.refs_1_, bf16[304,256]{1,0:T(8,128)(2,1)} %get-tuple-element.157.refs_2_, ...), custom_call_target="tpu_custom_call" | custom-call | flops 4294967296 | bytes 4194304 | tf_op jit(solution)/shard_map/attend_back/pallas_call | solution.py:247
  365.2 5.7 %back_terms.3 = (bf16[1024,1024]{1,0:T(8,128)(2,1)}, bf16[1024,768]{1,0:T(8,128)(2,1)}) custom-call(bf16[1024,256]{1,0:T(8,128)(2,1)} %get-tuple-element.161.refs_0_, bf16[1024,256]{1,0:T(8,128)(2,1)} %get-tuple-element.162.refs_1_, bf16[1024,256]{1,0:T(8,128)(2,1)} %get-tuple-element.163.refs_2_, bf16[1024,768]{1,0:T(8,128)(2,1)} %copy.66.refs_2_.refs_3_), custom_call_target="tpu_custom_call" | custom-call | flops 1610612736 | bytes 3145728 | tf_op jit(solution)/shard_map/back_terms/pallas_call | solution.py:479
  371.1 4.9 %weight_grads.10 = bf16[4,4,128,512]{3,2,1,0:T(8,128)(2,1)} custom-call(s32[1]{0:T(128)} %bitcast.16.mp, bf16[256,1024]{1,0:T(8,128)(2,1)} %order.25.refs_0_, bf16[256,1024]{1,0:T(8,128)(2,1)} %get-tuple-element.168.refs_1_, bf16[256,256]{1,0:T(8,128)(2,1)} %get-tuple-element.99.refs_0_.refs_5_.refs_2_, bf16[256,256]{1,0:T(8,128)(2,1)} %copy-done.25, ...), custom_call_target="tpu_custom_call" | custom-call | flops 536870912 | bytes 2097152 | tf_op jit(solution)/shard_map/weight_grads/pallas_call | solution.py:686
  389.0 5.4 %weight_grads.11 = (bf16[2,4,128,512]{3,2,1,0:T(8,128)(2,1)}, bf16[2,4,128,512]{3,2,1,0:T(8,128)(2,1)}) custom-call(s32[1]{0:T(128)} %bitcast.16.mp, bf16[256,1024]{1,0:T(8,128)(2,1)} %order.25.refs_0_, bf16[256,1024]{1,0:T(8,128)(2,1)} %get-tuple-element.168.refs_1_, bf16[256,256]{1,0:T(8,128)(2,1)} %get-tuple-element.99.refs_0_.refs_5_.refs_2_, ...), custom_call_target="tpu_custom_call" | custom-call | flops 536870912 | bytes 2097152 | tf_op jit(solution)/shard_map/weight_grads/pallas_call | solution.py:686
  424.3 13.8 %collective-permute-done.39 = bf16[272,1280]{1,0:T(8,128)(2,1)} collective-permute-done((bf16[272,1280]{1,0:T(8,128)(2,1)S(1)}, bf16[272,1280]{1,0:T(8,128)(2,1)}, u32[]{:S(2)}, u32[]{:S(2)}) %collective-permute-start.39) | collective-permute-done | bytes 696352 | tf_op jit(solution)/shard_map/ppermute | solution.py:741
  453.1 10.2 %collective-permute-done.42 = bf16[1,4,128,512]{3,2,1,0:T(8,128)(2,1)S(1)} collective-permute-done((bf16[1,4,128,512]{3,2,1,0:T(8,128)(2,1)}, bf16[1,4,128,512]{3,2,1,0:T(8,128)(2,1)S(1)}, u32[]{:S(2)}, u32[]{:S(2)}) %collective-permute-start.42) | collective-permute-done | bytes 524320 | tf_op jit(solution)/shard_map/ppermute | solution.py:741
  (314 shorter events, 171.7 us)
Async XLA Ops:
  7.2 60.9 %all-gather.8.cloned.1.call-start = ((), (), s32[]{:S(2)}) async-start(), calls=%async_computation.7 | async-start | bytes 2621440 | tf_op jit(solution)/shard_map/all_gather | solution.py:816
  9.1 118.3 %all-gather.10.cloned.1.call-start = ((), (), s32[]{:S(2)}) async-start(), calls=%async_computation.8 | async-start | bytes 2621440 | tf_op jit(solution)/shard_map/all_gather | solution.py:823
  14.0 22.8 %collective-permute-start.1 = (bf16[128,768]{1,0:T(8,128)(2,1)S(1)}, bf16[128,768]{1,0:T(8,128)(2,1)S(1)}, u32[]{:S(2)}, u32[]{:S(2)}) collective-permute-start(bf16[128,768]{1,0:T(8,128)(2,1)S(1)} %pad_maximum_fusion.12), channel_id=1, source_target_pairs={{0,2},{1,3},{2,0},{3,1},{4,6},{5,7},{6,4},{7,5},{8,10},{9,11},{10,... | collective-permute-start | bytes 589832 | tf_op jit(solution)/shard_map/ppermute | solution.py:741
  16.6 20.3 %collective-permute-start.2 = (bf16[128,768]{1,0:T(8,128)(2,1)S(1)}, bf16[128,768]{1,0:T(8,128)(2,1)S(1)}, u32[]{:S(2)}, u32[]{:S(2)}) collective-permute-start(bf16[128,768]{1,0:T(8,128)(2,1)S(1)} %pad_maximum_fusion.12), channel_id=1, source_target_pairs={{0,3},{1,2},{2,1},{3,0},{4,7},{5,6},{6,5},{7,4},{8,11},{9,10},{10,... | collective-permute-start | bytes 589832 | tf_op jit(solution)/shard_map/ppermute | solution.py:741
  68.1 119.0 %all-gather.6.cloned.1.call-start = ((), (), s32[]{:S(2)}) async-start(), calls=%async_computation.3 | async-start | bytes 2621440 | tf_op jit(solution)/shard_map/all_gather | solution.py:835
  69.3 27.9 %collective-permute-start.4 = (bf16[2,3,128,768]{3,2,1,0:T(8,128)(2,1)S(1)}, bf16[2,3,128,768]{3,2,1,0:T(8,128)(2,1)S(1)}, u32[]{:S(2)}, u32[]{:S(2)}) collective-permute-start(bf16[2,3,128,768]{3,2,1,0:T(8,128)(2,1)S(1)} %copy-done.1), channel_id=1, source_target_pairs={{0,16},{1,17},{2,18},{3,19},{4,20},{5,21},{6,22},{7,23},{8,24},{9,... | collective-permute-start | bytes 3538952 | tf_op jit(solution)/shard_map/ppermute | solution.py:741
  70.8 31.9 %collective-permute-start.8 = (bf16[2,3,128,768]{3,2,1,0:T(8,128)(2,1)S(1)}, bf16[2,3,128,768]{3,2,1,0:T(8,128)(2,1)}, u32[]{:S(2)}, u32[]{:S(2)}) collective-permute-start(bf16[2,3,128,768]{3,2,1,0:T(8,128)(2,1)S(1)} %copy-done.1), channel_id=1, source_target_pairs={{0,4},{1,5},{2,6},{3,7},{4,0},{5,1},{6,2},{7,3},{8,12},{9,13},{10,... | collective-permute-start | bytes 3538952 | tf_op jit(solution)/shard_map/ppermute | solution.py:741
  98.3 21.1 %collective-permute-start.9 = (bf16[2,3,128,768]{3,2,1,0:T(8,128)(2,1)}, bf16[2,3,128,768]{3,2,1,0:T(8,128)(2,1)}, u32[]{:S(2)}, u32[]{:S(2)}) collective-permute-start(bf16[2,3,128,768]{3,2,1,0:T(8,128)(2,1)} %get-tuple-element.103.refs_7_.refs_8_), channel_id=1, source_target_pairs={{0,4},{1,5},{2,6},{3,7},{4,0},{5,1},{6,2},{7,3},{8,12},{9,13},{10,... | collective-permute-start | bytes 3538952 | tf_op jit(solution)/shard_map/ppermute | solution.py:741
  98.3 15.2 %collective-permute-start.5 = (bf16[256,256]{1,0:T(8,128)(2,1)}, bf16[256,256]{1,0:T(8,128)(2,1)S(1)}, u32[]{:S(2)}, u32[]{:S(2)}) collective-permute-start(bf16[256,256]{1,0:T(8,128)(2,1)} %get-tuple-element.100.refs_6_), channel_id=1, source_target_pairs={{0,1},{1,0},{2,3},{3,2},{4,5},{5,4},{6,7},{7,6},{8,9},{9,8},{10,11... | collective-permute-start | bytes 393224 | tf_op jit(solution)/shard_map/ppermute | solution.py:741
  98.3 18.6 %collective-permute-start.6 = (bf16[256,256]{1,0:T(8,128)(2,1)}, bf16[256,256]{1,0:T(8,128)(2,1)S(1)}, u32[]{:S(2)}, u32[]{:S(2)}) collective-permute-start(bf16[256,256]{1,0:T(8,128)(2,1)} %get-tuple-element.101.refs_7_), channel_id=1, source_target_pairs={{0,2},{1,3},{2,0},{3,1},{4,6},{5,7},{6,4},{7,5},{8,10},{9,11},{10,... | collective-permute-start | bytes 393224 | tf_op jit(solution)/shard_map/ppermute | solution.py:741
  101.3 18.0 %collective-permute-start.7 = (bf16[256,256]{1,0:T(8,128)(2,1)}, bf16[256,256]{1,0:T(8,128)(2,1)}, u32[]{:S(2)}, u32[]{:S(2)}) collective-permute-start(bf16[256,256]{1,0:T(8,128)(2,1)} %get-tuple-element.102.refs_8_), channel_id=1, source_target_pairs={{0,3},{1,2},{2,1},{3,0},{4,7},{5,6},{6,5},{7,4},{8,11},{9,10},{10,... | collective-permute-start | bytes 393224 | tf_op jit(solution)/shard_map/ppermute | solution.py:741
  127.4 223.7 %reduce-scatter.4.cloned.1.call-start = ((), (), s32[]{:S(2)}) async-start(), calls=%async_computation.4 | async-start | bytes 2621440 | tf_op jit(solution)/shard_map/reduce_scatter | solution.py:895
  130.1 19.3 %collective-permute-start.12 = (bf16[3,128,1024]{2,1,0:T(8,128)(2,1)S(1)}, bf16[3,128,1024]{2,1,0:T(8,128)(2,1)S(1)}, u32[]{:S(2)}, u32[]{:S(2)}) collective-permute-start(bf16[3,128,1024]{2,1,0:T(8,128)(2,1)S(1)} %get-tuple-element.231), channel_id=1, source_target_pairs={{0,16},{1,17},{2,18},{3,19},{4,20},{5,21},{6,22},{7,23},{8,24},{9,... | collective-permute-start | bytes 2359304 | tf_op jit(solution)/shard_map/ppermute | solution.py:741
  131.6 19.1 %collective-permute-start.10 = (bf16[3,128,1024]{2,1,0:T(8,128)(2,1)S(1)}, bf16[3,128,1024]{2,1,0:T(8,128)(2,1)S(1)}, u32[]{:S(2)}, u32[]{:S(2)}) collective-permute-start(bf16[3,128,1024]{2,1,0:T(8,128)(2,1)S(1)} %get-tuple-element.232), channel_id=1, source_target_pairs={{0,8},{1,9},{2,10},{3,11},{4,12},{5,13},{6,14},{7,15},{8,0},{9,1},... | collective-permute-start | bytes 2359304 | tf_op jit(solution)/shard_map/ppermute | solution.py:741
  152.5 48.5 %collective-permute-start.21 = (bf16[2,3,128,1024]{3,2,1,0:T(8,128)(2,1)}, bf16[2,3,128,1024]{3,2,1,0:T(8,128)(2,1)}, u32[]{:S(2)}, u32[]{:S(2)}) collective-permute-start(bf16[2,3,128,1024]{3,2,1,0:T(8,128)(2,1)} %pad_maximum_fusion.3.refs_15_), channel_id=1, source_target_pairs={{0,8},{1,9},{2,10},{3,11},{4,12},{5,13},{6,14},{7,15},{8,0},{9,1},... | collective-permute-start | bytes 4718600 | tf_op jit(solution)/shard_map/ppermute | solution.py:741
  154.0 47.0 %collective-permute-start.20 = (bf16[2,3,128,1024]{3,2,1,0:T(8,128)(2,1)}, bf16[2,3,128,1024]{3,2,1,0:T(8,128)(2,1)}, u32[]{:S(2)}, u32[]{:S(2)}) collective-permute-start(bf16[2,3,128,1024]{3,2,1,0:T(8,128)(2,1)} %pad_maximum_fusion.2.refs_11_), channel_id=1, source_target_pairs={{0,16},{1,17},{2,18},{3,19},{4,20},{5,21},{6,22},{7,23},{8,24},{9,... | collective-permute-start | bytes 4718600 | tf_op jit(solution)/shard_map/ppermute | solution.py:741
  156.7 34.2 %collective-permute-start.14 = (bf16[256,256]{1,0:T(8,128)(2,1)}, bf16[256,256]{1,0:T(8,128)(2,1)S(1)}, u32[]{:S(2)}, u32[]{:S(2)}) collective-permute-start(bf16[256,256]{1,0:T(8,128)(2,1)} %get-tuple-element.111), channel_id=1, source_target_pairs={{0,1},{1,0},{2,3},{3,2},{4,5},{5,4},{6,7},{7,6},{8,9},{9,8},{10,11... | collective-permute-start | bytes 393224 | tf_op jit(solution)/shard_map/ppermute | solution.py:741
  162.4 28.5 %collective-permute-start.15 = (bf16[256,256]{1,0:T(8,128)(2,1)}, bf16[256,256]{1,0:T(8,128)(2,1)S(1)}, u32[]{:S(2)}, u32[]{:S(2)}) collective-permute-start(bf16[256,256]{1,0:T(8,128)(2,1)} %get-tuple-element.112), channel_id=1, source_target_pairs={{0,2},{1,3},{2,0},{3,1},{4,6},{5,7},{6,4},{7,5},{8,10},{9,11},{10,... | collective-permute-start | bytes 393224 | tf_op jit(solution)/shard_map/ppermute | solution.py:741
  162.4 28.5 %collective-permute-start.16 = (bf16[256,256]{1,0:T(8,128)(2,1)}, bf16[256,256]{1,0:T(8,128)(2,1)S(1)}, u32[]{:S(2)}, u32[]{:S(2)}) collective-permute-start(bf16[256,256]{1,0:T(8,128)(2,1)} %get-tuple-element.113), channel_id=1, source_target_pairs={{0,3},{1,2},{2,1},{3,0},{4,7},{5,6},{6,5},{7,4},{8,11},{9,10},{10,... | collective-permute-start | bytes 393224 | tf_op jit(solution)/shard_map/ppermute | solution.py:741
  242.3 61.1 %collective-permute-start.31 = (bf16[4,2,128,2304]{3,2,1,0:T(8,128)(2,1)}, bf16[4,2,128,2304]{3,2,1,0:T(8,128)(2,1)}, u32[]{:S(2)}, u32[]{:S(2)}) collective-permute-start(bf16[4,2,128,2304]{3,2,1,0:T(8,128)(2,1)} %weight_grads.7.refs_4_), channel_id=1, source_target_pairs={{0,4},{1,5},{2,6},{3,7},{4,0},{5,1},{6,2},{7,3},{8,12},{9,13},{10,... | collective-permute-start | bytes 14155784 | tf_op jit(solution)/shard_map/ppermute | solution.py:741
  247.6 55.8 %collective-permute-start.30 = (bf16[4,2,128,2304]{3,2,1,0:T(8,128)(2,1)}, bf16[4,2,128,2304]{3,2,1,0:T(8,128)(2,1)}, u32[]{:S(2)}, u32[]{:S(2)}) collective-permute-start(bf16[4,2,128,2304]{3,2,1,0:T(8,128)(2,1)} %weight_grads.6.refs_3_), channel_id=1, source_target_pairs={{0,4},{1,5},{2,6},{3,7},{4,0},{5,1},{6,2},{7,3},{8,12},{9,13},{10,... | collective-permute-start | bytes 14155784 | tf_op jit(solution)/shard_map/ppermute | solution.py:741
  283.1 159.6 %reduce-scatter.6.cloned.1.call-start = ((), (), s32[]{:S(2)}) async-start(), calls=%async_computation.5 | async-start | bytes 2621440 | tf_op jit(solution)/shard_map/reduce_scatter | solution.py:931
  283.2 20.2 %collective-permute-start.28 = (bf16[256,256]{1,0:T(8,128)(2,1)S(1)}, bf16[256,256]{1,0:T(8,128)(2,1)S(1)}, u32[]{:S(2)}, u32[]{:S(2)}) collective-permute-start(bf16[256,256]{1,0:T(8,128)(2,1)S(1)} %copy-done.62), channel_id=1, source_target_pairs={{0,2},{1,3},{2,0},{3,1},{4,6},{5,7},{6,4},{7,5},{8,10},{9,11},{10,... | collective-permute-start | bytes 393224 | tf_op jit(solution)/shard_map/ppermute | solution.py:741
  285.3 18.0 %collective-permute-start.29 = (bf16[256,256]{1,0:T(8,128)(2,1)S(1)}, bf16[256,256]{1,0:T(8,128)(2,1)S(1)}, u32[]{:S(2)}, u32[]{:S(2)}) collective-permute-start(bf16[256,256]{1,0:T(8,128)(2,1)S(1)} %copy-done.60), channel_id=1, source_target_pairs={{0,3},{1,2},{2,1},{3,0},{4,7},{5,6},{6,5},{7,4},{8,11},{9,10},{10,... | collective-permute-start | bytes 393224 | tf_op jit(solution)/shard_map/ppermute | solution.py:741
  310.4 60.6 %collective-permute-start.36 = (bf16[2,2,128,2304]{3,2,1,0:T(8,128)(2,1)}, bf16[2,2,128,2304]{3,2,1,0:T(8,128)(2,1)}, u32[]{:S(2)}, u32[]{:S(2)}) collective-permute-start(bf16[2,2,128,2304]{3,2,1,0:T(8,128)(2,1)} %get-tuple-element.148.refs_5_), channel_id=1, source_target_pairs={{0,16},{1,17},{2,18},{3,19},{4,20},{5,21},{6,22},{7,23},{8,24},{9,... | collective-permute-start | bytes 7077896 | tf_op jit(solution)/shard_map/ppermute | solution.py:741
  318.0 53.1 %collective-permute-start.35 = (bf16[2,2,128,2304]{3,2,1,0:T(8,128)(2,1)}, bf16[2,2,128,2304]{3,2,1,0:T(8,128)(2,1)}, u32[]{:S(2)}, u32[]{:S(2)}) collective-permute-start(bf16[2,2,128,2304]{3,2,1,0:T(8,128)(2,1)} %get-tuple-element.146.refs_4_), channel_id=1, source_target_pairs={{0,8},{1,9},{2,10},{3,11},{4,12},{5,13},{6,14},{7,15},{8,0},{9,1},... | collective-permute-start | bytes 7077896 | tf_op jit(solution)/shard_map/ppermute | solution.py:741
  371.0 109.9 %reduce-scatter.8.cloned.1.call-start = ((), (), s32[]{:S(2)}) async-start(), calls=%async_computation.6 | async-start | bytes 2949120 | tf_op jit(solution)/shard_map/reduce_scatter | solution.py:966
  380.0 31.4 %collective-permute-start.47 = (bf16[1,2,128,2304]{3,2,1,0:T(8,128)(2,1)}, bf16[1,2,128,2304]{3,2,1,0:T(8,128)(2,1)S(1)}, u32[]{:S(2)}, u32[]{:S(2)}) collective-permute-start(bf16[1,2,128,2304]{3,2,1,0:T(8,128)(2,1)} %slice.162), channel_id=1, source_target_pairs={{0,8},{1,9},{2,10},{3,11},{4,12},{5,13},{6,14},{7,15},{8,0},{9,1},... | collective-permute-start | bytes 3538952 | tf_op jit(solution)/shard_map/ppermute | solution.py:741
  386.6 28.4 %collective-permute-start.46 = (bf16[1,2,128,2304]{3,2,1,0:T(8,128)(2,1)}, bf16[1,2,128,2304]{3,2,1,0:T(8,128)(2,1)}, u32[]{:S(2)}, u32[]{:S(2)}) collective-permute-start(bf16[1,2,128,2304]{3,2,1,0:T(8,128)(2,1)} %slice.161), channel_id=1, source_target_pairs={{0,16},{1,17},{2,18},{3,19},{4,20},{5,21},{6,22},{7,23},{8,24},{9,... | collective-permute-start | bytes 3538952 | tf_op jit(solution)/shard_map/ppermute | solution.py:741
  394.3 50.7 %collective-permute-start.41 = (bf16[2,4,128,512]{3,2,1,0:T(8,128)(2,1)}, bf16[2,4,128,512]{3,2,1,0:T(8,128)(2,1)}, u32[]{:S(2)}, u32[]{:S(2)}) collective-permute-start(bf16[2,4,128,512]{3,2,1,0:T(8,128)(2,1)} %get-tuple-element.169.refs_3_.refs_2_), channel_id=1, source_target_pairs={{0,8},{1,9},{2,10},{3,11},{4,12},{5,13},{6,14},{7,15},{8,0},{9,1},... | collective-permute-start | bytes 3145736 | tf_op jit(solution)/shard_map/ppermute | solution.py:741
  401.3 15.6 %collective-permute-start.38 = (bf16[528,1280]{1,0:T(8,128)(2,1)}, bf16[528,1280]{1,0:T(8,128)(2,1)}, u32[]{:S(2)}, u32[]{:S(2)}) collective-permute-start(bf16[528,1280]{1,0:T(8,128)(2,1)} %pad_maximum_fusion.4), channel_id=1, source_target_pairs={{0,4},{1,5},{2,6},{3,7},{4,0},{5,1},{6,2},{7,3},{8,12},{9,13},{10,... | collective-permute-start | bytes 4055048 | tf_op jit(solution)/shard_map/ppermute | solution.py:741
  421.1 17.1 %collective-permute-start.39 = (bf16[272,1280]{1,0:T(8,128)(2,1)S(1)}, bf16[272,1280]{1,0:T(8,128)(2,1)}, u32[]{:S(2)}, u32[]{:S(2)}) collective-permute-start(bf16[272,1280]{1,0:T(8,128)(2,1)S(1)} %pad_maximum_fusion.8), channel_id=1, source_target_pairs={{0,16},{1,17},{2,18},{3,19},{4,20},{5,21},{6,22},{7,23},{8,24},{9,... | collective-permute-start | bytes 2088968 | tf_op jit(solution)/shard_map/ppermute | solution.py:741
  (85 other events, 450.9 us)
Sparse Core Ops, SparseCore 0:
  9.6 58.4 all-gather.7
  70.2 57.1 all-gather.9
  129.6 57.4 all-gather.5
  283.2 46.7 reduce-scatter.3
  371.1 43.1 reduce-scatter.5
  424.4 50.7 reduce-scatter.7

commit v4 on v3

--- a/solution.py
+++ b/solution.py
@@ -956,10 +956,10 @@
     attn_sum = send(attn_sum, 2)
     home_here, home_there = fold_halves((home_grads[0], home_got))
     home_got, norm_terms = send_with_terms(home_there, norm_terms, 4)
+    attn_sum = attn_sum[0], *after([attn_sum[1]], home_got)
     home_here, home_there = fold_halves((home_here, home_got))
     home_got, sums = send_with_terms(home_there, norm_terms, 2)
     attn_here, attn_there = fold_halves(attn_sum)
-    (attn_there,) = after([attn_there], home_got)
     attn_sum = send((attn_here, attn_there), 4)
     home_sum = home_here, home_got
     ffn_sums = jnp.concatenate([layout.fold(*pair)[0] for pair in ffn_sums])

time: 498 us -> 497 us (level)
    unnamed x130 -> x120, local copies, waits for them, and re-layouts: 19.8 us -> 20.3 us
where the time goes in v4:
time: 497 us; the launch traced here: 490 us
  waiting for transfers between devices  195 us (39%)
  Pallas kernels  123 us (25%)
  starting transfers between devices  69.3 us (14%)
  local copies, waits for them, and re-layouts  42.9 us (9%)
  other arithmetic  30.3 us (6%)
  between operations  15.1 us (3%)
  matrix products  14.3 us (3%)
    ppermute x48, waiting for transfers between devices, permute(): return lax.ppermute(value, ('dp', 'mp'), pairs)  153 us
    ppermute x48, starting transfers between devices, permute(): return lax.ppermute(value, ('dp', 'mp'), pairs)  68.6 us
    pallas_call x5, Pallas kernels, call(): pl.pallas_call(kernel, in_specs=[here] * len(operands) + [there] * len(st...  43.8 us
    pallas_call x6, Pallas kernels, weight_grads(): pl.pallas_call(lambda mp, *refs: kernel(*refs), grid_spec=pltpu.PrefetchS...  32.9 us
    pallas_call x2, Pallas kernels, attend_back(): pl.pallas_call(functools.partial(attend_back_kernel, count=count, key_blo...  27.7 us
    all_gather x1, waiting for transfers between devices, local(): full_memory = lax.all_gather(memory_there, 'mp', axis=0, tiled=True)  22.3 us
    unnamed x120, local copies, waits for them, and re-layouts  20.3 us
    pallas_call x2, Pallas kernels, attend(): pl.pallas_call(functools.partial(attend_kernel, count=count, key_block=ke...  18.5 us
  transfers between devices with their start and end apart: 54, of which 27 were waited for; matrix products, arithmetic and copies ran while one was open for 14% of the time, Pallas kernels for 20%

profile of v4, /device:TPU:0, one launch (start us, length us, event | category | flops | bytes accessed | tf_op | source)
XLA Modules:
  0.0 489.7 jit_solution(12392183263144921166)
XLA Ops:
  16.6 5.7 %collective-permute-done = bf16[128,768]{1,0:T(8,128)(2,1)S(1)} collective-permute-done((bf16[128,768]{1,0:T(8,128)(2,1)S(1)}, bf16[128,768]{1,0:T(8,128)(2,1)S(1)}, u32[]{:S(2)}, u32[]{:S(2)}) %collective-permute-start) | collective-permute-done | bytes 196640 | tf_op jit(solution)/shard_map/ppermute | solution.py:741
  22.4 14.5 %collective-permute-done.1 = bf16[128,768]{1,0:T(8,128)(2,1)S(1)} collective-permute-done((bf16[128,768]{1,0:T(8,128)(2,1)S(1)}, bf16[128,768]{1,0:T(8,128)(2,1)S(1)}, u32[]{:S(2)}, u32[]{:S(2)}) %collective-permute-start.1) | collective-permute-done | bytes 196640 | tf_op jit(solution)/shard_map/ppermute | solution.py:741
  51.0 17.1 %all-gather.8.cloned.1.call-done = bf16[1024,1,1024]{2,0,1:T(8,128)(2,1)} async-done(((bf16[256,1,1024]{2,0,1:T(8,128)(2,1)}), bf16[1024,1,1024]{2,0,1:T(8,128)(2,1)}) %all-gather.8.cloned.1.call-update) | async-done | bytes 2097168 | tf_op jit(solution)/shard_map/all_gather | solution.py:816
  75.2 9.2 %attend.2 = (bf16[256,256]{1,0:T(8,128)(2,1)}, bf16[256,256]{1,0:T(8,128)(2,1)}, bf16[256,256]{1,0:T(8,128)(2,1)}, bf16[256,256]{1,0:T(8,128)(2,1)}, f32[2,8,1024]{2,1,0:T(8,128)}) custom-call(bf16[1024,768]{1,0:T(8,128)(2,1)} %convolution_convert_fusion.refs_0_.refs_1_.refs_2_.refs_10_.refs_11_, ...), custom_call_target="tpu_custom_call" | custom-call | flops 2147483648 | bytes 2097152 | tf_op jit(solution)/shard_map/attend/pallas_call | solution.py:219
  84.4 12.8 %collective-permute-done.4.refs_4_ = bf16[2,3,128,768]{3,2,1,0:T(8,128)(2,1)S(1)} collective-permute-done((bf16[2,3,128,768]{3,2,1,0:T(8,128)(2,1)S(1)}, bf16[2,3,128,768]{3,2,1,0:T(8,128)(2,1)S(1)}, u32[]{:S(2)}, u32[]{:S(2)}) %collective-permute-start.4) | collective-permute-done | bytes 1179680 | tf_op jit(solution)/shard_map/ppermute | solution.py:741
  102.7 10.8 %collective-permute-done.5.refs_1_.refs_3_ = bf16[256,256]{1,0:T(8,128)(2,1)S(1)} collective-permute-done((bf16[256,256]{1,0:T(8,128)(2,1)}, bf16[256,256]{1,0:T(8,128)(2,1)S(1)}, u32[]{:S(2)}, u32[]{:S(2)}) %collective-permute-start.5) | collective-permute-done | bytes 131104 | tf_op jit(solution)/shard_map/ppermute | solution.py:741
  119.4 5.9 %enter_cross.1 = (f32[256,1024]{1,0:T(8,128)}, f32[256,128]{1,0:T(8,128)}, bf16[256,1024]{1,0:T(8,128)(2,1)}, bf16[256,256]{1,0:T(8,128)(2,1)}, bf16[256,256]{1,...) custom-call(bf16[256,1024]{1,0:T(8,128)(2,1)} %bitcast.93, f32[3,1024]{1,0:T(4,128)} %gain_ref.5, ...), custom_call_target="tpu_custom_call" | custom-call | flops 1073741824 | bytes 6840320 | tf_op jit(solution)/shard_map/enter_cross/pallas_call | solution.py:479
  133.0 16.4 %collective-permute-done.12 = bf16[3,128,1024]{2,1,0:T(8,128)(2,1)S(1)} collective-permute-done((bf16[3,128,1024]{2,1,0:T(8,128)(2,1)S(1)}, bf16[3,128,1024]{2,1,0:T(8,128)(2,1)S(1)}, u32[]{:S(2)}, u32[]{:S(2)}) %collective-permute-start.12) | collective-permute-done | bytes 786464 | tf_op jit(solution)/shard_map/ppermute | solution.py:741
  156.7 5.7 %collective-permute-start.14 = (bf16[256,256]{1,0:T(8,128)(2,1)}, bf16[256,256]{1,0:T(8,128)(2,1)S(1)}, u32[]{:S(2)}, u32[]{:S(2)}) collective-permute-start(bf16[256,256]{1,0:T(8,128)(2,1)} %get-tuple-element.111), channel_id=1, source_target_pairs={{0,1},{1,0},{2,3},{3,2},{4,5},{5,4},{6,7},{7,6},{8,9},{9,8},{10,11... | collective-permute-start | bytes 393224 | tf_op jit(solution)/shard_map/ppermute | solution.py:741
  164.8 22.3 %all-gather.6.cloned.1.call-done.refs_2_ = bf16[1024,1024]{1,0:T(8,128)(2,1)} async-done(((bf16[256,1024]{1,0:T(8,128)(2,1)}), bf16[1024,1024]{1,0:T(8,128)(2,1)}) %all-gather.6.cloned.1.call-update) | async-done | bytes 2097168 | tf_op jit(solution)/shard_map/all_gather | solution.py:835
  191.7 9.3 %attend.3 = (bf16[256,256]{1,0:T(8,128)(2,1)}, bf16[256,256]{1,0:T(8,128)(2,1)}, bf16[256,256]{1,0:T(8,128)(2,1)}, bf16[256,256]{1,0:T(8,128)(2,1)}, f32[2,8,1024]{2,1,0:T(8,128)}) custom-call(bf16[256,256]{1,0:T(8,128)(2,1)} %get-tuple-element.110.refs_0_, bf16[256,256]{1,0:T(8,128)(2,1)} %copy-done.47, bf16[256,256]{1,0:T(8,128)(2,1)} %copy-done.48, ...), custom_call_target="tpu_custom_call" | custom-call | flops 2147483648 | bytes 2097152 | tf_op jit(solution)/shard_map/attend/pallas_call | solution.py:219
  209.0 5.8 %collective-permute-done.18.refs_2_.refs_7_ = bf16[256,256]{1,0:T(8,128)(2,1)S(1)} collective-permute-done((bf16[256,256]{1,0:T(8,128)(2,1)S(1)}, bf16[256,256]{1,0:T(8,128)(2,1)S(1)}, u32[]{:S(2)}, u32[]{:S(2)}) %collective-permute-start.18) | collective-permute-done | bytes 131104 | tf_op jit(solution)/shard_map/ppermute | solution.py:741
  216.6 20.5 %feed_forward.1 = (bf16[256,1024]{1,0:T(8,128)(2,1)}, bf16[256,1024]{1,0:T(8,128)(2,1)}, bf16[256,1024]{1,0:T(8,128)(2,1)}, f32[256,1024]{1,0:T(8,128)}, bf16[25...) custom-call(f32[256,1024]{1,0:T(8,128)} %get-tuple-element.104.first, ...), custom_call_target="tpu_custom_call" | custom-call | flops 8589934592 | bytes 24141824 | tf_op jit(solution)/shard_map/feed_forward/pallas_call | solution.py:479
  237.2 5.1 %weight_grads.7.refs_4_ = bf16[4,2,128,2304]{3,2,1,0:T(8,128)(2,1)} custom-call(s32[1]{0:T(128)} %bitcast.16.mp, bf16[256,1024]{1,0:T(8,128)(2,1)} %get-tuple-element.129.refs_0_, bf16[256,1024]{1,0:T(8,128)(2,1)} %get-tuple-element.130.refs_1_, bf16[256,1024]{1,0:T(8,128)(2,1)} %get-tuple-element.131.refs_2_, ...), custom_call_target="tpu_custom_call" | custom-call | flops 1207959552 | bytes 4718592 | tf_op jit(solution)/shard_map/weight_grads/pallas_call | solution.py:686
  242.4 5.2 %weight_grads.6.refs_3_ = bf16[4,2,128,2304]{3,2,1,0:T(8,128)(2,1)} custom-call(s32[1]{0:T(128)} %bitcast.16.mp, bf16[256,1024]{1,0:T(8,128)(2,1)} %get-tuple-element.129.refs_0_, bf16[256,1024]{1,0:T(8,128)(2,1)} %get-tuple-element.130.refs_1_, bf16[256,1024]{1,0:T(8,128)(2,1)} %get-tuple-element.131.refs_2_, ...), custom_call_target="tpu_custom_call" | custom-call | flops 1207959552 | bytes 4718592 | tf_op jit(solution)/shard_map/weight_grads/pallas_call | solution.py:686
  255.6 7.5 %collective-permute-done.25.refs_1_ = bf16[256,256]{1,0:T(8,128)(2,1)S(1)} collective-permute-done((bf16[256,256]{1,0:T(8,128)(2,1)S(1)}, bf16[256,256]{1,0:T(8,128)(2,1)S(1)}, u32[]{:S(2)}, u32[]{:S(2)}) %collective-permute-start.25) | collective-permute-done | bytes 131104 | tf_op jit(solution)/shard_map/ppermute | solution.py:741
  264.4 13.7 %attend_back.2 = (bf16[256,256]{1,0:T(8,128)(2,1)}, bf16[256,256]{1,0:T(8,128)(2,1)}, bf16[256,256]{1,0:T(8,128)(2,1)}, bf16[256,256]{1,0:T(8,128)(2,1)}, bf16[1...) custom-call(bf16[256,256]{1,0:T(8,128)(2,1)} %get-tuple-element.110.refs_0_, bf16[256,256]{1,0:T(8,128)(2,1)} %copy-done.47, ...), custom_call_target="tpu_custom_call" | custom-call | flops 4294967296 | bytes 4194304 | tf_op jit(solution)/shard_map/attend_back/pallas_call | solution.py:247
  287.2 16.2 %collective-permute-done.28.refs_2_.refs_1_ = bf16[256,256]{1,0:T(8,128)(2,1)S(1)} collective-permute-done((bf16[256,256]{1,0:T(8,128)(2,1)S(1)}, bf16[256,256]{1,0:T(8,128)(2,1)S(1)}, u32[]{:S(2)}, u32[]{:S(2)}) %collective-permute-start.28) | collective-permute-done | bytes 131104 | tf_op jit(solution)/shard_map/ppermute | solution.py:741
  304.1 6.3 %weight_grads.9 = (bf16[2,2,128,2304]{3,2,1,0:T(8,128)(2,1)}, bf16[2,2,128,2304]{3,2,1,0:T(8,128)(2,1)}) custom-call(s32[1]{0:T(128)} %bitcast.16.mp, bf16[256,1024]{1,0:T(8,128)(2,1)} %get-tuple-element.129.refs_0_, bf16[256,1024]{1,0:T(8,128)(2,1)} %get-tuple-element.130.refs_1_, bf16[256,1024]{1,0:T(8,128)(2,1)} %get-tuple-element.131.refs_2_, ...), custom_call_target="tpu_custom_call" | custom-call | flops 1207959552 | bytes 4718592 | tf_op jit(solution)/shard_map/weight_grads/pallas_call | solution.py:686
  311.8 6.0 %weight_grads.8 = (bf16[2,2,128,2304]{3,2,1,0:T(8,128)(2,1)}, bf16[2,2,128,2304]{3,2,1,0:T(8,128)(2,1)}) custom-call(s32[1]{0:T(128)} %bitcast.16.mp, bf16[256,1024]{1,0:T(8,128)(2,1)} %get-tuple-element.129.refs_0_, bf16[256,1024]{1,0:T(8,128)(2,1)} %get-tuple-element.130.refs_1_, bf16[256,1024]{1,0:T(8,128)(2,1)} %get-tuple-element.131.refs_2_, ...), custom_call_target="tpu_custom_call" | custom-call | flops 1207959552 | bytes 4718592 | tf_op jit(solution)/shard_map/weight_grads/pallas_call | solution.py:686
  319.3 8.9 %collective-permute-start.27 = (bf16[256,256]{1,0:T(8,128)(2,1)S(1)}, bf16[256,256]{1,0:T(8,128)(2,1)S(1)}, u32[]{:S(2)}, u32[]{:S(2)}) collective-permute-start(bf16[256,256]{1,0:T(8,128)(2,1)S(1)} %copy-done.46), channel_id=1, source_target_pairs={{0,1},{1,0},{2,3},{3,2},{4,5},{5,4},{6,7},{7,6},{8,9},{9,8},{10,11... | collective-permute-start | bytes 393224 | tf_op jit(solution)/shard_map/ppermute | solution.py:741
  331.8 6.7 %leave_cross.1 = (f32[256,1024]{1,0:T(8,128)}, bf16[256,1024]{1,0:T(8,128)(2,1)}, bf16[304,256]{1,0:T(8,128)(2,1)}, bf16[304,256]{1,0:T(8,128)(2,1)}, bf16[304,2...) custom-call(f32[256,1024]{1,0:T(8,128)} %get-tuple-element.122.cross_grad_ref, f32[3,1024]{1,0:T(4,128)} %gain_ref.5, ...), custom_call_target="tpu_custom_call" | custom-call | flops 1073741824 | bytes 8548352 | tf_op jit(solution)/shard_map/leave_cross/pallas_call | solution.py:479
  345.1 5.0 %collective-permute-done.33.refs_1_ = bf16[304,256]{1,0:T(8,128)(2,1)S(1)} collective-permute-done((bf16[304,256]{1,0:T(8,128)(2,1)}, bf16[304,256]{1,0:T(8,128)(2,1)S(1)}, u32[]{:S(2)}, u32[]{:S(2)}) %collective-permute-start.33) | collective-permute-done | bytes 155680 | tf_op jit(solution)/shard_map/ppermute | solution.py:741
  351.0 14.0 %attend_back.3 = (bf16[1024,256]{1,0:T(8,128)(2,1)}, bf16[1024,256]{1,0:T(8,128)(2,1)}, bf16[1024,256]{1,0:T(8,128)(2,1)}) custom-call(bf16[1024,768]{1,0:T(8,128)(2,1)} %convolution_convert_fusion.refs_0_.refs_1_.refs_2_.refs_10_.refs_11_, bf16[304,256]{1,0:T(8,128)(2,1)} %get-tuple-element.153.refs_1_, bf16[304,256]{1,0:T(8,128)(2,1)} %get-tuple-element.157.refs_2_, ...), custom_call_target="tpu_custom_call" | custom-call | flops 4294967296 | bytes 4194304 | tf_op jit(solution)/shard_map/attend_back/pallas_call | solution.py:247
  365.0 5.7 %back_terms.3 = (bf16[1024,1024]{1,0:T(8,128)(2,1)}, bf16[1024,768]{1,0:T(8,128)(2,1)}) custom-call(bf16[1024,256]{1,0:T(8,128)(2,1)} %get-tuple-element.161.refs_0_, bf16[1024,256]{1,0:T(8,128)(2,1)} %get-tuple-element.162.refs_1_, bf16[1024,256]{1,0:T(8,128)(2,1)} %get-tuple-element.163.refs_2_, bf16[1024,768]{1,0:T(8,128)(2,1)} %copy.67.refs_2_.refs_3_), custom_call_target="tpu_custom_call" | custom-call | flops 1610612736 | bytes 3145728 | tf_op jit(solution)/shard_map/back_terms/pallas_call | solution.py:479
  370.9 4.9 %weight_grads.10 = bf16[4,4,128,512]{3,2,1,0:T(8,128)(2,1)} custom-call(s32[1]{0:T(128)} %bitcast.16.mp, bf16[256,1024]{1,0:T(8,128)(2,1)} %order.25.refs_0_, bf16[256,1024]{1,0:T(8,128)(2,1)} %get-tuple-element.168.refs_1_, bf16[256,256]{1,0:T(8,128)(2,1)} %get-tuple-element.99.refs_0_.refs_5_.refs_2_, bf16[256,256]{1,0:T(8,128)(2,1)} %copy-done.25, ...), custom_call_target="tpu_custom_call" | custom-call | flops 536870912 | bytes 2097152 | tf_op jit(solution)/shard_map/weight_grads/pallas_call | solution.py:686
  388.8 5.3 %weight_grads.11 = (bf16[2,4,128,512]{3,2,1,0:T(8,128)(2,1)}, bf16[2,4,128,512]{3,2,1,0:T(8,128)(2,1)}) custom-call(s32[1]{0:T(128)} %bitcast.16.mp, bf16[256,1024]{1,0:T(8,128)(2,1)} %order.25.refs_0_, bf16[256,1024]{1,0:T(8,128)(2,1)} %get-tuple-element.168.refs_1_, bf16[256,256]{1,0:T(8,128)(2,1)} %get-tuple-element.99.refs_0_.refs_5_.refs_2_, ...), custom_call_target="tpu_custom_call" | custom-call | flops 536870912 | bytes 2097152 | tf_op jit(solution)/shard_map/weight_grads/pallas_call | solution.py:686
  409.1 5.3 %collective-permute-done.46.refs_0_ = bf16[1,2,128,2304]{3,2,1,0:T(8,128)(2,1)} collective-permute-done((bf16[1,2,128,2304]{3,2,1,0:T(8,128)(2,1)}, bf16[1,2,128,2304]{3,2,1,0:T(8,128)(2,1)}, u32[]{:S(2)}, u32[]{:S(2)}) %collective-permute-start.46) | collective-permute-done | bytes 1179680 | tf_op jit(solution)/shard_map/ppermute | solution.py:741
  424.7 13.5 %collective-permute-done.39 = bf16[272,1280]{1,0:T(8,128)(2,1)} collective-permute-done((bf16[272,1280]{1,0:T(8,128)(2,1)}, bf16[272,1280]{1,0:T(8,128)(2,1)}, u32[]{:S(2)}, u32[]{:S(2)}) %collective-permute-start.39) | collective-permute-done | bytes 696352 | tf_op jit(solution)/shard_map/ppermute | solution.py:741
  444.2 6.1 %collective-permute-done.41.refs_0_ = bf16[2,4,128,512]{3,2,1,0:T(8,128)(2,1)S(1)} collective-permute-done((bf16[2,4,128,512]{3,2,1,0:T(8,128)(2,1)}, bf16[2,4,128,512]{3,2,1,0:T(8,128)(2,1)S(1)}, u32[]{:S(2)}, u32[]{:S(2)}) %collective-permute-start.41) | collective-permute-done | bytes 1048608 | tf_op jit(solution)/shard_map/ppermute | solution.py:741
  458.7 5.3 %collective-permute-done.42 = bf16[1,4,128,512]{3,2,1,0:T(8,128)(2,1)S(1)} collective-permute-done((bf16[1,4,128,512]{3,2,1,0:T(8,128)(2,1)S(1)}, bf16[1,4,128,512]{3,2,1,0:T(8,128)(2,1)S(1)}, u32[]{:S(2)}, u32[]{:S(2)}) %collective-permute-start.42) | collective-permute-done | bytes 524320 | tf_op jit(solution)/shard_map/ppermute | solution.py:741
  473.0 5.9 %collective-permute-done.44 = bf16[128,512]{1,0:T(8,128)(2,1)S(1)} collective-permute-done((bf16[128,512]{1,0:T(8,128)(2,1)S(1)}, bf16[128,512]{1,0:T(8,128)(2,1)S(1)}, u32[]{:S(2)}, u32[]{:S(2)}) %collective-permute-start.44) | collective-permute-done | bytes 131104 | tf_op jit(solution)/shard_map/ppermute | solution.py:741
  (303 shorter events, 171.8 us)
Async XLA Ops:
  7.2 60.9 %all-gather.8.cloned.1.call-start = ((), (), s32[]{:S(2)}) async-start(), calls=%async_computation.7 | async-start | bytes 2621440 | tf_op jit(solution)/shard_map/all_gather | solution.py:816
  9.1 118.3 %all-gather.10.cloned.1.call-start = ((), (), s32[]{:S(2)}) async-start(), calls=%async_computation.8 | async-start | bytes 2621440 | tf_op jit(solution)/shard_map/all_gather | solution.py:823
  14.0 22.8 %collective-permute-start.1 = (bf16[128,768]{1,0:T(8,128)(2,1)S(1)}, bf16[128,768]{1,0:T(8,128)(2,1)S(1)}, u32[]{:S(2)}, u32[]{:S(2)}) collective-permute-start(bf16[128,768]{1,0:T(8,128)(2,1)S(1)} %pad_maximum_fusion.12), channel_id=1, source_target_pairs={{0,2},{1,3},{2,0},{3,1},{4,6},{5,7},{6,4},{7,5},{8,10},{9,11},{10,... | collective-permute-start | bytes 589832 | tf_op jit(solution)/shard_map/ppermute | solution.py:741
  16.6 20.3 %collective-permute-start.2 = (bf16[128,768]{1,0:T(8,128)(2,1)S(1)}, bf16[128,768]{1,0:T(8,128)(2,1)S(1)}, u32[]{:S(2)}, u32[]{:S(2)}) collective-permute-start(bf16[128,768]{1,0:T(8,128)(2,1)S(1)} %pad_maximum_fusion.12), channel_id=1, source_target_pairs={{0,3},{1,2},{2,1},{3,0},{4,7},{5,6},{6,5},{7,4},{8,11},{9,10},{10,... | collective-permute-start | bytes 589832 | tf_op jit(solution)/shard_map/ppermute | solution.py:741
  68.1 119.0 %all-gather.6.cloned.1.call-start = ((), (), s32[]{:S(2)}) async-start(), calls=%async_computation.3 | async-start | bytes 2621440 | tf_op jit(solution)/shard_map/all_gather | solution.py:835
  69.3 27.9 %collective-permute-start.4 = (bf16[2,3,128,768]{3,2,1,0:T(8,128)(2,1)S(1)}, bf16[2,3,128,768]{3,2,1,0:T(8,128)(2,1)S(1)}, u32[]{:S(2)}, u32[]{:S(2)}) collective-permute-start(bf16[2,3,128,768]{3,2,1,0:T(8,128)(2,1)S(1)} %copy-done.1), channel_id=1, source_target_pairs={{0,16},{1,17},{2,18},{3,19},{4,20},{5,21},{6,22},{7,23},{8,24},{9,... | collective-permute-start | bytes 3538952 | tf_op jit(solution)/shard_map/ppermute | solution.py:741
  70.8 31.9 %collective-permute-start.8 = (bf16[2,3,128,768]{3,2,1,0:T(8,128)(2,1)S(1)}, bf16[2,3,128,768]{3,2,1,0:T(8,128)(2,1)}, u32[]{:S(2)}, u32[]{:S(2)}) collective-permute-start(bf16[2,3,128,768]{3,2,1,0:T(8,128)(2,1)S(1)} %copy-done.1), channel_id=1, source_target_pairs={{0,4},{1,5},{2,6},{3,7},{4,0},{5,1},{6,2},{7,3},{8,12},{9,13},{10,... | collective-permute-start | bytes 3538952 | tf_op jit(solution)/shard_map/ppermute | solution.py:741
  98.3 21.1 %collective-permute-start.9 = (bf16[2,3,128,768]{3,2,1,0:T(8,128)(2,1)}, bf16[2,3,128,768]{3,2,1,0:T(8,128)(2,1)}, u32[]{:S(2)}, u32[]{:S(2)}) collective-permute-start(bf16[2,3,128,768]{3,2,1,0:T(8,128)(2,1)} %get-tuple-element.103.refs_7_.refs_8_), channel_id=1, source_target_pairs={{0,4},{1,5},{2,6},{3,7},{4,0},{5,1},{6,2},{7,3},{8,12},{9,13},{10,... | collective-permute-start | bytes 3538952 | tf_op jit(solution)/shard_map/ppermute | solution.py:741
  98.3 15.2 %collective-permute-start.5 = (bf16[256,256]{1,0:T(8,128)(2,1)}, bf16[256,256]{1,0:T(8,128)(2,1)S(1)}, u32[]{:S(2)}, u32[]{:S(2)}) collective-permute-start(bf16[256,256]{1,0:T(8,128)(2,1)} %get-tuple-element.100.refs_6_), channel_id=1, source_target_pairs={{0,1},{1,0},{2,3},{3,2},{4,5},{5,4},{6,7},{7,6},{8,9},{9,8},{10,11... | collective-permute-start | bytes 393224 | tf_op jit(solution)/shard_map/ppermute | solution.py:741
  98.3 18.6 %collective-permute-start.6 = (bf16[256,256]{1,0:T(8,128)(2,1)}, bf16[256,256]{1,0:T(8,128)(2,1)S(1)}, u32[]{:S(2)}, u32[]{:S(2)}) collective-permute-start(bf16[256,256]{1,0:T(8,128)(2,1)} %get-tuple-element.101.refs_7_), channel_id=1, source_target_pairs={{0,2},{1,3},{2,0},{3,1},{4,6},{5,7},{6,4},{7,5},{8,10},{9,11},{10,... | collective-permute-start | bytes 393224 | tf_op jit(solution)/shard_map/ppermute | solution.py:741
  101.3 18.0 %collective-permute-start.7 = (bf16[256,256]{1,0:T(8,128)(2,1)}, bf16[256,256]{1,0:T(8,128)(2,1)}, u32[]{:S(2)}, u32[]{:S(2)}) collective-permute-start(bf16[256,256]{1,0:T(8,128)(2,1)} %get-tuple-element.102.refs_8_), channel_id=1, source_target_pairs={{0,3},{1,2},{2,1},{3,0},{4,7},{5,6},{6,5},{7,4},{8,11},{9,10},{10,... | collective-permute-start | bytes 393224 | tf_op jit(solution)/shard_map/ppermute | solution.py:741
  127.4 223.5 %reduce-scatter.4.cloned.1.call-start = ((), (), s32[]{:S(2)}) async-start(), calls=%async_computation.4 | async-start | bytes 2621440 | tf_op jit(solution)/shard_map/reduce_scatter | solution.py:895
  130.1 19.3 %collective-permute-start.12 = (bf16[3,128,1024]{2,1,0:T(8,128)(2,1)S(1)}, bf16[3,128,1024]{2,1,0:T(8,128)(2,1)S(1)}, u32[]{:S(2)}, u32[]{:S(2)}) collective-permute-start(bf16[3,128,1024]{2,1,0:T(8,128)(2,1)S(1)} %get-tuple-element.231), channel_id=1, source_target_pairs={{0,16},{1,17},{2,18},{3,19},{4,20},{5,21},{6,22},{7,23},{8,24},{9,... | collective-permute-start | bytes 2359304 | tf_op jit(solution)/shard_map/ppermute | solution.py:741
  131.6 19.1 %collective-permute-start.10 = (bf16[3,128,1024]{2,1,0:T(8,128)(2,1)S(1)}, bf16[3,128,1024]{2,1,0:T(8,128)(2,1)S(1)}, u32[]{:S(2)}, u32[]{:S(2)}) collective-permute-start(bf16[3,128,1024]{2,1,0:T(8,128)(2,1)S(1)} %get-tuple-element.232), channel_id=1, source_target_pairs={{0,8},{1,9},{2,10},{3,11},{4,12},{5,13},{6,14},{7,15},{8,0},{9,1},... | collective-permute-start | bytes 2359304 | tf_op jit(solution)/shard_map/ppermute | solution.py:741
  152.5 48.5 %collective-permute-start.21 = (bf16[2,3,128,1024]{3,2,1,0:T(8,128)(2,1)}, bf16[2,3,128,1024]{3,2,1,0:T(8,128)(2,1)}, u32[]{:S(2)}, u32[]{:S(2)}) collective-permute-start(bf16[2,3,128,1024]{3,2,1,0:T(8,128)(2,1)} %pad_maximum_fusion.3.refs_15_), channel_id=1, source_target_pairs={{0,8},{1,9},{2,10},{3,11},{4,12},{5,13},{6,14},{7,15},{8,0},{9,1},... | collective-permute-start | bytes 4718600 | tf_op jit(solution)/shard_map/ppermute | solution.py:741
  154.1 46.9 %collective-permute-start.20 = (bf16[2,3,128,1024]{3,2,1,0:T(8,128)(2,1)}, bf16[2,3,128,1024]{3,2,1,0:T(8,128)(2,1)}, u32[]{:S(2)}, u32[]{:S(2)}) collective-permute-start(bf16[2,3,128,1024]{3,2,1,0:T(8,128)(2,1)} %pad_maximum_fusion.2.refs_11_), channel_id=1, source_target_pairs={{0,16},{1,17},{2,18},{3,19},{4,20},{5,21},{6,22},{7,23},{8,24},{9,... | collective-permute-start | bytes 4718600 | tf_op jit(solution)/shard_map/ppermute | solution.py:741
  156.7 34.2 %collective-permute-start.14 = (bf16[256,256]{1,0:T(8,128)(2,1)}, bf16[256,256]{1,0:T(8,128)(2,1)S(1)}, u32[]{:S(2)}, u32[]{:S(2)}) collective-permute-start(bf16[256,256]{1,0:T(8,128)(2,1)} %get-tuple-element.111), channel_id=1, source_target_pairs={{0,1},{1,0},{2,3},{3,2},{4,5},{5,4},{6,7},{7,6},{8,9},{9,8},{10,11... | collective-permute-start | bytes 393224 | tf_op jit(solution)/shard_map/ppermute | solution.py:741
  162.4 28.5 %collective-permute-start.15 = (bf16[256,256]{1,0:T(8,128)(2,1)}, bf16[256,256]{1,0:T(8,128)(2,1)S(1)}, u32[]{:S(2)}, u32[]{:S(2)}) collective-permute-start(bf16[256,256]{1,0:T(8,128)(2,1)} %get-tuple-element.112), channel_id=1, source_target_pairs={{0,2},{1,3},{2,0},{3,1},{4,6},{5,7},{6,4},{7,5},{8,10},{9,11},{10,... | collective-permute-start | bytes 393224 | tf_op jit(solution)/shard_map/ppermute | solution.py:741
  162.4 28.5 %collective-permute-start.16 = (bf16[256,256]{1,0:T(8,128)(2,1)}, bf16[256,256]{1,0:T(8,128)(2,1)S(1)}, u32[]{:S(2)}, u32[]{:S(2)}) collective-permute-start(bf16[256,256]{1,0:T(8,128)(2,1)} %get-tuple-element.113), channel_id=1, source_target_pairs={{0,3},{1,2},{2,1},{3,0},{4,7},{5,6},{6,5},{7,4},{8,11},{9,10},{10,... | collective-permute-start | bytes 393224 | tf_op jit(solution)/shard_map/ppermute | solution.py:741
  242.3 61.0 %collective-permute-start.31 = (bf16[4,2,128,2304]{3,2,1,0:T(8,128)(2,1)}, bf16[4,2,128,2304]{3,2,1,0:T(8,128)(2,1)}, u32[]{:S(2)}, u32[]{:S(2)}) collective-permute-start(bf16[4,2,128,2304]{3,2,1,0:T(8,128)(2,1)} %weight_grads.7.refs_4_), channel_id=1, source_target_pairs={{0,4},{1,5},{2,6},{3,7},{4,0},{5,1},{6,2},{7,3},{8,12},{9,13},{10,... | collective-permute-start | bytes 14155784 | tf_op jit(solution)/shard_map/ppermute | solution.py:741
  247.6 55.8 %collective-permute-start.30 = (bf16[4,2,128,2304]{3,2,1,0:T(8,128)(2,1)}, bf16[4,2,128,2304]{3,2,1,0:T(8,128)(2,1)}, u32[]{:S(2)}, u32[]{:S(2)}) collective-permute-start(bf16[4,2,128,2304]{3,2,1,0:T(8,128)(2,1)} %weight_grads.6.refs_3_), channel_id=1, source_target_pairs={{0,4},{1,5},{2,6},{3,7},{4,0},{5,1},{6,2},{7,3},{8,12},{9,13},{10,... | collective-permute-start | bytes 14155784 | tf_op jit(solution)/shard_map/ppermute | solution.py:741
  283.1 158.7 %reduce-scatter.6.cloned.1.call-start = ((), (), s32[]{:S(2)}) async-start(), calls=%async_computation.5 | async-start | bytes 2621440 | tf_op jit(solution)/shard_map/reduce_scatter | solution.py:931
  283.1 20.2 %collective-permute-start.28 = (bf16[256,256]{1,0:T(8,128)(2,1)S(1)}, bf16[256,256]{1,0:T(8,128)(2,1)S(1)}, u32[]{:S(2)}, u32[]{:S(2)}) collective-permute-start(bf16[256,256]{1,0:T(8,128)(2,1)S(1)} %copy-done.57), channel_id=1, source_target_pairs={{0,2},{1,3},{2,0},{3,1},{4,6},{5,7},{6,4},{7,5},{8,10},{9,11},{10,... | collective-permute-start | bytes 393224 | tf_op jit(solution)/shard_map/ppermute | solution.py:741
  285.3 18.1 %collective-permute-start.29 = (bf16[256,256]{1,0:T(8,128)(2,1)S(1)}, bf16[256,256]{1,0:T(8,128)(2,1)S(1)}, u32[]{:S(2)}, u32[]{:S(2)}) collective-permute-start(bf16[256,256]{1,0:T(8,128)(2,1)S(1)} %copy-done.55), channel_id=1, source_target_pairs={{0,3},{1,2},{2,1},{3,0},{4,7},{5,6},{6,5},{7,4},{8,11},{9,10},{10,... | collective-permute-start | bytes 393224 | tf_op jit(solution)/shard_map/ppermute | solution.py:741
  310.4 60.4 %collective-permute-start.36 = (bf16[2,2,128,2304]{3,2,1,0:T(8,128)(2,1)}, bf16[2,2,128,2304]{3,2,1,0:T(8,128)(2,1)}, u32[]{:S(2)}, u32[]{:S(2)}) collective-permute-start(bf16[2,2,128,2304]{3,2,1,0:T(8,128)(2,1)} %get-tuple-element.148.refs_5_), channel_id=1, source_target_pairs={{0,16},{1,17},{2,18},{3,19},{4,20},{5,21},{6,22},{7,23},{8,24},{9,... | collective-permute-start | bytes 7077896 | tf_op jit(solution)/shard_map/ppermute | solution.py:741
  317.8 53.0 %collective-permute-start.35 = (bf16[2,2,128,2304]{3,2,1,0:T(8,128)(2,1)}, bf16[2,2,128,2304]{3,2,1,0:T(8,128)(2,1)}, u32[]{:S(2)}, u32[]{:S(2)}) collective-permute-start(bf16[2,2,128,2304]{3,2,1,0:T(8,128)(2,1)} %get-tuple-element.146.refs_4_), channel_id=1, source_target_pairs={{0,8},{1,9},{2,10},{3,11},{4,12},{5,13},{6,14},{7,15},{8,0},{9,1},... | collective-permute-start | bytes 7077896 | tf_op jit(solution)/shard_map/ppermute | solution.py:741
  370.8 109.0 %reduce-scatter.8.cloned.1.call-start = ((), (), s32[]{:S(2)}) async-start(), calls=%async_computation.6 | async-start | bytes 2949120 | tf_op jit(solution)/shard_map/reduce_scatter | solution.py:966
  379.8 29.3 %collective-permute-start.47 = (bf16[1,2,128,2304]{3,2,1,0:T(8,128)(2,1)}, bf16[1,2,128,2304]{3,2,1,0:T(8,128)(2,1)S(1)}, u32[]{:S(2)}, u32[]{:S(2)}) collective-permute-start(bf16[1,2,128,2304]{3,2,1,0:T(8,128)(2,1)} %slice.162), channel_id=1, source_target_pairs={{0,8},{1,9},{2,10},{3,11},{4,12},{5,13},{6,14},{7,15},{8,0},{9,1},... | collective-permute-start | bytes 3538952 | tf_op jit(solution)/shard_map/ppermute | solution.py:741
  385.5 28.9 %collective-permute-start.46 = (bf16[1,2,128,2304]{3,2,1,0:T(8,128)(2,1)}, bf16[1,2,128,2304]{3,2,1,0:T(8,128)(2,1)}, u32[]{:S(2)}, u32[]{:S(2)}) collective-permute-start(bf16[1,2,128,2304]{3,2,1,0:T(8,128)(2,1)} %slice.161), channel_id=1, source_target_pairs={{0,16},{1,17},{2,18},{3,19},{4,20},{5,21},{6,22},{7,23},{8,24},{9,... | collective-permute-start | bytes 3538952 | tf_op jit(solution)/shard_map/ppermute | solution.py:741
  420.6 17.7 %collective-permute-start.39 = (bf16[272,1280]{1,0:T(8,128)(2,1)}, bf16[272,1280]{1,0:T(8,128)(2,1)}, u32[]{:S(2)}, u32[]{:S(2)}) collective-permute-start(bf16[272,1280]{1,0:T(8,128)(2,1)} %pad_maximum_fusion.8), channel_id=1, source_target_pairs={{0,16},{1,17},{2,18},{3,19},{4,20},{5,21},{6,22},{7,23},{8,24},{9,... | collective-permute-start | bytes 2088968 | tf_op jit(solution)/shard_map/ppermute | solution.py:741
  423.9 26.4 %collective-permute-start.41 = (bf16[2,4,128,512]{3,2,1,0:T(8,128)(2,1)}, bf16[2,4,128,512]{3,2,1,0:T(8,128)(2,1)S(1)}, u32[]{:S(2)}, u32[]{:S(2)}) collective-permute-start(bf16[2,4,128,512]{3,2,1,0:T(8,128)(2,1)} %get-tuple-element.169.refs_3_.refs_2_), channel_id=1, source_target_pairs={{0,8},{1,9},{2,10},{3,11},{4,12},{5,13},{6,14},{7,15},{8,0},{9,1},... | collective-permute-start | bytes 3145736 | tf_op jit(solution)/shard_map/ppermute | solution.py:741
  441.3 15.5 %collective-permute-start.40 = (bf16[144,1280]{1,0:T(8,128)(2,1)S(1)}, bf16[144,1280]{1,0:T(8,128)(2,1)}, u32[]{:S(2)}, u32[]{:S(2)}) collective-permute-start(bf16[144,1280]{1,0:T(8,128)(2,1)S(1)} %pad_maximum_fusion.11), channel_id=1, source_target_pairs={{0,8},{1,9},{2,10},{3,11},{4,12},{5,13},{6,14},{7,15},{8,0},{9,1},... | collective-permute-start | bytes 1105928 | tf_op jit(solution)/shard_map/ppermute | solution.py:741
  (80 other events, 432.7 us)
Sparse Core Ops, SparseCore 0:
  9.6 58.4 all-gather.7
  70.2 57.1 all-gather.9
  129.6 57.4 all-gather.5
  283.2 46.6 reduce-scatter.3
  370.9 43.2 reduce-scatter.5
  424.1 48.9 reduce-scatter.7
